TPU v7x, 128 devices: a whole 4x4x4 slice. The times are simulated.
128 devices in a mesh: lat: 8 (over x, core), lon: 8 (over y_lo, z), tp: 2 (over y_hi).
Axes of the slice: x: 4, y: 4 (y_hi: 2, y_lo: 2; y = y_hi * 2 + y_lo), z: 4, core: 2. Of those that a mesh axis runs over, the one named last changes fastest.
Arguments:
- patches: bfloat16 [4, 192, 192, 512], P(None, 'lat', ('lon', 'tp')), may hold values from -6 to 6
- region_ids: int32 [4, 192, 192], P(None, 'lat', ('lon', 'tp')), may hold values from 0 to 3
- triple_one: bfloat16 [512, 3, 512], replicated, may hold values from -0.25 to 0.25
- output_one: bfloat16 [512, 512], replicated, may hold values from -0.25 to 0.25
- expand_one: bfloat16 [512, 2048], replicated, may hold values from -0.25 to 0.25
- shrink_one: bfloat16 [2048, 512], replicated, may hold values from -0.125 to 0.125
- scales_one: bfloat16 [8], replicated, may hold values from 4 to 16
- merge_weight: bfloat16 [2048, 1024], replicated, may hold values from -0.125 to 0.125
- triple_two: bfloat16 [1024, 3, 1024], P('tp'), may hold values from -0.1875 to 0.1875
- output_two: bfloat16 [1024, 1024], P('tp'), may hold values from -0.1875 to 0.1875
- expand_two: bfloat16 [4096, 1024], P('tp'), may hold values from -0.1875 to 0.1875
- shrink_two: bfloat16 [4096, 1024], P('tp'), may hold values from -0.09375 to 0.09375
- scales_two: bfloat16 [16], P('tp'), may hold values from 4 to 16
Outputs:
- skip: bfloat16 [4, 192, 192, 512], P(None, 'lat', ('lon', 'tp'))
- coarse: bfloat16 [4, 96, 96, 1024], P(None, 'lat', ('lon', 'tp'))
All inputs are finite; a program needn't handle non-finite values.
Results may differ from a plain program's by a relative error of at most 0.024.
Values may be sent and summed in bfloat16 or wider, within the bound.
No kernel may reach another device: no remote copies, remote signals or barrier semaphores. Data moves between devices by JAX's collectives and lax.ppermute only.
A program may use at most 192 MiB of HBM per device.

v0:
```python
import functools
import math

import jax
import jax.numpy as jnp
import numpy as np
from jax import lax
from jax.experimental import pallas as pl
from jax.experimental.pallas import tpu as pltpu
from jax.sharding import PartitionSpec as P

BF = jnp.bfloat16
F32 = jnp.float32
MASK = 192.0
LOG2E = math.log2(math.e)
MIB = 1024 * 1024


def home_level(lg, l):
    return (2 * lg + l + 1) % 4


def pick_rows():
    rows, keep = np.zeros((1152, 48), np.float32), np.zeros((1152, 24), np.float32)
    group = np.zeros((1152, 1), np.float32)
    at = 0
    for w in range(4):
        for part in range(2 if w == 3 else 1):
            outer = [(h, g) for h in range(2) for g in range(2)]
            if w < 3:
                outer = [(h, g) for g in range(2) for h in range(2)]
            for half, lg in outer:
                for l in range(2):
                    for i in range(3 * part, 3 * part + 3) if w == 3 else range(6):
                        for j in range(6):
                            rows[at, (half * 6 + j) * 4 + 2 * lg + l] = 1
                            keep[at, 6 * w + i] = 1
                            group[at] = 4 * lg
                            at += 1
    return rows, np.concatenate([keep, group], axis=1)


def place(level, i, j):
    lg, l = ((level - 1) % 4) // 2, ((level - 1) % 4) % 2
    if i < 3 or i >= 21:
        edge, ie = (0, i) if i < 3 else (1, i - 21)
        return edge * 72 + lg * 36 + l * 18 + ie * 6 + j
    w, iw = (i - 3) // 6, (i - 3) % 6
    return 144 + w * 144 + lg * 72 + l * 36 + iw * 6 + j


def home_rows():
    mat = np.zeros((576, 576), np.float32)
    for level in range(4):
        for j in range(6):
            for i in range(24):
                mat[level * 144 + j * 24 + i, place(level, i, j)] = 1
    return mat


def merge_rows():
    mat = np.zeros((2, 4, 144, 864), np.float32)
    for g in range(2):
        for m in range(4):
            pi, pj = m // 2, m % 2
            for level in range(4):
                for ii in range(6):
                    i = 2 * (6 * g + ii) + pi
                    for jj in range(6):
                        half, j = jj // 3, 2 * (jj % 3) + pj
                        at = place(level, i, j)
                        chunk = 0 if at < 144 else at // 144 - g
                        row = (level // 2) * 72 + (level % 2) * 36 + ii * 6 + jj
                        mat[g, m, row, 288 * chunk + half * 144 + at % 144] = 1
    return mat.reshape(2, 576, 864)


def coarse_rows():
    mat = np.zeros((144, 144), np.float32)
    for level in range(4):
        for ii in range(6):
            for jj in range(6):
                row = (ii * 6 + jj) * 4 + level
                mat[row, (level // 2) * 72 + (level % 2) * 36 + ii * 6 + jj] = 1
    return mat


def const(mat):
    return jnp.asarray(mat, dtype=BF)


def dot(a, b):
    return lax.dot_general(a, b, (((1,), (0,)), ((), ())), preferred_element_type=F32)


def dot_nt(a, b):
    return lax.dot_general(a, b, (((1,), (1,)), ((), ())), preferred_element_type=F32)


def normed(values):
    centred = values - jnp.mean(values, axis=-1, keepdims=True)
    spread = jnp.mean(centred * centred, axis=-1, keepdims=True)
    return centred * lax.rsqrt(spread + 1e-05)


def gelu(x):
    inner = x * (0.7978845608028654 + 0.035677408136300125 * (x * x))
    return (0.5 * x) * (1.0 + jnp.tanh(inner))


def unit(packed, ones, factor=None):
    wide = packed.astype(F32)
    squares = (wide * wide).astype(BF)
    total = jnp.concatenate([dot(squares[:, :256], ones), dot(squares[:, 256:], ones)], axis=1)
    result = wide * lax.rsqrt(total + 1e-06)
    if factor is not None:
        result = result * factor
    return result.astype(BF)


def heads(q, k, v, lanes, aug_q=None, aug_k=None):
    count = q.shape[0]
    low, high = lanes[0:1], lanes[1:2]
    first = lax.broadcasted_iota(jnp.int32, (count, 128), 1) < 64
    if aug_q is not None:
        aug_q = jnp.concatenate([aug_q, aug_q], axis=0)
    ones = jnp.ones((v.shape[0], 128), BF)
    parts = []
    for pair in range(4):
        span = slice(pair * 128, pair * 128 + 128)
        qp, kp = q[:, span], k[:, span]
        qp = jnp.concatenate([qp * low, qp * high], axis=0)
        if aug_q is not None:
            qp = jnp.concatenate([qp, aug_q], axis=1)
            kp = jnp.concatenate([kp, aug_k], axis=1)
        weights = jnp.exp2(dot_nt(qp, kp)).astype(BF)
        acc = dot(weights, jnp.concatenate([v[:, span], ones], axis=1))
        both = jnp.where(first, acc[:count, :128], acc[count:, :128])
        total = jnp.where(first, acc[:count, 128:], acc[count:, 128:])
        parts.append(both / total)
    return jnp.concatenate(parts, axis=1).astype(BF)


def call(kernel, outs, args, flops, vmem=16, smem=(), hbm=(), scratch=()):
    def space(n):
        return pltpu.SMEM if n in smem else pltpu.HBM if n in hbm else pltpu.VMEM

    moved = sum(int(np.prod(a.shape)) * a.dtype.itemsize for a in args)
    return pl.pallas_call(
        kernel,
        out_shape=[jax.ShapeDtypeStruct(shape, kind) for shape, kind in outs],
        in_specs=[pl.BlockSpec(memory_space=space(n)) for n in range(len(args))],
        out_specs=[pl.BlockSpec(memory_space=pltpu.VMEM) for _ in outs],
        scratch_shapes=list(scratch),
        compiler_params=pltpu.CompilerParams(vmem_limit_bytes=vmem * MIB),
        cost_estimate=pl.CostEstimate(flops=flops, bytes_accessed=moved, transcendentals=0),
    )(*args)


def pack_kernel(x, left, right):
    row = lax.broadcasted_iota(jnp.int32, (144, 144), 0)
    col = lax.broadcasted_iota(jnp.int32, (144, 144), 1)
    six = (row * 10923) >> 16
    lat = jnp.where(row < 18, six, jnp.where(row < 36, six + 18, six - 3))
    perm = jnp.where(col == (row - 6 * six) * 24 + lat, 1.0, 0.0).astype(BF)
    for half, dst in enumerate((left, right)):
        got = []
        for level in (1, 2, 3, 0):
            at = level * 288 + half * 144
            got.append(dot(perm, x[at:at + 144]))
        rows = [g[e:e + 18] for e in (0, 18) for g in got]
        dst[:144] = jnp.concatenate(rows, axis=0).astype(BF)
        rows = [g[w:w + 36] for w in (36, 72, 108) for g in got]
        dst[144:] = jnp.concatenate(rows, axis=0).astype(BF)


def ready_kernel(
    at, ids, rows, keep, sone, stwo, spread, o_two, classes, s_one, s_two, quarter, sem
):
    copy = pltpu.make_async_copy(
        o_two.at[pl.ds(pl.multiple_of(at[0] * 128, 128), 128)], quarter, sem
    )
    copy.start()
    for src, dst in ((sone, s_one), (stwo, s_two)):
        dst[...] = dot(src[...], spread[...])[0:1] * LOG2E
    grid = jnp.concatenate([ids[c] for c in range(12)], axis=0).astype(F32).astype(BF)
    picked = jnp.concatenate([dot(rows[...], grid), jnp.ones((1152, 1), F32)], axis=1)
    name = jnp.sum(picked * keep[...].astype(F32), axis=1, keepdims=True)
    lane = lax.broadcasted_iota(jnp.int32, (1152, 128), 1)
    hit = (lane.astype(F32) == name) | (lane == 8)
    classes[...] = jnp.where(hit, 1.0, 0.0).astype(BF)
    copy.wait()


def rim_kernel(left_all, right_all, classes, down, up):
    left, right = left_all[:144].astype(F32), right_all[:144].astype(F32)
    marks = classes[864:].astype(F32)
    up[...] = jnp.concatenate([right[:72], left[:72]], axis=0).astype(BF)
    wide = jnp.concatenate([marks[b * 72:b * 72 + 72] for b in range(4)], axis=1)
    down[...] = jnp.concatenate([right[72:], left[72:], wide], axis=0).astype(BF)


def join_kernel(at, a, b, c, d, out):
    mine = at[0]
    for step, part in enumerate((a, b, c, d)):
        out[pl.ds(pl.multiple_of((mine ^ step) * 128, 128), 128)] = part[...]


def windows_of(right, left):
    parts = []
    for at in range(0, right.shape[0], 72):
        parts += [right[at:at + 72], left[at:at + 72]]
    return jnp.concatenate(parts, axis=0)


def halves_of(rows):
    right = [rows[at:at + 72] for at in range(0, rows.shape[0], 144)]
    left = [rows[at + 72:at + 144] for at in range(0, rows.shape[0], 144)]
    return jnp.concatenate(right, axis=0).astype(BF), jnp.concatenate(left, axis=0).astype(BF)


def project(x, w3, ones, srow, first=None):
    q = unit(dot_nt(x[:first], w3[0]).astype(BF), ones[...], srow[...])
    k = unit(dot_nt(x, w3[1]).astype(BF), ones[...])
    return q, k, dot_nt(x, w3[2]).astype(BF)


def first_kernel(right, left, classes, w3, out, ones, lanes, srow, hr, hl):
    wide = windows_of(right[144:432].astype(F32), left[144:432].astype(F32))
    q, k, v = project(wide.astype(BF), w3, ones, srow)
    att = []
    for at in range(0, 576, 144):
        span = slice(at, at + 144)
        mark = classes[span]
        att.append(heads(q[span], k[span], v[span], lanes[...], mark * lanes[2:3], mark))
    hr[...], hl[...] = halves_of(wide + normed(dot(jnp.concatenate(att, axis=0), out[...])))


def second_kernel(right_all, left_all, down, up, classes, w3, out, ones, lanes, srow, hr, hl):
    right, left = (
        jnp.concatenate([ref[432:].astype(F32), ref[:144].astype(F32)], axis=0)
        for ref in (right_all, left_all)
    )
    wide = windows_of(right, left)
    x = jnp.concatenate([wide.astype(BF), down[:144], up[...]], axis=0)
    q, k, v = project(x, w3, ones, srow, 576)
    got = down[144:216]
    far = jnp.concatenate([got[:, b * 128:b * 128 + 128].astype(F32) for b in range(4)], axis=0)
    far = far.astype(BF)
    att = []
    for at in (0, 144):
        span = slice(at, at + 144)
        mark = classes[576 + at:720 + at]
        att.append(heads(q[span], k[span], v[span], lanes[...], mark * lanes[2:3], mark))
    marks = (jnp.concatenate([far[144:], far[:144]], axis=0), classes[864:1152])
    for e in range(2):
        own, ext = slice(288 + e * 144, 432 + e * 144), slice(576 + e * 144, 720 + e * 144)
        keys = jnp.concatenate([k[own], k[ext]], axis=0)
        values = jnp.concatenate([v[own], v[ext]], axis=0)
        att.append(
            heads(q[own], keys, values, lanes[...], marks[e][:144] * lanes[2:3], marks[e])
        )
    hr[...], hl[...] = halves_of(wide + normed(dot(jnp.concatenate(att, axis=0), out[...])))


def feed_one(h, expand, shrink):
    acc = None
    for c in range(4):
        span = slice(c * 512, c * 512 + 512)
        grown = gelu(dot(h, expand[:, span])).astype(BF)
        term = dot(grown, shrink[span, :])
        acc = term if acc is None else acc + term
    return (h.astype(F32) + normed(acc)).astype(BF)


def feed_kernel(h1, h2, expand, shrink, out1, out2):
    got = feed_one(jnp.concatenate([h1[...], h2[...]], axis=0), expand, shrink)
    out1[...] = got[:288]
    out2[...] = got[288:]


def feed_some_kernel(h, expand, shrink, out):
    out[...] = feed_one(h[...], expand, shrink)


def merge_kernel(l1, l2, r1, r2, pm, weight, coarse, ball, *, g):
    for half, (one, two) in enumerate(((l1, l2), (r1, r2))):
        for n, block in enumerate((two[144:], (one[:144], one[144:])[g], (one[144:], two[:144])[g])):
            ball[288 * n + half * 144:288 * n + half * 144 + 144] = block
    picked = dot(pm[g], ball[...])
    quartet = jnp.concatenate([picked[m * 144:m * 144 + 144] for m in range(4)], axis=1)
    coarse[...] = dot(normed(quartet).astype(BF), weight[...]).astype(BF)


def skip_kernel(l1, l2, r1, r2, perm, skip):
    for half, (one, two) in enumerate(((l1, l2), (r1, r2))):
        own = jnp.concatenate([two[144:], one[...], two[:144]], axis=0)
        got = dot(perm[...], own).astype(BF)
        for l in range(4):
            at = l * 288 + half * 144
            skip[at:at + 144] = got[l * 144:l * 144 + 144]


def attend_two_kernel(me, own, other, w3, ones, lanes, srow, x_out, att_out):
    a, b = own[...].astype(F32), other[...].astype(F32)
    first = me[0] == 0
    t0, t1 = jnp.where(first, a, b), jnp.where(first, b, a)
    x = jnp.concatenate([t0[:72], t1[:72], t0[72:], t1[72:]], axis=0).astype(BF)
    x_out[...] = x
    q = unit(dot_nt(x, w3[0]).astype(BF), ones[...], srow[...])
    k = unit(dot_nt(x, w3[1]).astype(BF), ones[...])
    v = dot_nt(x, w3[2]).astype(BF)
    for lg in range(2):
        span = slice(lg * 144, lg * 144 + 144)
        att_out[span] = heads(q[span], k[span], v[span], lanes[...])


def feed_two_kernel(me, x, mine, theirs, o_mine, o_theirs, expand, shrink, keep, send, hid_own):
    branch = dot(mine[...], o_mine[...]) + dot(theirs[...], o_theirs[...])
    hid = (x[...].astype(F32) + normed(branch)).astype(BF)
    acc = None
    for c in range(4):
        span = slice(c * 512, c * 512 + 512)
        grown = gelu(dot_nt(hid, expand[span, :])).astype(BF)
        term = dot(grown, shrink[span, :])
        acc = term if acc is None else acc + term
    first = me[0] == 0

    def split(values):
        p0 = jnp.concatenate([values[0:72], values[144:216]], axis=0)
        p1 = jnp.concatenate([values[72:144], values[216:288]], axis=0)
        return jnp.where(first, p0, p1), jnp.where(first, p1, p0)

    own, far = split(acc)
    keep[...] = own
    send[...] = far.astype(BF)
    hid_own[...] = split(hid.astype(F32))[0].astype(BF)


def finish_rows(k, r, h, pout):
    done = (h[...].astype(F32) + normed(k[...] + r[...].astype(F32))).astype(BF)
    return dot(pout[...], done).reshape(6, 6, 4, 1024).astype(BF)


def finish_first_kernel(k, r, h, pout, rows):
    rows[...] = finish_rows(k, r, h, pout)


def finish_kernel(first, k, r, h, pout, coarse):
    coarse[:6] = first[...]
    coarse[6:] = finish_rows(k, r, h, pout)


def behind(value, axis, steps):
    count = lax.axis_size(axis)
    return lax.ppermute(value, axis, [(s, (s + steps) % count) for s in range(count)])


def after(value, done):
    return lax.optimization_barrier((value, done))[0]


def across(value, axis, flip):
    return lax.ppermute(value, axis, [(s, s ^ flip) for s in range(lax.axis_size(axis))])


def shards(
    patches,
    region_ids,
    triple_one,
    output_one,
    expand_one,
    shrink_one,
    scales_one,
    merge_weight,
    triple_two,
    output_two,
    expand_two,
    shrink_two,
    scales_two,
):
    me = lax.axis_index("tp").astype(jnp.int32).reshape(1)
    lat_at = (lax.axis_index("lat") & 3).astype(jnp.int32).reshape(1)
    ones = const(np.kron(np.eye(4), np.ones((64, 64))))
    lane_of = np.zeros((8, 128), np.float32)
    lane_of[0, :64] = 1
    lane_of[1, 64:] = 1
    lane_of[2] = MASK
    lane_of[2, 8] = -MASK
    lanes = const(lane_of)
    spread = const(np.kron(np.eye(8), np.ones((1, 64))))
    col_axes = ("lon", "tp")
    tok = lambda n: ((n, 512), BF)

    flat = patches.transpose(0, 2, 1, 3).reshape(1152, 512)
    left, right = call(
        pack_kernel,
        [tok(576)] * 2,
        [flat],
        10**9,
    )
    region_ids = after(region_ids, right)
    left = behind(left, col_axes, -1)
    pick, keep = pick_rows()
    classes, s_one, s_two, quarter = call(
        ready_kernel,
        [((1152, 128), BF), ((1, 512), F32), ((1, 512), F32), ((128, 1024), BF)],
        [
            lat_at,
            region_ids.transpose(2, 0, 1),
            const(pick),
            const(keep),
            scales_one.reshape(1, 8),
            scales_two.reshape(1, 8),
            spread,
            output_two,
        ],
        10**9,
        smem=(0,),
        hbm=(7,),
        scratch=[pltpu.SemaphoreType.DMA],
    )
    quarter = after(quarter, left)
    oa = behind(quarter, "tp", 1)
    down, up = call(rim_kernel, [tok(216), tok(144)], [left, right, classes], 10**6)
    classes = after(classes, down)
    down, up = behind(down, "lat", 1), behind(up, "lat", -1)

    w_one = triple_one.transpose(1, 0, 2)
    shared = [classes, w_one, output_one, ones, lanes, s_one]
    hr1, hl1 = call(first_kernel, [tok(288)] * 2, [right, left] + shared, 4 * 10**9)
    hl1 = behind(hl1, col_axes, 1)
    shared[0] = after(classes, hr1)
    hr2, hl2 = call(
        second_kernel, [tok(288)] * 2, [right, left, down, up] + shared, 6 * 10**9
    )
    hl2 = behind(hl2, col_axes, 1)

    feeds = [expand_one, shrink_one]
    br1, br2 = call(feed_kernel, [tok(288)] * 2, [hr1, hr2] + feeds, 3 * 10**9)
    oa = after(oa, br1)
    ob, oc = across(oa, "lat", 1), across(oa, "lat", 2)
    bl1 = call(feed_some_kernel, [tok(288)], [after(hl1, br1)] + feeds, 2 * 10**9)[0]
    bl2 = call(feed_some_kernel, [tok(288)], [after(hl2, bl1)] + feeds, 2 * 10**9)[0]
    blocks = [bl1, bl2, br1, br2]
    od = across(after(oc, bl2), "lat", 1)
    pm, coarse_in = const(merge_rows()), []
    for g in range(2):
        if g:
            blocks = [after(blocks[0], coarse_in[0])] + blocks[1:]
        coarse_in += call(
            functools.partial(merge_kernel, g=g),
            [((144, 1024), BF)],
            blocks + [pm, merge_weight],
            10**9,
            scratch=[pltpu.VMEM((864, 512), BF)],
        )
    c0, c1 = coarse_in
    d0, d1 = behind(c0, "tp", 1), behind(c1, "tp", 1)
    blocks[0], od = after(blocks[0], c1), after(od, c1)
    skip = call(skip_kernel, [tok(1152)], blocks + [const(home_rows())], 2 * 10**9)[0]
    o_theirs = call(
        join_kernel, [((512, 1024), BF)], [lat_at, oa, ob, oc, od], 10**9, smem=(0,)
    )[0]
    c0, skip, o_theirs = lax.optimization_barrier((c0, skip, o_theirs))
    skip = skip.reshape(4, 12, 24, 512).transpose(0, 2, 1, 3)

    w_two = triple_two.transpose(1, 0, 2)
    attended = []
    for own, other in ((c0, d0), (c1, d1)):
        if attended:
            own = after(own, attended[0][1])
        x, mine = call(
            attend_two_kernel,
            [((288, 1024), BF), tok(288)],
            [me, own, other, w_two, ones, lanes, s_two],
            2 * 10**9,
            smem=(0,),
        )
        attended.append((x, mine, behind(mine, "tp", 1)))
    kept = []
    for x, mine, theirs in attended:
        if kept:
            x = after(x, kept[0][0])
        keep, send, hid_own = call(
            feed_two_kernel,
            [((144, 1024), F32), ((144, 1024), BF), ((144, 1024), BF)],
            [me, x, mine, theirs, output_two, o_theirs, expand_two, shrink_two],
            10**8,
            smem=(0,),
        )
        kept.append((keep, behind(send, "tp", 1), hid_own))
    pout = const(coarse_rows())
    first = call(finish_first_kernel, [((6, 6, 4, 1024), BF)], [*kept[0], pout], 10**8)[0]
    coarse = call(finish_kernel, [((12, 6, 4, 1024), BF)], [first, *kept[1], pout], 10**8)[0]
    return (skip, coarse.transpose(2, 0, 1, 3))


def solution(mesh):
    in_specs = (
        P(None, "lat", ("lon", "tp"), None),
        P(None, "lat", ("lon", "tp")),
        P(),
        P(),
        P(),
        P(),
        P(),
        P(),
        P("tp", None, None),
        P("tp", None),
        P("tp", None),
        P("tp", None),
        P("tp"),
    )
    out_specs = (P(None, "lat", ("lon", "tp"), None), P(None, "lat", ("lon", "tp"), None))
    return jax.shard_map(shards, mesh=mesh, in_specs=in_specs, out_specs=out_specs, check_vma=False)
```

profile of v0, /device:TPU:0, one launch (start us, length us, event | category | flops | bytes accessed | tf_op | source)
XLA Modules:
  0.0 99.6 jit_solution(2635782924685990490)
XLA Ops:
  0.6 0.0 copy-start.19
  0.7 1.4 %copy-done.10 = bf16[4,24,12,512]{3,1,2,0:T(8,128)(2,1)S(1)} copy-done((bf16[4,24,12,512]{3,1,2,0:T(8,128)(2,1)S(1)}, bf16[4,24,12,512]{3,1,2,0:T(8,128)(2,1)}, u32[]{:S(2)}) %copy-start.10) | copy-done | bytes 1179672
  2.0 0.0 copy-start.17
  2.0 0.5 shard_map.212
  2.5 6.6 %collective-permute-start = (bf16[576,512]{1,0:T(8,128)(2,1)S(1)}, bf16[576,512]{1,0:T(8,128)(2,1)S(1)}, u32[]{:S(2)}, u32[]{:S(2)}) collective-permute-start(bf16[576,512]{1,0:T(8,128)(2,1)S(1)} %get-tuple-element.43), channel_id=1, source_target_pairs={{0,15},{1,0},{2,1},{3,2},{4,3},{5,4},{6,5},{7,6},{8,7},{9,8},{10,9... | collective-permute-start | bytes 1769480 | tf_op jit(solution)/shard_map/ppermute | solution.py:356
  9.2 0.0 copy-start.18
  9.2 0.0 copy-start.20
  9.2 0.4 shard_map.213
  9.6 12.1 %collective-permute-done.left_all.left = bf16[576,512]{1,0:T(8,128)(2,1)S(1)} collective-permute-done((bf16[576,512]{1,0:T(8,128)(2,1)S(1)}, bf16[576,512]{1,0:T(8,128)(2,1)S(1)}, u32[]{:S(2)}, u32[]{:S(2)}) %collective-permute-start) | collective-permute-done | bytes 589856 | tf_op jit(solution)/shard_map/ppermute | solution.py:356
  21.8 0.0 collective-permute-start.2
  21.8 2.9 %collective-permute-start.3 = (bf16[144,512]{1,0:T(8,128)(2,1)S(1)}, bf16[144,512]{1,0:T(8,128)(2,1)S(1)}, u32[]{:S(2)}, u32[]{:S(2)}) collective-permute-start(bf16[144,512]{1,0:T(8,128)(2,1)S(1)} %get-tuple-element.51), channel_id=1, source_target_pairs={{0,112},{16,0},{32,16},{48,32},{64,48},{80,64},{96,80},{112,96},{1... | collective-permute-start | bytes 442376 | tf_op jit(solution)/shard_map/ppermute | solution.py:356
  24.7 3.4 %shard_map.215 = (bf16[288,512]{1,0:T(8,128)(2,1)S(1)}, bf16[288,512]{1,0:T(8,128)(2,1)S(1)}) custom-call(bf16[576,512]{1,0:T(8,128)(2,1)S(1)} %get-tuple-element.42.right_all.right, bf16[576,512]{1,0:T(8,128)(2,1)S(1)} %collective-permute-done.left_all.left, bf16[1152,128]{1,0:T(8,128)(2,1)S(1)} %get-tuple-element.52.classes, ...), custom_call_target="tpu_custom_call" | custom-call | flops 4000000000 | bytes 3706880 | tf_op jit(solution)/shard_map/pallas_call | solution.py:149
  28.1 1.7 %collective-permute-start.1 = (bf16[288,512]{1,0:T(8,128)(2,1)S(1)}, bf16[288,512]{1,0:T(8,128)(2,1)S(1)}, u32[]{:S(2)}, u32[]{:S(2)}) collective-permute-start(bf16[288,512]{1,0:T(8,128)(2,1)S(1)} %get-tuple-element.49), channel_id=1, source_target_pairs={{0,1},{1,2},{2,3},{3,4},{4,5},{5,6},{6,7},{7,8},{8,9},{9,10},{10,1... | collective-permute-start | bytes 884744 | tf_op jit(solution)/shard_map/ppermute | solution.py:356
  29.8 0.8 collective-permute-start.5
  30.6 4.4 %shard_map.216 = (bf16[288,512]{1,0:T(8,128)(2,1)S(1)}, bf16[288,512]{1,0:T(8,128)(2,1)S(1)}) custom-call(bf16[576,512]{1,0:T(8,128)(2,1)S(1)} %get-tuple-element.42.right_all.right, bf16[576,512]{1,0:T(8,128)(2,1)S(1)} %collective-permute-done.left_all.left, bf16[216,512]{1,0:T(8,128)(2,1)S(1)} %collective-permute-done.2.down, ...), custom_call_target="tpu_custom_call" | custom-call | flops 6000000000 | bytes 4075520 | tf_op jit(solution)/shard_map/pallas_call | solution.py:149
  34.9 3.0 %collective-permute-start.4 = (bf16[288,512]{1,0:T(8,128)(2,1)S(1)}, bf16[288,512]{1,0:T(8,128)(2,1)S(1)}, u32[]{:S(2)}, u32[]{:S(2)}) collective-permute-start(bf16[288,512]{1,0:T(8,128)(2,1)S(1)} %get-tuple-element.56), channel_id=1, source_target_pairs={{0,1},{1,2},{2,3},{3,4},{4,5},{5,6},{6,7},{7,8},{8,9},{9,10},{10,1... | collective-permute-start | bytes 884744 | tf_op jit(solution)/shard_map/ppermute | solution.py:356
  37.9 3.3 %shard_map.217 = (bf16[288,512]{1,0:T(8,128)(2,1)S(1)}, bf16[288,512]{1,0:T(8,128)(2,1)S(1)}) custom-call(bf16[288,512]{1,0:T(8,128)(2,1)S(1)} %get-tuple-element.50.h1, bf16[288,512]{1,0:T(8,128)(2,1)S(1)} %get-tuple-element.53.h2, bf16[512,2048]{1,0:T(8,128)(2,1)S(1)} %copy-done.7, bf16[2048,512]{1,0:T(8,128)(2,1)S(1)} %copy-done.8), custom_call_target="tpu_custom_call" | custom-call | flops 3000000000 | bytes 4784128 | tf_op jit(solution)/shard_map/pallas_call | solution.py:149
  41.3 2.8 %collective-permute-done.5.a = bf16[128,1024]{1,0:T(8,128)(2,1)S(1)} collective-permute-done((bf16[128,1024]{1,0:T(8,128)(2,1)S(1)}, bf16[128,1024]{1,0:T(8,128)(2,1)S(1)}, u32[]{:S(2)}, u32[]{:S(2)}) %collective-permute-start.5) | collective-permute-done | bytes 262176 | tf_op jit(solution)/shard_map/ppermute | solution.py:356
  44.1 0.2 collective-permute-start.7
  44.3 3.2 %collective-permute-done.1.h = bf16[288,512]{1,0:T(8,128)(2,1)S(1)} collective-permute-done((bf16[288,512]{1,0:T(8,128)(2,1)S(1)}, bf16[288,512]{1,0:T(8,128)(2,1)S(1)}, u32[]{:S(2)}, u32[]{:S(2)}) %collective-permute-start.1) | collective-permute-done | bytes 294944 | tf_op jit(solution)/shard_map/ppermute | solution.py:356
  47.5 2.0 %shard_map.218.l1 = bf16[288,512]{1,0:T(8,128)(2,1)S(1)} custom-call(bf16[288,512]{1,0:T(8,128)(2,1)S(1)} %collective-permute-done.1.h, bf16[512,2048]{1,0:T(8,128)(2,1)S(1)} %copy-done.7, bf16[2048,512]{1,0:T(8,128)(2,1)S(1)} %copy-done.8), custom_call_target="tpu_custom_call" | custom-call | flops 2000000000 | bytes 4489216 | tf_op jit(solution)/shard_map/pallas_call | solution.py:149
  49.5 0.0 copy-start.3
  49.5 2.2 %collective-permute-done.4.h = bf16[288,512]{1,0:T(8,128)(2,1)S(1)} collective-permute-done((bf16[288,512]{1,0:T(8,128)(2,1)S(1)}, bf16[288,512]{1,0:T(8,128)(2,1)S(1)}, u32[]{:S(2)}, u32[]{:S(2)}) %collective-permute-start.4) | collective-permute-done | bytes 294944 | tf_op jit(solution)/shard_map/ppermute | solution.py:356
  51.7 2.0 %shard_map.219.l2 = bf16[288,512]{1,0:T(8,128)(2,1)S(1)} custom-call(bf16[288,512]{1,0:T(8,128)(2,1)S(1)} %collective-permute-done.4.h, bf16[512,2048]{1,0:T(8,128)(2,1)S(1)} %copy-done.7, bf16[2048,512]{1,0:T(8,128)(2,1)S(1)} %copy-done.8), custom_call_target="tpu_custom_call" | custom-call | flops 2000000000 | bytes 4489216 | tf_op jit(solution)/shard_map/pallas_call | solution.py:149
  53.8 1.8 %shard_map.220.own = bf16[144,1024]{1,0:T(8,128)(2,1)S(1)} custom-call(bf16[288,512]{1,0:T(8,128)(2,1)S(1)} %shard_map.218.l1, bf16[288,512]{1,0:T(8,128)(2,1)S(1)} %shard_map.219.l2, bf16[288,512]{1,0:T(8,128)(2,1)S(1)} %get-tuple-element.54.r1, bf16[288,512]{1,0:T(8,128)(2,1)S(1)} %get-tuple-element.58.r2, bf16[2,576,864]{2,1,0:T(8,128)(2,1)S(1)} %copy-done.3, ...), custom_call_target="tpu_custom_call" | custom-call | flops 1000000000 | bytes 7364608 | tf_op jit(solution)/shard_map/pallas_call | solution.py:149
  55.6 0.0 copy-start.15
  55.6 0.1 collective-permute-start.9
  55.7 0.1 collective-permute-start.8
  55.8 1.8 %shard_map.221.own = bf16[144,1024]{1,0:T(8,128)(2,1)S(1)} custom-call(bf16[288,512]{1,0:T(8,128)(2,1)S(1)} %shard_map.218.l1, bf16[288,512]{1,0:T(8,128)(2,1)S(1)} %shard_map.219.l2, bf16[288,512]{1,0:T(8,128)(2,1)S(1)} %get-tuple-element.54.r1, bf16[288,512]{1,0:T(8,128)(2,1)S(1)} %get-tuple-element.58.r2, bf16[2,576,864]{2,1,0:T(8,128)(2,1)S(1)} %copy-done.3, ...), custom_call_target="tpu_custom_call" | custom-call | flops 1000000000 | bytes 7364608 | tf_op jit(solution)/shard_map/pallas_call | solution.py:149
  57.5 3.7 %collective-permute-start.12 = (bf16[144,1024]{1,0:T(8,128)(2,1)S(1)}, bf16[144,1024]{1,0:T(8,128)(2,1)S(1)}, u32[]{:S(2)}, u32[]{:S(2)}) collective-permute-start(bf16[144,1024]{1,0:T(8,128)(2,1)S(1)} %shard_map.221.own), channel_id=1, source_target_pairs={{0,1},{1,0},{2,3},{3,2},{4,5},{5,4},{6,7},{7,6},{8,9},{9,8},{10,11... | collective-permute-start | bytes 884744 | tf_op jit(solution)/shard_map/ppermute | solution.py:356
  61.3 2.1 %shard_map.222 = bf16[1152,512]{1,0:T(8,128)(2,1)} custom-call(bf16[288,512]{1,0:T(8,128)(2,1)S(1)} %shard_map.218.l1, bf16[288,512]{1,0:T(8,128)(2,1)S(1)} %shard_map.219.l2, bf16[288,512]{1,0:T(8,128)(2,1)S(1)} %get-tuple-element.54.r1, bf16[288,512]{1,0:T(8,128)(2,1)S(1)} %get-tuple-element.58.r2, bf16[576,576]{1,0:T(8,128)(2,1)S(1)} %copy-done.15), custom_call_target="tpu_custom_call" | custom-call | flops 2000000000 | bytes 1843200 | tf_op jit(solution)/shard_map/pallas_call | solution.py:149
  63.4 0.1 shard_map.223.o_theirs
  63.5 2.0 %collective-permute-done.9.other = bf16[144,1024]{1,0:T(8,128)(2,1)S(1)} collective-permute-done((bf16[144,1024]{1,0:T(8,128)(2,1)S(1)}, bf16[144,1024]{1,0:T(8,128)(2,1)S(1)}, u32[]{:S(2)}, u32[]{:S(2)}) %collective-permute-start.9) | collective-permute-done | bytes 294944 | tf_op jit(solution)/shard_map/ppermute | solution.py:356
  65.5 2.2 %shard_map.224 = (bf16[288,1024]{1,0:T(8,128)(2,1)S(1)}, bf16[288,512]{1,0:T(8,128)(2,1)S(1)}) custom-call(s32[1]{0:T(128)} %bitcast.9.me, bf16[144,1024]{1,0:T(8,128)(2,1)S(1)} %shard_map.220.own, bf16[144,1024]{1,0:T(8,128)(2,1)S(1)} %collective-permute-done.9.other, bf16[3,512,1024]{2,1,0:T(8,128)(2,1)S(1)} %bitcast.14, bf16[256,256]{1,0:T(8,128)(2,1)S(1)} %copy-done.18, ...), custom_call_target="tpu_custom_call" | custom-call | flops 2000000000 | bytes 3870724 | tf_op jit(solution)/shard_map/pallas_call | solution.py:149
  67.7 0.1 collective-permute-start.10
  67.8 2.6 %collective-permute-done.12.other = bf16[144,1024]{1,0:T(8,128)(2,1)S(1)} collective-permute-done((bf16[144,1024]{1,0:T(8,128)(2,1)S(1)}, bf16[144,1024]{1,0:T(8,128)(2,1)S(1)}, u32[]{:S(2)}, u32[]{:S(2)}) %collective-permute-start.12) | collective-permute-done | bytes 294944 | tf_op jit(solution)/shard_map/ppermute | solution.py:356
  70.4 2.2 %shard_map.227 = (bf16[288,1024]{1,0:T(8,128)(2,1)S(1)}, bf16[288,512]{1,0:T(8,128)(2,1)S(1)}) custom-call(s32[1]{0:T(128)} %bitcast.9.me, bf16[144,1024]{1,0:T(8,128)(2,1)S(1)} %shard_map.221.own, bf16[144,1024]{1,0:T(8,128)(2,1)S(1)} %collective-permute-done.12.other, bf16[3,512,1024]{2,1,0:T(8,128)(2,1)S(1)} %bitcast.15, bf16[256,256]{1,0:T(8,128)(2,1)S(1)} %copy-done.18, ...), custom_call_target="tpu_custom_call" | custom-call | flops 2000000000 | bytes 3870724 | tf_op jit(solution)/shard_map/pallas_call | solution.py:149
  72.6 1.8 %collective-permute-start.13 = (bf16[288,512]{1,0:T(8,128)(2,1)S(1)}, bf16[288,512]{1,0:T(8,128)(2,1)S(1)}, u32[]{:S(2)}, u32[]{:S(2)}) collective-permute-start(bf16[288,512]{1,0:T(8,128)(2,1)S(1)} %get-tuple-element.78.mine), channel_id=1, source_target_pairs={{0,1},{1,0},{2,3},{3,2},{4,5},{5,4},{6,7},{7,6},{8,9},{9,8},{10,11... | collective-permute-start | bytes 884744 | tf_op jit(solution)/shard_map/ppermute | solution.py:356
  74.5 4.7 %collective-permute-done.10.theirs = bf16[288,512]{1,0:T(8,128)(2,1)S(1)} collective-permute-done((bf16[288,512]{1,0:T(8,128)(2,1)S(1)}, bf16[288,512]{1,0:T(8,128)(2,1)S(1)}, u32[]{:S(2)}, u32[]{:S(2)}) %collective-permute-start.10) | collective-permute-done | bytes 294944 | tf_op jit(solution)/shard_map/ppermute | solution.py:356
  79.2 4.1 %shard_map.225 = (f32[144,1024]{1,0:T(8,128)S(1)}, bf16[144,1024]{1,0:T(8,128)(2,1)S(1)}, bf16[144,1024]{1,0:T(8,128)(2,1)S(1)}) custom-call(s32[1]{0:T(128)} %bitcast.9.me, bf16[288,1024]{1,0:T(8,128)(2,1)S(1)} %get-tuple-element.69.x, bf16[288,512]{1,0:T(8,128)(2,1)S(1)} %get-tuple-element.70.mine, bf16[288,512]{1,0:T(8,128)(2,1)S(1)} %collective-permute-done.10.theirs, ...), custom_call_target="tpu_custom_call" | custom-call | flops 100000000 | bytes 11665412 | tf_op jit(solution)/shard_map/pallas_call | solution.py:149
  83.3 0.1 collective-permute-start.11
  83.4 1.1 %collective-permute-done.13.theirs = bf16[288,512]{1,0:T(8,128)(2,1)S(1)} collective-permute-done((bf16[288,512]{1,0:T(8,128)(2,1)S(1)}, bf16[288,512]{1,0:T(8,128)(2,1)S(1)}, u32[]{:S(2)}, u32[]{:S(2)}) %collective-permute-start.13) | collective-permute-done | bytes 294944 | tf_op jit(solution)/shard_map/ppermute | solution.py:356
  84.5 4.1 %shard_map.228 = (f32[144,1024]{1,0:T(8,128)S(1)}, bf16[144,1024]{1,0:T(8,128)(2,1)S(1)}, bf16[144,1024]{1,0:T(8,128)(2,1)S(1)}) custom-call(s32[1]{0:T(128)} %bitcast.9.me, bf16[288,1024]{1,0:T(8,128)(2,1)S(1)} %get-tuple-element.77.x, bf16[288,512]{1,0:T(8,128)(2,1)S(1)} %get-tuple-element.78.mine, bf16[288,512]{1,0:T(8,128)(2,1)S(1)} %collective-permute-done.13.theirs, ...), custom_call_target="tpu_custom_call" | custom-call | flops 100000000 | bytes 11665412 | tf_op jit(solution)/shard_map/pallas_call | solution.py:149
  88.6 2.5 %collective-permute-start.14 = (bf16[144,1024]{1,0:T(8,128)(2,1)S(1)}, bf16[144,1024]{1,0:T(8,128)(2,1)S(1)}, u32[]{:S(2)}, u32[]{:S(2)}) collective-permute-start(bf16[144,1024]{1,0:T(8,128)(2,1)S(1)} %get-tuple-element.80), channel_id=1, source_target_pairs={{0,1},{1,0},{2,3},{3,2},{4,5},{5,4},{6,7},{7,6},{8,9},{9,8},{10,11... | collective-permute-start | bytes 884744 | tf_op jit(solution)/shard_map/ppermute | solution.py:356
  91.1 0.8 collective-permute-done.11.r
  91.9 0.5 shard_map.226.first
  92.4 5.8 %collective-permute-done.14.r = bf16[144,1024]{1,0:T(8,128)(2,1)S(1)} collective-permute-done((bf16[144,1024]{1,0:T(8,128)(2,1)S(1)}, bf16[144,1024]{1,0:T(8,128)(2,1)S(1)}, u32[]{:S(2)}, u32[]{:S(2)}) %collective-permute-start.14) | collective-permute-done | bytes 294944 | tf_op jit(solution)/shard_map/ppermute | solution.py:356
  98.3 1.3 %shard_map.229 = bf16[12,6,4,1024]{3,2,1,0:T(4,128)(2,1)} custom-call(bf16[6,6,4,1024]{3,2,1,0:T(4,128)(2,1)S(1)} %shard_map.226.first, f32[144,1024]{1,0:T(8,128)S(1)} %get-tuple-element.79.k, bf16[144,1024]{1,0:T(8,128)(2,1)S(1)} %collective-permute-done.14.r, bf16[144,1024]{1,0:T(8,128)(2,1)S(1)} %get-tuple-element.81.h, bf16[144,144]{1,0:T(8,128)(2,1)S(1)} %copy-done.5), custom_call_target="tpu_custom_call" | custom-call | flops 100000000 | bytes 1516032 | tf_op jit(solution)/shard_map/pallas_call | solution.py:149
  (42 shorter events, 0.1 us)
Async XLA Ops:
  0.6 8.5 %copy-start.19 = (bf16[8,512]{1,0:T(8,128)(2,1)S(1)}, bf16[8,512]{1,0:T(8,128)(2,1)}, u32[]{:S(2)}) copy-start(bf16[8,512]{1,0:T(8,128)(2,1)} %constant.30.clone.spread) | copy-start | bytes 24580
  0.6 8.5 %copy-start.4 = (bf16[512,1024]{1,0:T(8,128)(2,1)S(1)}, bf16[512,1024]{1,0:T(8,128)(2,1)}, u32[]{:S(2)}) copy-start(bf16[512,1024]{1,0:T(8,128)(2,1)} %o_mine.3) | copy-start | bytes 3145732
  0.7 1.4 %copy-start.10 = (bf16[4,24,12,512]{3,1,2,0:T(8,128)(2,1)S(1)}, bf16[4,24,12,512]{3,1,2,0:T(8,128)(2,1)}, u32[]{:S(2)}) copy-start(bf16[4,24,12,512]{3,1,2,0:T(8,128)(2,1)} %param.21) | copy-start | bytes 3538948
  2.0 7.1 %copy-start.12 = (s32[4,24,12]{1,0,2:T(4,128)S(1)}, s32[4,24,12]{1,0,2:T(4,128)}, u32[]{:S(2)}) copy-start(s32[4,24,12]{1,0,2:T(4,128)} %param.22) | copy-start | bytes 13828
  2.0 7.1 %copy-start.13 = (bf16[8]{0:T(256)(128)(2,1)S(1)}, bf16[8]{0:T(256)(128)(2,1)}, u32[]{:S(2)}) copy-start(bf16[8]{0:T(256)(128)(2,1)} %param.27) | copy-start | bytes 52
  2.0 7.1 %copy-start.14 = (bf16[8]{0:T(256)(128)(2,1)S(1)}, bf16[8]{0:T(256)(128)(2,1)}, u32[]{:S(2)}) copy-start(bf16[8]{0:T(256)(128)(2,1)} %param.33) | copy-start | bytes 52
  2.0 7.1 %copy-start.16 = (bf16[1152,48]{1,0:T(8,128)(2,1)S(1)}, bf16[1152,48]{1,0:T(8,128)(2,1)}, u32[]{:S(2)}) copy-start(bf16[1152,48]{1,0:T(8,128)(2,1)} %constant.31.clone.rows) | copy-start | bytes 331780
  2.0 7.1 %copy-start.17 = (bf16[1152,25]{1,0:T(8,128)(2,1)S(1)}, bf16[1152,25]{1,0:T(8,128)(2,1)}, u32[]{:S(2)}) copy-start(bf16[1152,25]{1,0:T(8,128)(2,1)} %constant.32.clone.keep) | copy-start | bytes 172804
  2.5 19.2 %collective-permute-start = (bf16[576,512]{1,0:T(8,128)(2,1)S(1)}, bf16[576,512]{1,0:T(8,128)(2,1)S(1)}, u32[]{:S(2)}, u32[]{:S(2)}) collective-permute-start(bf16[576,512]{1,0:T(8,128)(2,1)S(1)} %get-tuple-element.43), channel_id=1, source_target_pairs={{0,15},{1,0},{2,1},{3,2},{4,3},{5,4},{6,5},{7,6},{8,7},{9,8},{10,9... | collective-permute-start | bytes 1769480 | tf_op jit(solution)/shard_map/ppermute | solution.py:356
  9.2 15.5 %copy-start.9 = (bf16[512,3,512]{2,0,1:T(8,128)(2,1)S(1)}, bf16[512,3,512]{2,0,1:T(8,128)(2,1)}, u32[]{:S(2)}) copy-start(bf16[512,3,512]{2,0,1:T(8,128)(2,1)} %param.23) | copy-start | bytes 4718596
  9.2 15.5 %copy-start.11 = (bf16[512,512]{1,0:T(8,128)(2,1)S(1)}, bf16[512,512]{1,0:T(8,128)(2,1)}, u32[]{:S(2)}) copy-start(bf16[512,512]{1,0:T(8,128)(2,1)} %out.3) | copy-start | bytes 1572868
  9.2 15.5 %copy-start.18 = (bf16[256,256]{1,0:T(8,128)(2,1)S(1)}, bf16[256,256]{1,0:T(8,128)(2,1)}, u32[]{:S(2)}) copy-start(bf16[256,256]{1,0:T(8,128)(2,1)} %constant.28.clone.ones) | copy-start | bytes 393220
  9.2 15.5 %copy-start.20 = (bf16[8,128]{1,0:T(8,128)(2,1)S(1)}, bf16[8,128]{1,0:T(8,128)(2,1)}, u32[]{:S(2)}) copy-start(bf16[8,128]{1,0:T(8,128)(2,1)} %constant.29.clone.lanes) | copy-start | bytes 6148
  21.8 8.8 %collective-permute-start.2 = (bf16[216,512]{1,0:T(8,128)(2,1)S(1)}, bf16[216,512]{1,0:T(8,128)(2,1)S(1)}, u32[]{:S(2)}, u32[]{:S(2)}) collective-permute-start(bf16[216,512]{1,0:T(8,128)(2,1)S(1)} %get-tuple-element.46), channel_id=1, source_target_pairs={{0,16},{16,32},{32,48},{48,64},{64,80},{80,96},{96,112},{112,0},{1... | collective-permute-start | bytes 663560 | tf_op jit(solution)/shard_map/ppermute | solution.py:356
  21.8 8.8 %collective-permute-start.3 = (bf16[144,512]{1,0:T(8,128)(2,1)S(1)}, bf16[144,512]{1,0:T(8,128)(2,1)S(1)}, u32[]{:S(2)}, u32[]{:S(2)}) collective-permute-start(bf16[144,512]{1,0:T(8,128)(2,1)S(1)} %get-tuple-element.51), channel_id=1, source_target_pairs={{0,112},{16,0},{32,16},{48,32},{64,48},{80,64},{96,80},{112,96},{1... | collective-permute-start | bytes 442376 | tf_op jit(solution)/shard_map/ppermute | solution.py:356
  28.1 19.4 %collective-permute-start.1 = (bf16[288,512]{1,0:T(8,128)(2,1)S(1)}, bf16[288,512]{1,0:T(8,128)(2,1)S(1)}, u32[]{:S(2)}, u32[]{:S(2)}) collective-permute-start(bf16[288,512]{1,0:T(8,128)(2,1)S(1)} %get-tuple-element.49), channel_id=1, source_target_pairs={{0,1},{1,2},{2,3},{3,4},{4,5},{5,6},{6,7},{7,8},{8,9},{9,10},{10,1... | collective-permute-start | bytes 884744 | tf_op jit(solution)/shard_map/ppermute | solution.py:356
  29.8 8.2 %copy-start.7 = (bf16[512,2048]{1,0:T(8,128)(2,1)S(1)}, bf16[512,2048]{1,0:T(8,128)(2,1)}, u32[]{:S(2)}) copy-start(bf16[512,2048]{1,0:T(8,128)(2,1)} %expand.7) | copy-start | bytes 6291460
  29.8 8.2 %copy-start.8 = (bf16[2048,512]{1,0:T(8,128)(2,1)S(1)}, bf16[2048,512]{1,0:T(8,128)(2,1)}, u32[]{:S(2)}) copy-start(bf16[2048,512]{1,0:T(8,128)(2,1)} %shrink.7) | copy-start | bytes 6291460
  29.8 14.3 %collective-permute-start.5 = (bf16[128,1024]{1,0:T(8,128)(2,1)S(1)}, bf16[128,1024]{1,0:T(8,128)(2,1)S(1)}, u32[]{:S(2)}, u32[]{:S(2)}) collective-permute-start(bf16[128,1024]{1,0:T(8,128)(2,1)S(1)} %get-tuple-element.62), channel_id=1, source_target_pairs={{0,1},{1,0},{2,3},{3,2},{4,5},{5,4},{6,7},{7,6},{8,9},{9,8},{10,11... | collective-permute-start | bytes 786440 | tf_op jit(solution)/shard_map/ppermute | solution.py:356
  34.9 16.8 %collective-permute-start.4 = (bf16[288,512]{1,0:T(8,128)(2,1)S(1)}, bf16[288,512]{1,0:T(8,128)(2,1)S(1)}, u32[]{:S(2)}, u32[]{:S(2)}) collective-permute-start(bf16[288,512]{1,0:T(8,128)(2,1)S(1)} %get-tuple-element.56), channel_id=1, source_target_pairs={{0,1},{1,2},{2,3},{3,4},{4,5},{5,6},{6,7},{7,8},{8,9},{9,10},{10,1... | collective-permute-start | bytes 884744 | tf_op jit(solution)/shard_map/ppermute | solution.py:356
  44.1 19.3 %collective-permute-start.6 = (bf16[128,1024]{1,0:T(8,128)(2,1)S(1)}, bf16[128,1024]{1,0:T(8,128)(2,1)S(1)}, u32[]{:S(2)}, u32[]{:S(2)}) collective-permute-start(bf16[128,1024]{1,0:T(8,128)(2,1)S(1)} %collective-permute-done.5.a), channel_id=1, source_target_pairs={{0,16},{16,0},{32,48},{48,32},{64,80},{80,64},{96,112},{112,96},{1... | collective-permute-start | bytes 786440 | tf_op jit(solution)/shard_map/ppermute | solution.py:364
  44.1 11.6 %collective-permute-start.7 = (bf16[128,1024]{1,0:T(8,128)(2,1)S(1)}, bf16[128,1024]{1,0:T(8,128)(2,1)S(1)}, u32[]{:S(2)}, u32[]{:S(2)}) collective-permute-start(bf16[128,1024]{1,0:T(8,128)(2,1)S(1)} %collective-permute-done.5.a), channel_id=1, source_target_pairs={{0,32},{16,48},{32,0},{48,16},{64,96},{80,112},{96,64},{112,80},{1... | collective-permute-start | bytes 786440 | tf_op jit(solution)/shard_map/ppermute | solution.py:364
  49.5 4.2 %copy-start.2 = (bf16[2048,1024]{1,0:T(8,128)(2,1)S(1)}, bf16[2048,1024]{1,0:T(8,128)(2,1)}, u32[]{:S(2)}) copy-start(bf16[2048,1024]{1,0:T(8,128)(2,1)} %weight.3) | copy-start | bytes 12582916
  49.5 4.2 %copy-start.3 = (bf16[2,576,864]{2,1,0:T(8,128)(2,1)S(1)}, bf16[2,576,864]{2,1,0:T(8,128)(2,1)}, u32[]{:S(2)}) copy-start(bf16[2,576,864]{2,1,0:T(8,128)(2,1)} %constant.33.clone.pm) | copy-start | bytes 5971972
  55.6 5.7 %copy-start.15 = (bf16[576,576]{1,0:T(8,128)(2,1)S(1)}, bf16[576,576]{1,0:T(8,128)(2,1)}, u32[]{:S(2)}) copy-start(bf16[576,576]{1,0:T(8,128)(2,1)} %constant.34.clone.perm) | copy-start | bytes 1990660
  55.6 9.9 %collective-permute-start.9 = (bf16[144,1024]{1,0:T(8,128)(2,1)S(1)}, bf16[144,1024]{1,0:T(8,128)(2,1)S(1)}, u32[]{:S(2)}, u32[]{:S(2)}) collective-permute-start(bf16[144,1024]{1,0:T(8,128)(2,1)S(1)} %shard_map.220.own), channel_id=1, source_target_pairs={{0,1},{1,0},{2,3},{3,2},{4,5},{5,4},{6,7},{7,6},{8,9},{9,8},{10,11... | collective-permute-start | bytes 884744 | tf_op jit(solution)/shard_map/ppermute | solution.py:356
  55.7 7.7 %collective-permute-start.8 = (bf16[128,1024]{1,0:T(8,128)(2,1)S(1)}, bf16[128,1024]{1,0:T(8,128)(2,1)S(1)}, u32[]{:S(2)}, u32[]{:S(2)}) collective-permute-start(bf16[128,1024]{1,0:T(8,128)(2,1)S(1)} %collective-permute-done.7.c), channel_id=1, source_target_pairs={{0,16},{16,0},{32,48},{48,32},{64,80},{80,64},{96,112},{112,96},{1... | collective-permute-start | bytes 786440 | tf_op jit(solution)/shard_map/ppermute | solution.py:364
  57.5 12.9 %collective-permute-start.12 = (bf16[144,1024]{1,0:T(8,128)(2,1)S(1)}, bf16[144,1024]{1,0:T(8,128)(2,1)S(1)}, u32[]{:S(2)}, u32[]{:S(2)}) collective-permute-start(bf16[144,1024]{1,0:T(8,128)(2,1)S(1)} %shard_map.221.own), channel_id=1, source_target_pairs={{0,1},{1,0},{2,3},{3,2},{4,5},{5,4},{6,7},{7,6},{8,9},{9,8},{10,11... | collective-permute-start | bytes 884744 | tf_op jit(solution)/shard_map/ppermute | solution.py:356
  63.4 2.1 %copy-start.6 = (bf16[512,3,1024]{2,0,1:T(8,128)(2,1)S(1)}, bf16[512,3,1024]{2,0,1:T(8,128)(2,1)}, u32[]{:S(2)}) copy-start(bf16[512,3,1024]{2,0,1:T(8,128)(2,1)} %param.29) | copy-start | bytes 9437188
  65.5 13.7 %copy-start.1 = (bf16[2048,1024]{1,0:T(8,128)(2,1)S(1)}, bf16[2048,1024]{1,0:T(8,128)(2,1)}, u32[]{:S(2)}) copy-start(bf16[2048,1024]{1,0:T(8,128)(2,1)} %shrink.9) | copy-start | bytes 12582916
  67.7 11.5 %copy-start = (bf16[2048,1024]{1,0:T(8,128)(2,1)S(1)}, bf16[2048,1024]{1,0:T(8,128)(2,1)}, u32[]{:S(2)}) copy-start(bf16[2048,1024]{1,0:T(8,128)(2,1)} %expand.9) | copy-start | bytes 12582916
  67.7 11.5 %collective-permute-start.10 = (bf16[288,512]{1,0:T(8,128)(2,1)S(1)}, bf16[288,512]{1,0:T(8,128)(2,1)S(1)}, u32[]{:S(2)}, u32[]{:S(2)}) collective-permute-start(bf16[288,512]{1,0:T(8,128)(2,1)S(1)} %get-tuple-element.70.mine), channel_id=1, source_target_pairs={{0,1},{1,0},{2,3},{3,2},{4,5},{5,4},{6,7},{7,6},{8,9},{9,8},{10,11... | collective-permute-start | bytes 884744 | tf_op jit(solution)/shard_map/ppermute | solution.py:356
  72.6 11.9 %collective-permute-start.13 = (bf16[288,512]{1,0:T(8,128)(2,1)S(1)}, bf16[288,512]{1,0:T(8,128)(2,1)S(1)}, u32[]{:S(2)}, u32[]{:S(2)}) collective-permute-start(bf16[288,512]{1,0:T(8,128)(2,1)S(1)} %get-tuple-element.78.mine), channel_id=1, source_target_pairs={{0,1},{1,0},{2,3},{3,2},{4,5},{5,4},{6,7},{7,6},{8,9},{9,8},{10,11... | collective-permute-start | bytes 884744 | tf_op jit(solution)/shard_map/ppermute | solution.py:356
  83.3 8.6 %collective-permute-start.11 = (bf16[144,1024]{1,0:T(8,128)(2,1)S(1)}, bf16[144,1024]{1,0:T(8,128)(2,1)S(1)}, u32[]{:S(2)}, u32[]{:S(2)}) collective-permute-start(bf16[144,1024]{1,0:T(8,128)(2,1)S(1)} %get-tuple-element.73), channel_id=1, source_target_pairs={{0,1},{1,0},{2,3},{3,2},{4,5},{5,4},{6,7},{7,6},{8,9},{9,8},{10,11... | collective-permute-start | bytes 884744 | tf_op jit(solution)/shard_map/ppermute | solution.py:356
  83.4 8.6 %copy-start.5 = (bf16[144,144]{1,0:T(8,128)(2,1)S(1)}, bf16[144,144]{1,0:T(8,128)(2,1)}, u32[]{:S(2)}) copy-start(bf16[144,144]{1,0:T(8,128)(2,1)} %constant.35.clone.pout) | copy-start | bytes 124420
  88.6 9.6 %collective-permute-start.14 = (bf16[144,1024]{1,0:T(8,128)(2,1)S(1)}, bf16[144,1024]{1,0:T(8,128)(2,1)S(1)}, u32[]{:S(2)}, u32[]{:S(2)}) collective-permute-start(bf16[144,1024]{1,0:T(8,128)(2,1)S(1)} %get-tuple-element.80), channel_id=1, source_target_pairs={{0,1},{1,0},{2,3},{3,2},{4,5},{5,4},{6,7},{7,6},{8,9},{9,8},{10,11... | collective-permute-start | bytes 884744 | tf_op jit(solution)/shard_map/ppermute | solution.py:356
where the time goes:
time: 100 us; the launch traced here: 99.6 us
  waiting for transfers between devices  37.4 us (37%)
  Pallas kernels  36.1 us (36%)
  starting transfers between devices  23.6 us (24%)
  local copies, waits for them, and re-layouts  1.46 us (1%)
    ppermute x12, waiting for transfers between devices, behind(): lax.ppermute(value, axis, [(s, (s + steps) % count) for s in range(count)])  37.4 us
    pallas_call x18, Pallas kernels, call(): pl.pallas_call(kernel, out_shape=[jax.ShapeDtypeStruct(shape, kind) for s...  36.1 us
    ppermute x12, starting transfers between devices, behind(): lax.ppermute(value, axis, [(s, (s + steps) % count) for s in range(count)])  23.3 us
  transfers between devices with their start and end apart: 15, of which 10 were waited for; matrix products, arithmetic and copies ran while one was open for 0% of the time, Pallas kernels for 34%

commit v1 on v0

--- a/solution.py
+++ b/solution.py
@@ -157,28 +157,24 @@
     )(*args)
 
 
-def pack_kernel(x, left, right):
+def pack_kernel(x, out):
     row = lax.broadcasted_iota(jnp.int32, (144, 144), 0)
     col = lax.broadcasted_iota(jnp.int32, (144, 144), 1)
     six = (row * 10923) >> 16
     lat = jnp.where(row < 18, six, jnp.where(row < 36, six + 18, six - 3))
     perm = jnp.where(col == (row - 6 * six) * 24 + lat, 1.0, 0.0).astype(BF)
-    for half, dst in enumerate((left, right)):
-        got = []
-        for level in (1, 2, 3, 0):
-            at = level * 288 + half * 144
-            got.append(dot(perm, x[at:at + 144]))
-        rows = [g[e:e + 18] for e in (0, 18) for g in got]
-        dst[:144] = jnp.concatenate(rows, axis=0).astype(BF)
-        rows = [g[w:w + 36] for w in (36, 72, 108) for g in got]
-        dst[144:] = jnp.concatenate(rows, axis=0).astype(BF)
+    got = [dot(perm, x[level]) for level in (1, 2, 3, 0)]
+    rows = [g[e:e + 18] for e in (0, 18) for g in got]
+    out[:144] = jnp.concatenate(rows, axis=0).astype(BF)
+    rows = [g[w:w + 36] for w in (36, 72, 108) for g in got]
+    out[144:] = jnp.concatenate(rows, axis=0).astype(BF)
 
 
 def ready_kernel(
-    at, ids, rows, keep, sone, stwo, spread, o_two, classes, s_one, s_two, quarter, sem
+    at, ids, rows, keep, sone, stwo, spread, o_two, classes, s_one, s_two, part, sem
 ):
     copy = pltpu.make_async_copy(
-        o_two.at[pl.ds(pl.multiple_of(at[0] * 128, 128), 128)], quarter, sem
+        o_two.at[pl.ds(pl.multiple_of(at[0] * 128, 128), 128)], part, sem
     )
     copy.start()
     for src, dst in ((sone, s_one), (stwo, s_two)):
@@ -198,12 +194,6 @@
     up[...] = jnp.concatenate([right[:72], left[:72]], axis=0).astype(BF)
     wide = jnp.concatenate([marks[b * 72:b * 72 + 72] for b in range(4)], axis=1)
     down[...] = jnp.concatenate([right[72:], left[72:], wide], axis=0).astype(BF)
-
-
-def join_kernel(at, a, b, c, d, out):
-    mine = at[0]
-    for step, part in enumerate((a, b, c, d)):
-        out[pl.ds(pl.multiple_of((mine ^ step) * 128, 128), 128)] = part[...]
 
 
 def windows_of(right, left):
@@ -264,19 +254,13 @@
 
 
 def feed_one(h, expand, shrink):
-    acc = None
-    for c in range(4):
-        span = slice(c * 512, c * 512 + 512)
-        grown = gelu(dot(h, expand[:, span])).astype(BF)
-        term = dot(grown, shrink[span, :])
-        acc = term if acc is None else acc + term
-    return (h.astype(F32) + normed(acc)).astype(BF)
+    grown = gelu(dot(h, expand[...])).astype(BF)
+    return (h.astype(F32) + normed(dot(grown, shrink[...]))).astype(BF)
 
 
 def feed_kernel(h1, h2, expand, shrink, out1, out2):
-    got = feed_one(jnp.concatenate([h1[...], h2[...]], axis=0), expand, shrink)
-    out1[...] = got[:288]
-    out2[...] = got[288:]
+    out1[...] = feed_one(h1[...], expand, shrink)
+    out2[...] = feed_one(h2[...], expand, shrink)
 
 
 def feed_some_kernel(h, expand, shrink, out):
@@ -315,15 +299,15 @@
         att_out[span] = heads(q[span], k[span], v[span], lanes[...])
 
 
-def feed_two_kernel(me, x, mine, theirs, o_mine, o_theirs, expand, shrink, keep, send, hid_own):
+def feed_two_kernel(
+    me, quad, x, mine, theirs, o_mine, oa, ob, oc, od, expand, shrink, keep, send, hid_own, o_theirs
+):
+    for step, part in enumerate((oa, ob, oc, od)):
+        at = pl.multiple_of((quad[0] ^ step) * 128, 128)
+        o_theirs[pl.ds(at, 128)] = part[...]
     branch = dot(mine[...], o_mine[...]) + dot(theirs[...], o_theirs[...])
     hid = (x[...].astype(F32) + normed(branch)).astype(BF)
-    acc = None
-    for c in range(4):
-        span = slice(c * 512, c * 512 + 512)
-        grown = gelu(dot_nt(hid, expand[span, :])).astype(BF)
-        term = dot(grown, shrink[span, :])
-        acc = term if acc is None else acc + term
+    acc = dot(gelu(dot_nt(hid, expand[...])).astype(BF), shrink[...])
     first = me[0] == 0
 
     def split(values):
@@ -380,7 +364,7 @@
     scales_two,
 ):
     me = lax.axis_index("tp").astype(jnp.int32).reshape(1)
-    lat_at = (lax.axis_index("lat") & 3).astype(jnp.int32).reshape(1)
+    quad = (lax.axis_index("lat") & 3).astype(jnp.int32).reshape(1)
     ones = const(np.kron(np.eye(4), np.ones((64, 64))))
     lane_of = np.zeros((8, 128), np.float32)
     lane_of[0, :64] = 1
@@ -392,21 +376,17 @@
     col_axes = ("lon", "tp")
     tok = lambda n: ((n, 512), BF)
 
-    flat = patches.transpose(0, 2, 1, 3).reshape(1152, 512)
-    left, right = call(
-        pack_kernel,
-        [tok(576)] * 2,
-        [flat],
-        10**9,
-    )
+    home = patches.transpose(0, 2, 1, 3).reshape(4, 2, 144, 512)
+    left = call(pack_kernel, [tok(576)], [home[:, 0]], 10**8)[0]
+    right = call(pack_kernel, [tok(576)], [after(home, left)[:, 1]], 10**9)[0]
     region_ids = after(region_ids, right)
     left = behind(left, col_axes, -1)
     pick, keep = pick_rows()
-    classes, s_one, s_two, quarter = call(
+    classes, s_one, s_two, part = call(
         ready_kernel,
         [((1152, 128), BF), ((1, 512), F32), ((1, 512), F32), ((128, 1024), BF)],
         [
-            lat_at,
+            quad,
             region_ids.transpose(2, 0, 1),
             const(pick),
             const(keep),
@@ -420,8 +400,7 @@
         hbm=(7,),
         scratch=[pltpu.SemaphoreType.DMA],
     )
-    quarter = after(quarter, left)
-    oa = behind(quarter, "tp", 1)
+    oa = behind(after(part, left), "tp", 1)
     down, up = call(rim_kernel, [tok(216), tok(144)], [left, right, classes], 10**6)
     classes = after(classes, down)
     down, up = behind(down, "lat", 1), behind(up, "lat", -1)
@@ -432,18 +411,17 @@
     hl1 = behind(hl1, col_axes, 1)
     shared[0] = after(classes, hr1)
     hr2, hl2 = call(
-        second_kernel, [tok(288)] * 2, [right, left, down, up] + shared, 6 * 10**9
+        second_kernel, [tok(288)] * 2, [right, left, down, up] + shared, 15 * 10**8
     )
     hl2 = behind(hl2, col_axes, 1)
 
     feeds = [expand_one, shrink_one]
     br1, br2 = call(feed_kernel, [tok(288)] * 2, [hr1, hr2] + feeds, 3 * 10**9)
-    oa = after(oa, br1)
+    bl1 = call(feed_some_kernel, [tok(288)], [after(hl1, (br1, oa))] + feeds, 2 * 10**9)[0]
+    oa = after(oa, bl1)
     ob, oc = across(oa, "lat", 1), across(oa, "lat", 2)
-    bl1 = call(feed_some_kernel, [tok(288)], [after(hl1, br1)] + feeds, 2 * 10**9)[0]
     bl2 = call(feed_some_kernel, [tok(288)], [after(hl2, bl1)] + feeds, 2 * 10**9)[0]
     blocks = [bl1, bl2, br1, br2]
-    od = across(after(oc, bl2), "lat", 1)
     pm, coarse_in = const(merge_rows()), []
     for g in range(2):
         if g:
@@ -457,19 +435,16 @@
         )
     c0, c1 = coarse_in
     d0, d1 = behind(c0, "tp", 1), behind(c1, "tp", 1)
-    blocks[0], od = after(blocks[0], c1), after(od, c1)
+    od = across(after(oc, (c1, ob)), "lat", 1)
+    blocks[0] = after(blocks[0], c1)
     skip = call(skip_kernel, [tok(1152)], blocks + [const(home_rows())], 2 * 10**9)[0]
-    o_theirs = call(
-        join_kernel, [((512, 1024), BF)], [lat_at, oa, ob, oc, od], 10**9, smem=(0,)
-    )[0]
-    c0, skip, o_theirs = lax.optimization_barrier((c0, skip, o_theirs))
+    c0, skip = lax.optimization_barrier((c0, skip))
     skip = skip.reshape(4, 12, 24, 512).transpose(0, 2, 1, 3)
-
     w_two = triple_two.transpose(1, 0, 2)
     attended = []
     for own, other in ((c0, d0), (c1, d1)):
         if attended:
-            own = after(own, attended[0][1])
+            own = after(own, (attended[0][1], od))
         x, mine = call(
             attend_two_kernel,
             [((288, 1024), BF), tok(288)],
@@ -485,9 +460,10 @@
         keep, send, hid_own = call(
             feed_two_kernel,
             [((144, 1024), F32), ((144, 1024), BF), ((144, 1024), BF)],
-            [me, x, mine, theirs, output_two, o_theirs, expand_two, shrink_two],
+            [me, quad, x, mine, theirs, output_two, oa, ob, oc, od, expand_two, shrink_two],
             10**8,
-            smem=(0,),
+            smem=(0, 1),
+            scratch=[pltpu.VMEM((512, 1024), BF)],
         )
         kept.append((keep, behind(send, "tp", 1), hid_own))
     pout = const(coarse_rows())

time: 100 us -> 107 us (1.070)
  local copies, waits for them, and re-layouts: 1.46 us -> 8.77 us
  waiting for transfers between devices: 37.4 us -> 31.3 us
  Pallas kernels: 36.1 us -> 39.1 us
  starting transfers between devices: 23.6 us -> 26.1 us
    ppermute x12, waiting for transfers between devices: 37.4 us -> 31.3 us  [behind(): lax.ppermute(value, axis, [(s, (s + steps) % count) for s in range(count)])]
    unnamed x42 -> x58, local copies, waits for them, and re-layouts: 1.46 us -> 7.52 us
    pallas_call x18, Pallas kernels: 36.1 us -> 39.1 us  [call(): pl.pallas_call(kernel, out_shape=[jax.ShapeDtypeStruct(shape, kind) for s...]
    ppermute x12, starting transfers between devices: 23.3 us -> 25.7 us  [behind(): lax.ppermute(value, axis, [(s, (s + steps) % count) for s in range(count)])]
    squeeze x0 -> x2, local copies, waits for them, and re-layouts: none -> 1.25 us  [the longest x1 1.2 us: shards(): left = call(pack_kernel, [tok(576)], [home[:, 0]], 10 ** 8)[0]]
  transfers between devices with their start and end apart: 15 -> 15, of which waited for: 10 -> 8; matrix products, arithmetic and copies ran while one was open for 0% -> 0% of each run, Pallas kernels for 34% -> 35%
where the time goes in v1:
time: 107 us; the launch traced here: 106 us
  Pallas kernels  39.1 us (37%)
  waiting for transfers between devices  31.3 us (29%)
  starting transfers between devices  26.1 us (24%)
  local copies, waits for them, and re-layouts  8.77 us (8%)
    pallas_call x18, Pallas kernels, call(): pl.pallas_call(kernel, out_shape=[jax.ShapeDtypeStruct(shape, kind) for s...  39.1 us
    ppermute x12, waiting for transfers between devices, behind(): lax.ppermute(value, axis, [(s, (s + steps) % count) for s in range(count)])  31.3 us
    ppermute x12, starting transfers between devices, behind(): lax.ppermute(value, axis, [(s, (s + steps) % count) for s in range(count)])  25.7 us
    unnamed x58, local copies, waits for them, and re-layouts  7.52 us
  transfers between devices with their start and end apart: 15, of which 8 were waited for; matrix products, arithmetic and copies ran while one was open for 0% of the time, Pallas kernels for 35%

profile of v1, /device:TPU:0, one launch (start us, length us, event | category | flops | bytes accessed | tf_op | source)
XLA Modules:
  0.0 106.3 jit_solution(9462710743910104655)
XLA Ops:
  0.6 1.2 %slice_bitcast_fusion.1.x = bf16[4,144,512]{2,1,0:T(8,128)(2,1)S(1)} fusion(bf16[4,2,144,512]{3,2,1,0:T(8,128)(2,1)} %bitcast.27), kind=kLoop, calls=%fused_computation.1 | loop fusion | bytes 1179648 | tf_op jit(solution)/shard_map/squeeze | solution.py:380
  1.8 0.3 shard_map.212
  2.1 6.6 %collective-permute-start = (bf16[576,512]{1,0:T(8,128)(2,1)S(1)}, bf16[576,512]{1,0:T(8,128)(2,1)S(1)}, u32[]{:S(2)}, u32[]{:S(2)}) collective-permute-start(bf16[576,512]{1,0:T(8,128)(2,1)S(1)} %shard_map.212), channel_id=1, source_target_pairs={{0,15},{1,0},{2,1},{3,2},{4,3},{5,4},{6,5},{7,6},{8,7},{9,8},{10,9... | collective-permute-start | bytes 1769480 | tf_op jit(solution)/shard_map/ppermute | solution.py:340
  8.9 0.0 copy-start.22
  8.9 0.3 shard_map.213.right_all.right
  9.2 0.8 copy-done.5
  10.1 0.1 copy-done.22
  10.2 1.0 copy-done.23
  11.1 0.4 shard_map.214
  11.6 9.8 %collective-permute-done.left_all.left = bf16[576,512]{1,0:T(8,128)(2,1)S(1)} collective-permute-done((bf16[576,512]{1,0:T(8,128)(2,1)S(1)}, bf16[576,512]{1,0:T(8,128)(2,1)S(1)}, u32[]{:S(2)}, u32[]{:S(2)}) %collective-permute-start) | collective-permute-done | bytes 589856 | tf_op jit(solution)/shard_map/ppermute | solution.py:340
  21.4 0.0 collective-permute-start.2
  21.4 2.9 %collective-permute-start.3 = (bf16[144,512]{1,0:T(8,128)(2,1)S(1)}, bf16[144,512]{1,0:T(8,128)(2,1)S(1)}, u32[]{:S(2)}, u32[]{:S(2)}) collective-permute-start(bf16[144,512]{1,0:T(8,128)(2,1)S(1)} %get-tuple-element.47), channel_id=1, source_target_pairs={{0,112},{16,0},{32,16},{48,32},{64,48},{80,64},{96,80},{112,96},{1... | collective-permute-start | bytes 442376 | tf_op jit(solution)/shard_map/ppermute | solution.py:340
  24.4 3.3 %shard_map.216 = (bf16[288,512]{1,0:T(8,128)(2,1)S(1)}, bf16[288,512]{1,0:T(8,128)(2,1)S(1)}) custom-call(bf16[576,512]{1,0:T(8,128)(2,1)S(1)} %shard_map.213.right_all.right, bf16[576,512]{1,0:T(8,128)(2,1)S(1)} %collective-permute-done.left_all.left, bf16[1152,128]{1,0:T(8,128)(2,1)S(1)} %get-tuple-element.48.classes, bf16[3,512,512]{2,1,0:T(8,128)(2,1)S(1)} %bitcast.22, ...), custom_call_target="tpu_custom_call" | custom-call | flops 4000000000 | bytes 3706880 | tf_op jit(solution)/shard_map/pallas_call | solution.py:149
  27.7 1.7 %collective-permute-start.1 = (bf16[288,512]{1,0:T(8,128)(2,1)S(1)}, bf16[288,512]{1,0:T(8,128)(2,1)S(1)}, u32[]{:S(2)}, u32[]{:S(2)}) collective-permute-start(bf16[288,512]{1,0:T(8,128)(2,1)S(1)} %get-tuple-element.45), channel_id=1, source_target_pairs={{0,1},{1,2},{2,3},{3,4},{4,5},{5,6},{6,7},{7,8},{8,9},{9,10},{10,1... | collective-permute-start | bytes 884744 | tf_op jit(solution)/shard_map/ppermute | solution.py:340
  29.4 0.8 collective-permute-start.4
  30.2 4.4 %shard_map.217 = (bf16[288,512]{1,0:T(8,128)(2,1)S(1)}, bf16[288,512]{1,0:T(8,128)(2,1)S(1)}) custom-call(bf16[576,512]{1,0:T(8,128)(2,1)S(1)} %shard_map.213.right_all.right, bf16[576,512]{1,0:T(8,128)(2,1)S(1)} %collective-permute-done.left_all.left, bf16[216,512]{1,0:T(8,128)(2,1)S(1)} %collective-permute-done.2.down, ...), custom_call_target="tpu_custom_call" | custom-call | flops 1500000000 | bytes 4075520 | tf_op jit(solution)/shard_map/pallas_call | solution.py:149
  34.6 3.0 %collective-permute-start.5 = (bf16[288,512]{1,0:T(8,128)(2,1)S(1)}, bf16[288,512]{1,0:T(8,128)(2,1)S(1)}, u32[]{:S(2)}, u32[]{:S(2)}) collective-permute-start(bf16[288,512]{1,0:T(8,128)(2,1)S(1)} %get-tuple-element.54), channel_id=1, source_target_pairs={{0,1},{1,2},{2,3},{3,4},{4,5},{5,6},{6,7},{7,8},{8,9},{9,10},{10,1... | collective-permute-start | bytes 884744 | tf_op jit(solution)/shard_map/ppermute | solution.py:340
  37.6 3.1 %shard_map.218 = (bf16[288,512]{1,0:T(8,128)(2,1)S(1)}, bf16[288,512]{1,0:T(8,128)(2,1)S(1)}) custom-call(bf16[288,512]{1,0:T(8,128)(2,1)S(1)} %get-tuple-element.46.h1, bf16[288,512]{1,0:T(8,128)(2,1)S(1)} %get-tuple-element.49.h2, bf16[512,2048]{1,0:T(8,128)(2,1)S(1)} %copy-done.14, bf16[2048,512]{1,0:T(8,128)(2,1)S(1)} %copy-done.15), custom_call_target="tpu_custom_call" | custom-call | flops 3000000000 | bytes 4784128 | tf_op jit(solution)/shard_map/pallas_call | solution.py:149
  40.7 3.1 %collective-permute-done.4.oa = bf16[128,1024]{1,0:T(8,128)(2,1)} collective-permute-done((bf16[128,1024]{1,0:T(8,128)(2,1)S(1)}, bf16[128,1024]{1,0:T(8,128)(2,1)}, u32[]{:S(2)}, u32[]{:S(2)}) %collective-permute-start.4) | collective-permute-done | bytes 262176 | tf_op jit(solution)/shard_map/ppermute | solution.py:340
  43.8 3.3 %collective-permute-done.1.h = bf16[288,512]{1,0:T(8,128)(2,1)S(1)} collective-permute-done((bf16[288,512]{1,0:T(8,128)(2,1)S(1)}, bf16[288,512]{1,0:T(8,128)(2,1)S(1)}, u32[]{:S(2)}, u32[]{:S(2)}) %collective-permute-start.1) | collective-permute-done | bytes 294944 | tf_op jit(solution)/shard_map/ppermute | solution.py:340
  47.1 1.7 %shard_map.219.l1 = bf16[288,512]{1,0:T(8,128)(2,1)S(1)} custom-call(bf16[288,512]{1,0:T(8,128)(2,1)S(1)} %collective-permute-done.1.h, bf16[512,2048]{1,0:T(8,128)(2,1)S(1)} %copy-done.14, bf16[2048,512]{1,0:T(8,128)(2,1)S(1)} %copy-done.15), custom_call_target="tpu_custom_call" | custom-call | flops 2000000000 | bytes 4489216 | tf_op jit(solution)/shard_map/pallas_call | solution.py:149
  48.9 0.1 collective-permute-start.8
  49.0 0.3 collective-permute-start.9
  49.3 2.1 %collective-permute-done.5.h = bf16[288,512]{1,0:T(8,128)(2,1)S(1)} collective-permute-done((bf16[288,512]{1,0:T(8,128)(2,1)S(1)}, bf16[288,512]{1,0:T(8,128)(2,1)S(1)}, u32[]{:S(2)}, u32[]{:S(2)}) %collective-permute-start.5) | collective-permute-done | bytes 294944 | tf_op jit(solution)/shard_map/ppermute | solution.py:340
  51.4 1.7 %shard_map.220.l2 = bf16[288,512]{1,0:T(8,128)(2,1)S(1)} custom-call(bf16[288,512]{1,0:T(8,128)(2,1)S(1)} %collective-permute-done.5.h, bf16[512,2048]{1,0:T(8,128)(2,1)S(1)} %copy-done.14, bf16[2048,512]{1,0:T(8,128)(2,1)S(1)} %copy-done.15), custom_call_target="tpu_custom_call" | custom-call | flops 2000000000 | bytes 4489216 | tf_op jit(solution)/shard_map/pallas_call | solution.py:149
  53.1 0.4 copy-done.2
  53.6 2.5 %shard_map.221.own = bf16[144,1024]{1,0:T(8,128)(2,1)} custom-call(bf16[288,512]{1,0:T(8,128)(2,1)S(1)} %shard_map.219.l1, bf16[288,512]{1,0:T(8,128)(2,1)S(1)} %shard_map.220.l2, bf16[288,512]{1,0:T(8,128)(2,1)S(1)} %get-tuple-element.50.r1, bf16[288,512]{1,0:T(8,128)(2,1)S(1)} %get-tuple-element.56.r2, bf16[2,576,864]{2,1,0:T(8,128)(2,1)S(1)} %copy-done.4, ...), custom_call_target="tpu_custom_call" | custom-call | flops 1000000000 | bytes 7364608 | tf_op jit(solution)/shard_map/pallas_call | solution.py:149
  56.1 2.2 %copy-done.3 = bf16[2048,1024]{1,0:T(8,128)(2,1)S(1)} copy-done((bf16[2048,1024]{1,0:T(8,128)(2,1)S(1)}, bf16[2048,1024]{1,0:T(8,128)(2,1)}, u32[]{:S(2)}) %copy-start.3) | copy-done | bytes 4194328
  58.3 1.0 copy-done.7
  59.2 1.0 copy-done.9
  60.2 1.0 copy-done.11
  61.2 1.8 %shard_map.222.own = bf16[144,1024]{1,0:T(8,128)(2,1)S(1)} custom-call(bf16[288,512]{1,0:T(8,128)(2,1)S(1)} %copy-done.9, bf16[288,512]{1,0:T(8,128)(2,1)S(1)} %copy-done.11, bf16[288,512]{1,0:T(8,128)(2,1)S(1)} %get-tuple-element.50.r1, bf16[288,512]{1,0:T(8,128)(2,1)S(1)} %copy-done.7, bf16[2,576,864]{2,1,0:T(8,128)(2,1)S(1)} %copy-done.4, ...), custom_call_target="tpu_custom_call" | custom-call | flops 1000000000 | bytes 7364608 | tf_op jit(solution)/shard_map/pallas_call | solution.py:149
  63.0 3.6 %collective-permute-start.12 = (bf16[144,1024]{1,0:T(8,128)(2,1)S(1)}, bf16[144,1024]{1,0:T(8,128)(2,1)S(1)}, u32[]{:S(2)}, u32[]{:S(2)}) collective-permute-start(bf16[144,1024]{1,0:T(8,128)(2,1)S(1)} %shard_map.222.own), channel_id=1, source_target_pairs={{0,1},{1,0},{2,3},{3,2},{4,5},{5,4},{6,7},{7,6},{8,9},{9,8},{10,11... | collective-permute-start | bytes 884744 | tf_op jit(solution)/shard_map/ppermute | solution.py:340
  66.6 2.1 %shard_map.223 = bf16[1152,512]{1,0:T(8,128)(2,1)} custom-call(bf16[288,512]{1,0:T(8,128)(2,1)S(1)} %copy-done.9, bf16[288,512]{1,0:T(8,128)(2,1)S(1)} %copy-done.11, bf16[288,512]{1,0:T(8,128)(2,1)S(1)} %get-tuple-element.50.r1, bf16[288,512]{1,0:T(8,128)(2,1)S(1)} %copy-done.7, bf16[576,576]{1,0:T(8,128)(2,1)S(1)} %copy-done.21), custom_call_target="tpu_custom_call" | custom-call | flops 2000000000 | bytes 1843200 | tf_op jit(solution)/shard_map/pallas_call | solution.py:149
  68.7 3.4 %shard_map.224 = (bf16[288,1024]{1,0:T(8,128)(2,1)S(1)}, bf16[288,512]{1,0:T(8,128)(2,1)S(1)}) custom-call(s32[1]{0:T(128)} %bitcast.12.me, bf16[144,1024]{1,0:T(8,128)(2,1)} %shard_map.221.own, bf16[144,1024]{1,0:T(8,128)(2,1)} %collective-permute-done.6.other, bf16[3,512,1024]{2,1,0:T(8,128)(2,1)S(1)} %bitcast.20, bf16[256,256]{1,0:T(8,128)(2,1)S(1)} %copy-done.25, ...), custom_call_target="tpu_custom_call" | custom-call | flops 2000000000 | bytes 3870724 | tf_op jit(solution)/shard_map/pallas_call | solution.py:149
  72.1 0.4 collective-permute-start.7
  72.6 2.2 %shard_map.227 = (bf16[288,1024]{1,0:T(8,128)(2,1)S(1)}, bf16[288,512]{1,0:T(8,128)(2,1)S(1)}) custom-call(s32[1]{0:T(128)} %bitcast.12.me, bf16[144,1024]{1,0:T(8,128)(2,1)S(1)} %shard_map.222.own, bf16[144,1024]{1,0:T(8,128)(2,1)S(1)} %collective-permute-done.12.other, bf16[3,512,1024]{2,1,0:T(8,128)(2,1)S(1)} %bitcast.21, ...), custom_call_target="tpu_custom_call" | custom-call | flops 2000000000 | bytes 3870724 | tf_op jit(solution)/shard_map/pallas_call | solution.py:149
  74.8 3.5 %collective-permute-start.13 = (bf16[288,512]{1,0:T(8,128)(2,1)S(1)}, bf16[288,512]{1,0:T(8,128)(2,1)S(1)}, u32[]{:S(2)}, u32[]{:S(2)}) collective-permute-start(bf16[288,512]{1,0:T(8,128)(2,1)S(1)} %get-tuple-element.72.mine), channel_id=1, source_target_pairs={{0,1},{1,0},{2,3},{3,2},{4,5},{5,4},{6,7},{7,6},{8,9},{9,8},{10,11... | collective-permute-start | bytes 884744 | tf_op jit(solution)/shard_map/ppermute | solution.py:340
  78.3 5.5 %collective-permute-done.7.theirs = bf16[288,512]{1,0:T(8,128)(2,1)S(1)} collective-permute-done((bf16[288,512]{1,0:T(8,128)(2,1)S(1)}, bf16[288,512]{1,0:T(8,128)(2,1)S(1)}, u32[]{:S(2)}, u32[]{:S(2)}) %collective-permute-start.7) | collective-permute-done | bytes 294944 | tf_op jit(solution)/shard_map/ppermute | solution.py:340
  83.8 5.1 %shard_map.225 = (f32[144,1024]{1,0:T(8,128)S(1)}, bf16[144,1024]{1,0:T(8,128)(2,1)S(1)}, bf16[144,1024]{1,0:T(8,128)(2,1)S(1)}) custom-call(s32[1]{0:T(128)} %bitcast.12.me, s32[1]{0:T(128)} %bitcast.5.at.quad, bf16[288,1024]{1,0:T(8,128)(2,1)S(1)} %get-tuple-element.62.x, bf16[288,512]{1,0:T(8,128)(2,1)S(1)} %get-tuple-element.63.mine, ...), custom_call_target="tpu_custom_call" | custom-call | flops 100000000 | bytes 11665416 | tf_op jit(solution)/shard_map/pallas_call | solution.py:149
  88.8 0.3 collective-permute-start.11
  89.1 0.6 collective-permute-done.13.theirs
  89.7 5.1 %shard_map.228 = (f32[144,1024]{1,0:T(8,128)S(1)}, bf16[144,1024]{1,0:T(8,128)(2,1)S(1)}, bf16[144,1024]{1,0:T(8,128)(2,1)S(1)}) custom-call(s32[1]{0:T(128)} %bitcast.12.me, s32[1]{0:T(128)} %bitcast.5.at.quad, bf16[288,1024]{1,0:T(8,128)(2,1)S(1)} %get-tuple-element.71.x, bf16[288,512]{1,0:T(8,128)(2,1)S(1)} %get-tuple-element.72.mine, ...), custom_call_target="tpu_custom_call" | custom-call | flops 100000000 | bytes 11665416 | tf_op jit(solution)/shard_map/pallas_call | solution.py:149
  94.8 2.9 %collective-permute-start.14 = (bf16[144,1024]{1,0:T(8,128)(2,1)S(1)}, bf16[144,1024]{1,0:T(8,128)(2,1)S(1)}, u32[]{:S(2)}, u32[]{:S(2)}) collective-permute-start(bf16[144,1024]{1,0:T(8,128)(2,1)S(1)} %get-tuple-element.74), channel_id=1, source_target_pairs={{0,1},{1,0},{2,3},{3,2},{4,5},{5,4},{6,7},{7,6},{8,9},{9,8},{10,11... | collective-permute-start | bytes 884744 | tf_op jit(solution)/shard_map/ppermute | solution.py:340
  97.6 1.0 collective-permute-done.11.r
  98.7 0.5 shard_map.226.first
  99.1 5.8 %collective-permute-done.14.r = bf16[144,1024]{1,0:T(8,128)(2,1)S(1)} collective-permute-done((bf16[144,1024]{1,0:T(8,128)(2,1)S(1)}, bf16[144,1024]{1,0:T(8,128)(2,1)S(1)}, u32[]{:S(2)}, u32[]{:S(2)}) %collective-permute-start.14) | collective-permute-done | bytes 294944 | tf_op jit(solution)/shard_map/ppermute | solution.py:340
  105.0 1.3 %shard_map.229 = bf16[12,6,4,1024]{3,2,1,0:T(4,128)(2,1)} custom-call(bf16[6,6,4,1024]{3,2,1,0:T(4,128)(2,1)S(1)} %shard_map.226.first, f32[144,1024]{1,0:T(8,128)S(1)} %get-tuple-element.73.k, bf16[144,1024]{1,0:T(8,128)(2,1)S(1)} %collective-permute-done.14.r, bf16[144,1024]{1,0:T(8,128)(2,1)S(1)} %get-tuple-element.75.h, bf16[144,144]{1,0:T(8,128)(2,1)S(1)} %copy-done.12), custom_call_target="tpu_custom_call" | custom-call | flops 100000000 | bytes 1516032 | tf_op jit(solution)/shard_map/pallas_call | solution.py:149
  (60 shorter events, 0.2 us)
Async XLA Ops:
  0.6 8.2 %copy-start.28 = (bf16[4,24,12,512]{3,1,2,0:T(8,128)(2,1)S(1)}, bf16[4,24,12,512]{3,1,2,0:T(8,128)(2,1)}, u32[]{:S(2)}) copy-start(bf16[4,24,12,512]{3,1,2,0:T(8,128)(2,1)} %param.21) | copy-start | bytes 3538948
  2.1 19.2 %collective-permute-start = (bf16[576,512]{1,0:T(8,128)(2,1)S(1)}, bf16[576,512]{1,0:T(8,128)(2,1)S(1)}, u32[]{:S(2)}, u32[]{:S(2)}) collective-permute-start(bf16[576,512]{1,0:T(8,128)(2,1)S(1)} %shard_map.212), channel_id=1, source_target_pairs={{0,15},{1,0},{2,1},{3,2},{4,3},{5,4},{6,5},{7,6},{8,7},{9,8},{10,9... | collective-permute-start | bytes 1769480 | tf_op jit(solution)/shard_map/ppermute | solution.py:340
  8.8 1.2 %copy-start.5 = (bf16[512,1024]{1,0:T(8,128)(2,1)S(1)}, bf16[512,1024]{1,0:T(8,128)(2,1)}, u32[]{:S(2)}) copy-start(bf16[512,1024]{1,0:T(8,128)(2,1)} %o_mine.3) | copy-start | bytes 3145732
  8.9 1.2 %copy-start.18 = (s32[4,24,12]{1,0,2:T(4,128)S(1)}, s32[4,24,12]{1,0,2:T(4,128)}, u32[]{:S(2)}) copy-start(s32[4,24,12]{1,0,2:T(4,128)} %param.22) | copy-start | bytes 13828
  8.9 1.2 %copy-start.19 = (bf16[8]{0:T(256)(128)(2,1)S(1)}, bf16[8]{0:T(256)(128)(2,1)}, u32[]{:S(2)}) copy-start(bf16[8]{0:T(256)(128)(2,1)} %param.27) | copy-start | bytes 52
  8.9 1.2 %copy-start.20 = (bf16[8]{0:T(256)(128)(2,1)S(1)}, bf16[8]{0:T(256)(128)(2,1)}, u32[]{:S(2)}) copy-start(bf16[8]{0:T(256)(128)(2,1)} %param.33) | copy-start | bytes 52
  8.9 1.3 %copy-start.22 = (bf16[1152,48]{1,0:T(8,128)(2,1)S(1)}, bf16[1152,48]{1,0:T(8,128)(2,1)}, u32[]{:S(2)}) copy-start(bf16[1152,48]{1,0:T(8,128)(2,1)} %constant.31.clone.rows) | copy-start | bytes 331780
  8.9 1.3 %copy-start.26 = (bf16[8,512]{1,0:T(8,128)(2,1)S(1)}, bf16[8,512]{1,0:T(8,128)(2,1)}, u32[]{:S(2)}) copy-start(bf16[8,512]{1,0:T(8,128)(2,1)} %constant.30.clone.spread) | copy-start | bytes 24580
  10.2 1.0 copy-start.23
  11.1 13.2 %copy-start.16 = (bf16[512,3,512]{2,0,1:T(8,128)(2,1)S(1)}, bf16[512,3,512]{2,0,1:T(8,128)(2,1)}, u32[]{:S(2)}) copy-start(bf16[512,3,512]{2,0,1:T(8,128)(2,1)} %param.23) | copy-start | bytes 4718596
  11.1 13.2 %copy-start.17 = (bf16[512,512]{1,0:T(8,128)(2,1)S(1)}, bf16[512,512]{1,0:T(8,128)(2,1)}, u32[]{:S(2)}) copy-start(bf16[512,512]{1,0:T(8,128)(2,1)} %out.3) | copy-start | bytes 1572868
  11.1 13.2 %copy-start.24 = (bf16[256,256]{1,0:T(8,128)(2,1)S(1)}, bf16[256,256]{1,0:T(8,128)(2,1)}, u32[]{:S(2)}) copy-start(bf16[256,256]{1,0:T(8,128)(2,1)} %constant.28.clone.ones) | copy-start | bytes 393220
  11.1 13.2 %copy-start.27 = (bf16[8,128]{1,0:T(8,128)(2,1)S(1)}, bf16[8,128]{1,0:T(8,128)(2,1)}, u32[]{:S(2)}) copy-start(bf16[8,128]{1,0:T(8,128)(2,1)} %constant.29.clone.lanes) | copy-start | bytes 6148
  21.4 8.8 %collective-permute-start.2 = (bf16[216,512]{1,0:T(8,128)(2,1)S(1)}, bf16[216,512]{1,0:T(8,128)(2,1)S(1)}, u32[]{:S(2)}, u32[]{:S(2)}) collective-permute-start(bf16[216,512]{1,0:T(8,128)(2,1)S(1)} %get-tuple-element.42), channel_id=1, source_target_pairs={{0,16},{16,32},{32,48},{48,64},{64,80},{80,96},{96,112},{112,0},{1... | collective-permute-start | bytes 663560 | tf_op jit(solution)/shard_map/ppermute | solution.py:340
  21.4 8.8 %collective-permute-start.3 = (bf16[144,512]{1,0:T(8,128)(2,1)S(1)}, bf16[144,512]{1,0:T(8,128)(2,1)S(1)}, u32[]{:S(2)}, u32[]{:S(2)}) collective-permute-start(bf16[144,512]{1,0:T(8,128)(2,1)S(1)} %get-tuple-element.47), channel_id=1, source_target_pairs={{0,112},{16,0},{32,16},{48,32},{64,48},{80,64},{96,80},{112,96},{1... | collective-permute-start | bytes 442376 | tf_op jit(solution)/shard_map/ppermute | solution.py:340
  27.7 19.4 %collective-permute-start.1 = (bf16[288,512]{1,0:T(8,128)(2,1)S(1)}, bf16[288,512]{1,0:T(8,128)(2,1)S(1)}, u32[]{:S(2)}, u32[]{:S(2)}) collective-permute-start(bf16[288,512]{1,0:T(8,128)(2,1)S(1)} %get-tuple-element.45), channel_id=1, source_target_pairs={{0,1},{1,2},{2,3},{3,4},{4,5},{5,6},{6,7},{7,8},{8,9},{9,10},{10,1... | collective-permute-start | bytes 884744 | tf_op jit(solution)/shard_map/ppermute | solution.py:340
  29.4 8.2 %copy-start.14 = (bf16[512,2048]{1,0:T(8,128)(2,1)S(1)}, bf16[512,2048]{1,0:T(8,128)(2,1)}, u32[]{:S(2)}) copy-start(bf16[512,2048]{1,0:T(8,128)(2,1)} %expand.7) | copy-start | bytes 6291460
  29.4 8.2 %copy-start.15 = (bf16[2048,512]{1,0:T(8,128)(2,1)S(1)}, bf16[2048,512]{1,0:T(8,128)(2,1)}, u32[]{:S(2)}) copy-start(bf16[2048,512]{1,0:T(8,128)(2,1)} %shrink.7) | copy-start | bytes 6291460
  29.4 14.4 %collective-permute-start.4 = (bf16[128,1024]{1,0:T(8,128)(2,1)S(1)}, bf16[128,1024]{1,0:T(8,128)(2,1)}, u32[]{:S(2)}, u32[]{:S(2)}) collective-permute-start(bf16[128,1024]{1,0:T(8,128)(2,1)S(1)} %get-tuple-element.52), channel_id=1, source_target_pairs={{0,1},{1,0},{2,3},{3,2},{4,5},{5,4},{6,7},{7,6},{8,9},{9,8},{10,11... | collective-permute-start | bytes 786440 | tf_op jit(solution)/shard_map/ppermute | solution.py:340
  34.6 16.8 %collective-permute-start.5 = (bf16[288,512]{1,0:T(8,128)(2,1)S(1)}, bf16[288,512]{1,0:T(8,128)(2,1)S(1)}, u32[]{:S(2)}, u32[]{:S(2)}) collective-permute-start(bf16[288,512]{1,0:T(8,128)(2,1)S(1)} %get-tuple-element.54), channel_id=1, source_target_pairs={{0,1},{1,2},{2,3},{3,4},{4,5},{5,6},{6,7},{7,8},{8,9},{9,10},{10,1... | collective-permute-start | bytes 884744 | tf_op jit(solution)/shard_map/ppermute | solution.py:340
  40.7 12.4 %copy-start.6 = (bf16[288,512]{1,0:T(8,128)(2,1)}, bf16[288,512]{1,0:T(8,128)(2,1)S(1)}, u32[]{:S(2)}) copy-start(bf16[288,512]{1,0:T(8,128)(2,1)S(1)} %get-tuple-element.56.r2) | copy-start | bytes 884740
  48.9 4.3 %copy-start.8 = (bf16[288,512]{1,0:T(8,128)(2,1)}, bf16[288,512]{1,0:T(8,128)(2,1)S(1)}, u32[]{:S(2)}) copy-start(bf16[288,512]{1,0:T(8,128)(2,1)S(1)} %shard_map.219.l1) | copy-start | bytes 884740
  48.9 4.3 %copy-start.4 = (bf16[2,576,864]{2,1,0:T(8,128)(2,1)S(1)}, bf16[2,576,864]{2,1,0:T(8,128)(2,1)}, u32[]{:S(2)}) copy-start(bf16[2,576,864]{2,1,0:T(8,128)(2,1)} %constant.33.clone.pm) | copy-start | bytes 5971972
  48.9 17.7 %collective-permute-start.8 = (bf16[128,1024]{1,0:T(8,128)(2,1)}, bf16[128,1024]{1,0:T(8,128)(2,1)}, u32[]{:S(2)}, u32[]{:S(2)}) collective-permute-start(bf16[128,1024]{1,0:T(8,128)(2,1)} %collective-permute-done.4.oa), channel_id=1, source_target_pairs={{0,16},{16,0},{32,48},{48,32},{64,80},{80,64},{96,112},{112,96},{1... | collective-permute-start | bytes 786440 | tf_op jit(solution)/shard_map/ppermute | solution.py:348
  49.0 17.6 %collective-permute-start.9 = (bf16[128,1024]{1,0:T(8,128)(2,1)}, bf16[128,1024]{1,0:T(8,128)(2,1)}, u32[]{:S(2)}, u32[]{:S(2)}) collective-permute-start(bf16[128,1024]{1,0:T(8,128)(2,1)} %collective-permute-done.4.oa), channel_id=1, source_target_pairs={{0,32},{16,48},{32,0},{48,16},{64,96},{80,112},{96,64},{112,80},{1... | collective-permute-start | bytes 786440 | tf_op jit(solution)/shard_map/ppermute | solution.py:348
  51.4 2.2 %copy-start.2 = (bf16[2048,1024]{1,0:T(8,128)(2,1)S(1)}, bf16[2048,1024]{1,0:T(8,128)(2,1)}, u32[]{:S(2)}) copy-start(bf16[2048,1024]{1,0:T(8,128)(2,1)} %weight.3) | copy-start | bytes 12582916
  53.1 3.0 %copy-start.10 = (bf16[288,512]{1,0:T(8,128)(2,1)}, bf16[288,512]{1,0:T(8,128)(2,1)S(1)}, u32[]{:S(2)}) copy-start(bf16[288,512]{1,0:T(8,128)(2,1)S(1)} %shard_map.220.l2) | copy-start | bytes 884740
  56.1 12.6 %collective-permute-start.6 = (bf16[144,1024]{1,0:T(8,128)(2,1)}, bf16[144,1024]{1,0:T(8,128)(2,1)}, u32[]{:S(2)}, u32[]{:S(2)}) collective-permute-start(bf16[144,1024]{1,0:T(8,128)(2,1)} %shard_map.221.own), channel_id=1, source_target_pairs={{0,1},{1,0},{2,3},{3,2},{4,5},{5,4},{6,7},{7,6},{8,9},{9,8},{10,11... | collective-permute-start | bytes 884744 | tf_op jit(solution)/shard_map/ppermute | solution.py:340
  56.1 2.2 %copy-start.3 = (bf16[2048,1024]{1,0:T(8,128)(2,1)S(1)}, bf16[2048,1024]{1,0:T(8,128)(2,1)}, u32[]{:S(2)}) copy-start(bf16[2048,1024]{1,0:T(8,128)(2,1)} %weight.3) | copy-start | bytes 12582916
  58.3 1.0 copy-start.7
  59.2 1.0 copy-start.9
  60.2 1.0 copy-start.11
  61.2 5.4 %copy-start.21 = (bf16[576,576]{1,0:T(8,128)(2,1)S(1)}, bf16[576,576]{1,0:T(8,128)(2,1)}, u32[]{:S(2)}) copy-start(bf16[576,576]{1,0:T(8,128)(2,1)} %constant.34.clone.perm) | copy-start | bytes 1990660
  62.9 5.8 %copy-start.13 = (bf16[512,3,1024]{2,0,1:T(8,128)(2,1)S(1)}, bf16[512,3,1024]{2,0,1:T(8,128)(2,1)}, u32[]{:S(2)}) copy-start(bf16[512,3,1024]{2,0,1:T(8,128)(2,1)} %param.29) | copy-start | bytes 9437188
  63.0 5.7 %copy-start.25 = (bf16[256,256]{1,0:T(8,128)(2,1)S(1)}, bf16[256,256]{1,0:T(8,128)(2,1)}, u32[]{:S(2)}) copy-start(bf16[256,256]{1,0:T(8,128)(2,1)} %constant.28.clone.ones) | copy-start | bytes 393220
  63.0 9.6 %collective-permute-start.12 = (bf16[144,1024]{1,0:T(8,128)(2,1)S(1)}, bf16[144,1024]{1,0:T(8,128)(2,1)S(1)}, u32[]{:S(2)}, u32[]{:S(2)}) collective-permute-start(bf16[144,1024]{1,0:T(8,128)(2,1)S(1)} %shard_map.222.own), channel_id=1, source_target_pairs={{0,1},{1,0},{2,3},{3,2},{4,5},{5,4},{6,7},{7,6},{8,9},{9,8},{10,11... | collective-permute-start | bytes 884744 | tf_op jit(solution)/shard_map/ppermute | solution.py:340
  66.6 6.0 %collective-permute-start.10 = (bf16[128,1024]{1,0:T(8,128)(2,1)}, bf16[128,1024]{1,0:T(8,128)(2,1)S(1)}, u32[]{:S(2)}, u32[]{:S(2)}) collective-permute-start(bf16[128,1024]{1,0:T(8,128)(2,1)} %collective-permute-done.9.oc), channel_id=1, source_target_pairs={{0,16},{16,0},{32,48},{48,32},{64,80},{80,64},{96,112},{112,96},{1... | collective-permute-start | bytes 786440 | tf_op jit(solution)/shard_map/ppermute | solution.py:348
  68.7 15.0 %copy-start.1 = (bf16[2048,1024]{1,0:T(8,128)(2,1)S(1)}, bf16[2048,1024]{1,0:T(8,128)(2,1)}, u32[]{:S(2)}) copy-start(bf16[2048,1024]{1,0:T(8,128)(2,1)} %shrink.9) | copy-start | bytes 12582916
  72.1 11.6 %collective-permute-start.7 = (bf16[288,512]{1,0:T(8,128)(2,1)S(1)}, bf16[288,512]{1,0:T(8,128)(2,1)S(1)}, u32[]{:S(2)}, u32[]{:S(2)}) collective-permute-start(bf16[288,512]{1,0:T(8,128)(2,1)S(1)} %get-tuple-element.63.mine), channel_id=1, source_target_pairs={{0,1},{1,0},{2,3},{3,2},{4,5},{5,4},{6,7},{7,6},{8,9},{9,8},{10,11... | collective-permute-start | bytes 884744 | tf_op jit(solution)/shard_map/ppermute | solution.py:340
  72.6 11.2 %copy-start = (bf16[2048,1024]{1,0:T(8,128)(2,1)S(1)}, bf16[2048,1024]{1,0:T(8,128)(2,1)}, u32[]{:S(2)}) copy-start(bf16[2048,1024]{1,0:T(8,128)(2,1)} %expand.9) | copy-start | bytes 12582916
  74.8 14.9 %collective-permute-start.13 = (bf16[288,512]{1,0:T(8,128)(2,1)S(1)}, bf16[288,512]{1,0:T(8,128)(2,1)S(1)}, u32[]{:S(2)}, u32[]{:S(2)}) collective-permute-start(bf16[288,512]{1,0:T(8,128)(2,1)S(1)} %get-tuple-element.72.mine), channel_id=1, source_target_pairs={{0,1},{1,0},{2,3},{3,2},{4,5},{5,4},{6,7},{7,6},{8,9},{9,8},{10,11... | collective-permute-start | bytes 884744 | tf_op jit(solution)/shard_map/ppermute | solution.py:340
  88.8 9.8 %collective-permute-start.11 = (bf16[144,1024]{1,0:T(8,128)(2,1)S(1)}, bf16[144,1024]{1,0:T(8,128)(2,1)S(1)}, u32[]{:S(2)}, u32[]{:S(2)}) collective-permute-start(bf16[144,1024]{1,0:T(8,128)(2,1)S(1)} %get-tuple-element.67), channel_id=1, source_target_pairs={{0,1},{1,0},{2,3},{3,2},{4,5},{5,4},{6,7},{7,6},{8,9},{9,8},{10,11... | collective-permute-start | bytes 884744 | tf_op jit(solution)/shard_map/ppermute | solution.py:340
  89.1 9.5 %copy-start.12 = (bf16[144,144]{1,0:T(8,128)(2,1)S(1)}, bf16[144,144]{1,0:T(8,128)(2,1)}, u32[]{:S(2)}) copy-start(bf16[144,144]{1,0:T(8,128)(2,1)} %constant.35.clone.pout) | copy-start | bytes 124420
  94.8 10.2 %collective-permute-start.14 = (bf16[144,1024]{1,0:T(8,128)(2,1)S(1)}, bf16[144,1024]{1,0:T(8,128)(2,1)S(1)}, u32[]{:S(2)}, u32[]{:S(2)}) collective-permute-start(bf16[144,1024]{1,0:T(8,128)(2,1)S(1)} %get-tuple-element.74), channel_id=1, source_target_pairs={{0,1},{1,0},{2,3},{3,2},{4,5},{5,4},{6,7},{7,6},{8,9},{9,8},{10,11... | collective-permute-start | bytes 884744 | tf_op jit(solution)/shard_map/ppermute | solution.py:340

commit v2 on v0

--- a/solution.py
+++ b/solution.py
@@ -264,19 +264,13 @@
 
 
 def feed_one(h, expand, shrink):
-    acc = None
-    for c in range(4):
-        span = slice(c * 512, c * 512 + 512)
-        grown = gelu(dot(h, expand[:, span])).astype(BF)
-        term = dot(grown, shrink[span, :])
-        acc = term if acc is None else acc + term
-    return (h.astype(F32) + normed(acc)).astype(BF)
+    grown = gelu(dot(h, expand[...])).astype(BF)
+    return (h.astype(F32) + normed(dot(grown, shrink[...]))).astype(BF)
 
 
 def feed_kernel(h1, h2, expand, shrink, out1, out2):
-    got = feed_one(jnp.concatenate([h1[...], h2[...]], axis=0), expand, shrink)
-    out1[...] = got[:288]
-    out2[...] = got[288:]
+    out1[...] = feed_one(h1[...], expand, shrink)
+    out2[...] = feed_one(h2[...], expand, shrink)
 
 
 def feed_some_kernel(h, expand, shrink, out):
@@ -318,12 +312,7 @@
 def feed_two_kernel(me, x, mine, theirs, o_mine, o_theirs, expand, shrink, keep, send, hid_own):
     branch = dot(mine[...], o_mine[...]) + dot(theirs[...], o_theirs[...])
     hid = (x[...].astype(F32) + normed(branch)).astype(BF)
-    acc = None
-    for c in range(4):
-        span = slice(c * 512, c * 512 + 512)
-        grown = gelu(dot_nt(hid, expand[span, :])).astype(BF)
-        term = dot(grown, shrink[span, :])
-        acc = term if acc is None else acc + term
+    acc = dot(gelu(dot_nt(hid, expand[...])).astype(BF), shrink[...])
     first = me[0] == 0
 
     def split(values):
@@ -438,9 +427,9 @@
 
     feeds = [expand_one, shrink_one]
     br1, br2 = call(feed_kernel, [tok(288)] * 2, [hr1, hr2] + feeds, 3 * 10**9)
-    oa = after(oa, br1)
+    bl1 = call(feed_some_kernel, [tok(288)], [after(hl1, br1)] + feeds, 2 * 10**9)[0]
+    oa = after(oa, bl1)
     ob, oc = across(oa, "lat", 1), across(oa, "lat", 2)
-    bl1 = call(feed_some_kernel, [tok(288)], [after(hl1, br1)] + feeds, 2 * 10**9)[0]
     bl2 = call(feed_some_kernel, [tok(288)], [after(hl2, bl1)] + feeds, 2 * 10**9)[0]
     blocks = [bl1, bl2, br1, br2]
     od = across(after(oc, bl2), "lat", 1)

time: 100 us -> 99.6 us (level)
  Pallas kernels: 36.1 us -> 34.8 us
  starting transfers between devices: 23.6 us -> 24.8 us
    ppermute x12, waiting for transfers between devices: 37.4 us -> 33.8 us  [behind(): lax.ppermute(value, axis, [(s, (s + steps) % count) for s in range(count)])]
    ppermute x3, waiting for transfers between devices: 0.01 us -> 2.7 us  [across(): lax.ppermute(value, axis, [(s, s ^ flip) for s in range(lax.axis_size(axi...]
    pallas_call x18, Pallas kernels: 36.1 us -> 34.8 us  [call(): pl.pallas_call(kernel, out_shape=[jax.ShapeDtypeStruct(shape, kind) for s...]
    ppermute x12, starting transfers between devices: 23.3 us -> 24.5 us  [behind(): lax.ppermute(value, axis, [(s, (s + steps) % count) for s in range(count)])]
  transfers between devices with their start and end apart: 15 -> 15, of which waited for: 10 -> 9; matrix products, arithmetic and copies ran while one was open for 0% -> 0% of each run, Pallas kernels for 34% -> 33%
where the time goes in v2:
time: 99.6 us; the launch traced here: 99.4 us
  waiting for transfers between devices  36.5 us (37%)
  Pallas kernels  34.8 us (35%)
  starting transfers between devices  24.8 us (25%)
  local copies, waits for them, and re-layouts  2.34 us (2%)
    pallas_call x18, Pallas kernels, call(): pl.pallas_call(kernel, out_shape=[jax.ShapeDtypeStruct(shape, kind) for s...  34.8 us
    ppermute x12, waiting for transfers between devices, behind(): lax.ppermute(value, axis, [(s, (s + steps) % count) for s in range(count)])  33.8 us
    ppermute x12, starting transfers between devices, behind(): lax.ppermute(value, axis, [(s, (s + steps) % count) for s in range(count)])  24.5 us
    ppermute x3, waiting for transfers between devices, across(): lax.ppermute(value, axis, [(s, s ^ flip) for s in range(lax.axis_size(axi...  2.7 us
    unnamed x42, local copies, waits for them, and re-layouts  2.34 us
  transfers between devices with their start and end apart: 15, of which 9 were waited for; matrix products, arithmetic and copies ran while one was open for 0% of the time, Pallas kernels for 33%

profile of v2, /device:TPU:0, one launch (start us, length us, event | category | flops | bytes accessed | tf_op | source)
XLA Modules:
  0.0 99.4 jit_solution(11599541645495575457)
XLA Ops:
  0.6 0.0 copy-start.19
  0.7 1.4 %copy-done.10 = bf16[4,24,12,512]{3,1,2,0:T(8,128)(2,1)S(1)} copy-done((bf16[4,24,12,512]{3,1,2,0:T(8,128)(2,1)S(1)}, bf16[4,24,12,512]{3,1,2,0:T(8,128)(2,1)}, u32[]{:S(2)}) %copy-start.10) | copy-done | bytes 1179672
  2.0 0.0 copy-start.17
  2.0 0.5 shard_map.212
  2.5 6.6 %collective-permute-start = (bf16[576,512]{1,0:T(8,128)(2,1)S(1)}, bf16[576,512]{1,0:T(8,128)(2,1)S(1)}, u32[]{:S(2)}, u32[]{:S(2)}) collective-permute-start(bf16[576,512]{1,0:T(8,128)(2,1)S(1)} %get-tuple-element.43), channel_id=1, source_target_pairs={{0,15},{1,0},{2,1},{3,2},{4,3},{5,4},{6,5},{7,6},{8,7},{9,8},{10,9... | collective-permute-start | bytes 1769480 | tf_op jit(solution)/shard_map/ppermute | solution.py:345
  9.2 0.0 copy-start.18
  9.2 0.0 copy-start.20
  9.2 0.4 shard_map.213
  9.6 12.1 %collective-permute-done.left_all.left = bf16[576,512]{1,0:T(8,128)(2,1)S(1)} collective-permute-done((bf16[576,512]{1,0:T(8,128)(2,1)S(1)}, bf16[576,512]{1,0:T(8,128)(2,1)S(1)}, u32[]{:S(2)}, u32[]{:S(2)}) %collective-permute-start) | collective-permute-done | bytes 589856 | tf_op jit(solution)/shard_map/ppermute | solution.py:345
  21.8 0.0 collective-permute-start.2
  21.8 2.9 %collective-permute-start.3 = (bf16[144,512]{1,0:T(8,128)(2,1)S(1)}, bf16[144,512]{1,0:T(8,128)(2,1)S(1)}, u32[]{:S(2)}, u32[]{:S(2)}) collective-permute-start(bf16[144,512]{1,0:T(8,128)(2,1)S(1)} %get-tuple-element.51), channel_id=1, source_target_pairs={{0,112},{16,0},{32,16},{48,32},{64,48},{80,64},{96,80},{112,96},{1... | collective-permute-start | bytes 442376 | tf_op jit(solution)/shard_map/ppermute | solution.py:345
  24.7 3.4 %shard_map.215 = (bf16[288,512]{1,0:T(8,128)(2,1)S(1)}, bf16[288,512]{1,0:T(8,128)(2,1)S(1)}) custom-call(bf16[576,512]{1,0:T(8,128)(2,1)S(1)} %get-tuple-element.42.right_all.right, bf16[576,512]{1,0:T(8,128)(2,1)S(1)} %collective-permute-done.left_all.left, bf16[1152,128]{1,0:T(8,128)(2,1)S(1)} %get-tuple-element.52.classes, ...), custom_call_target="tpu_custom_call" | custom-call | flops 4000000000 | bytes 3706880 | tf_op jit(solution)/shard_map/pallas_call | solution.py:149
  28.1 1.7 %collective-permute-start.1 = (bf16[288,512]{1,0:T(8,128)(2,1)S(1)}, bf16[288,512]{1,0:T(8,128)(2,1)S(1)}, u32[]{:S(2)}, u32[]{:S(2)}) collective-permute-start(bf16[288,512]{1,0:T(8,128)(2,1)S(1)} %get-tuple-element.49), channel_id=1, source_target_pairs={{0,1},{1,2},{2,3},{3,4},{4,5},{5,6},{6,7},{7,8},{8,9},{9,10},{10,1... | collective-permute-start | bytes 884744 | tf_op jit(solution)/shard_map/ppermute | solution.py:345
  29.8 0.8 collective-permute-start.5
  30.6 4.4 %shard_map.216 = (bf16[288,512]{1,0:T(8,128)(2,1)S(1)}, bf16[288,512]{1,0:T(8,128)(2,1)S(1)}) custom-call(bf16[576,512]{1,0:T(8,128)(2,1)S(1)} %get-tuple-element.42.right_all.right, bf16[576,512]{1,0:T(8,128)(2,1)S(1)} %collective-permute-done.left_all.left, bf16[216,512]{1,0:T(8,128)(2,1)S(1)} %collective-permute-done.2.down, ...), custom_call_target="tpu_custom_call" | custom-call | flops 6000000000 | bytes 4075520 | tf_op jit(solution)/shard_map/pallas_call | solution.py:149
  34.9 3.0 %collective-permute-start.4 = (bf16[288,512]{1,0:T(8,128)(2,1)S(1)}, bf16[288,512]{1,0:T(8,128)(2,1)S(1)}, u32[]{:S(2)}, u32[]{:S(2)}) collective-permute-start(bf16[288,512]{1,0:T(8,128)(2,1)S(1)} %get-tuple-element.56), channel_id=1, source_target_pairs={{0,1},{1,2},{2,3},{3,4},{4,5},{5,6},{6,7},{7,8},{8,9},{9,10},{10,1... | collective-permute-start | bytes 884744 | tf_op jit(solution)/shard_map/ppermute | solution.py:345
  37.9 3.1 %shard_map.217 = (bf16[288,512]{1,0:T(8,128)(2,1)S(1)}, bf16[288,512]{1,0:T(8,128)(2,1)S(1)}) custom-call(bf16[288,512]{1,0:T(8,128)(2,1)S(1)} %get-tuple-element.50.h1, bf16[288,512]{1,0:T(8,128)(2,1)S(1)} %get-tuple-element.53.h2, bf16[512,2048]{1,0:T(8,128)(2,1)S(1)} %copy-done.7, bf16[2048,512]{1,0:T(8,128)(2,1)S(1)} %copy-done.8), custom_call_target="tpu_custom_call" | custom-call | flops 3000000000 | bytes 4784128 | tf_op jit(solution)/shard_map/pallas_call | solution.py:149
  41.1 6.4 %collective-permute-done.1.h = bf16[288,512]{1,0:T(8,128)(2,1)S(1)} collective-permute-done((bf16[288,512]{1,0:T(8,128)(2,1)S(1)}, bf16[288,512]{1,0:T(8,128)(2,1)S(1)}, u32[]{:S(2)}, u32[]{:S(2)}) %collective-permute-start.1) | collective-permute-done | bytes 294944 | tf_op jit(solution)/shard_map/ppermute | solution.py:345
  47.5 1.7 %shard_map.218.l1 = bf16[288,512]{1,0:T(8,128)(2,1)S(1)} custom-call(bf16[288,512]{1,0:T(8,128)(2,1)S(1)} %collective-permute-done.1.h, bf16[512,2048]{1,0:T(8,128)(2,1)S(1)} %copy-done.7, bf16[2048,512]{1,0:T(8,128)(2,1)S(1)} %copy-done.8), custom_call_target="tpu_custom_call" | custom-call | flops 2000000000 | bytes 4489216 | tf_op jit(solution)/shard_map/pallas_call | solution.py:149
  49.2 0.0 copy-start.3
  49.2 0.1 collective-permute-start.6
  49.3 0.3 collective-permute-start.7
  49.6 2.1 %collective-permute-done.4.h = bf16[288,512]{1,0:T(8,128)(2,1)S(1)} collective-permute-done((bf16[288,512]{1,0:T(8,128)(2,1)S(1)}, bf16[288,512]{1,0:T(8,128)(2,1)S(1)}, u32[]{:S(2)}, u32[]{:S(2)}) %collective-permute-start.4) | collective-permute-done | bytes 294944 | tf_op jit(solution)/shard_map/ppermute | solution.py:345
  51.7 1.7 %shard_map.219.l2 = bf16[288,512]{1,0:T(8,128)(2,1)S(1)} custom-call(bf16[288,512]{1,0:T(8,128)(2,1)S(1)} %collective-permute-done.4.h, bf16[512,2048]{1,0:T(8,128)(2,1)S(1)} %copy-done.7, bf16[2048,512]{1,0:T(8,128)(2,1)S(1)} %copy-done.8), custom_call_target="tpu_custom_call" | custom-call | flops 2000000000 | bytes 4489216 | tf_op jit(solution)/shard_map/pallas_call | solution.py:149
  53.5 1.8 %shard_map.220.own = bf16[144,1024]{1,0:T(8,128)(2,1)S(1)} custom-call(bf16[288,512]{1,0:T(8,128)(2,1)S(1)} %shard_map.218.l1, bf16[288,512]{1,0:T(8,128)(2,1)S(1)} %shard_map.219.l2, bf16[288,512]{1,0:T(8,128)(2,1)S(1)} %get-tuple-element.54.r1, bf16[288,512]{1,0:T(8,128)(2,1)S(1)} %get-tuple-element.58.r2, bf16[2,576,864]{2,1,0:T(8,128)(2,1)S(1)} %copy-done.3, ...), custom_call_target="tpu_custom_call" | custom-call | flops 1000000000 | bytes 7364608 | tf_op jit(solution)/shard_map/pallas_call | solution.py:149
  55.3 0.0 copy-start.15
  55.3 0.1 collective-permute-start.9
  55.4 2.7 %collective-permute-done.7.c = bf16[128,1024]{1,0:T(8,128)(2,1)S(1)} collective-permute-done((bf16[128,1024]{1,0:T(8,128)(2,1)S(1)}, bf16[128,1024]{1,0:T(8,128)(2,1)S(1)}, u32[]{:S(2)}, u32[]{:S(2)}) %collective-permute-start.7) | collective-permute-done | bytes 262176 | tf_op jit(solution)/shard_map/ppermute | solution.py:353
  58.1 1.8 %shard_map.221.own = bf16[144,1024]{1,0:T(8,128)(2,1)S(1)} custom-call(bf16[288,512]{1,0:T(8,128)(2,1)S(1)} %shard_map.218.l1, bf16[288,512]{1,0:T(8,128)(2,1)S(1)} %shard_map.219.l2, bf16[288,512]{1,0:T(8,128)(2,1)S(1)} %get-tuple-element.54.r1, bf16[288,512]{1,0:T(8,128)(2,1)S(1)} %get-tuple-element.58.r2, bf16[2,576,864]{2,1,0:T(8,128)(2,1)S(1)} %copy-done.3, ...), custom_call_target="tpu_custom_call" | custom-call | flops 1000000000 | bytes 7364608 | tf_op jit(solution)/shard_map/pallas_call | solution.py:149
  59.8 0.9 collective-permute-start.12
  60.7 2.1 %shard_map.222 = bf16[1152,512]{1,0:T(8,128)(2,1)} custom-call(bf16[288,512]{1,0:T(8,128)(2,1)S(1)} %shard_map.218.l1, bf16[288,512]{1,0:T(8,128)(2,1)S(1)} %shard_map.219.l2, bf16[288,512]{1,0:T(8,128)(2,1)S(1)} %get-tuple-element.54.r1, bf16[288,512]{1,0:T(8,128)(2,1)S(1)} %get-tuple-element.58.r2, bf16[576,576]{1,0:T(8,128)(2,1)S(1)} %copy-done.15), custom_call_target="tpu_custom_call" | custom-call | flops 2000000000 | bytes 1843200 | tf_op jit(solution)/shard_map/pallas_call | solution.py:149
  62.9 0.1 shard_map.223.o_theirs
  62.9 0.9 collective-permute-done.9.other
  63.9 0.9 copy-done.6
  64.7 2.2 %shard_map.224 = (bf16[288,1024]{1,0:T(8,128)(2,1)S(1)}, bf16[288,512]{1,0:T(8,128)(2,1)S(1)}) custom-call(s32[1]{0:T(128)} %bitcast.9.me, bf16[144,1024]{1,0:T(8,128)(2,1)S(1)} %shard_map.220.own, bf16[144,1024]{1,0:T(8,128)(2,1)S(1)} %collective-permute-done.9.other, bf16[3,512,1024]{2,1,0:T(8,128)(2,1)S(1)} %bitcast.14, bf16[256,256]{1,0:T(8,128)(2,1)S(1)} %copy-done.18, ...), custom_call_target="tpu_custom_call" | custom-call | flops 2000000000 | bytes 3870724 | tf_op jit(solution)/shard_map/pallas_call | solution.py:149
  67.0 3.0 %collective-permute-start.10 = (bf16[288,512]{1,0:T(8,128)(2,1)S(1)}, bf16[288,512]{1,0:T(8,128)(2,1)S(1)}, u32[]{:S(2)}, u32[]{:S(2)}) collective-permute-start(bf16[288,512]{1,0:T(8,128)(2,1)S(1)} %get-tuple-element.70.mine), channel_id=1, source_target_pairs={{0,1},{1,0},{2,3},{3,2},{4,5},{5,4},{6,7},{7,6},{8,9},{9,8},{10,11... | collective-permute-start | bytes 884744 | tf_op jit(solution)/shard_map/ppermute | solution.py:345
  70.0 0.9 collective-permute-done.12.other
  70.8 2.2 %shard_map.227 = (bf16[288,1024]{1,0:T(8,128)(2,1)S(1)}, bf16[288,512]{1,0:T(8,128)(2,1)S(1)}) custom-call(s32[1]{0:T(128)} %bitcast.9.me, bf16[144,1024]{1,0:T(8,128)(2,1)S(1)} %shard_map.221.own, bf16[144,1024]{1,0:T(8,128)(2,1)S(1)} %collective-permute-done.12.other, bf16[3,512,1024]{2,1,0:T(8,128)(2,1)S(1)} %bitcast.15, bf16[256,256]{1,0:T(8,128)(2,1)S(1)} %copy-done.18, ...), custom_call_target="tpu_custom_call" | custom-call | flops 2000000000 | bytes 3870724 | tf_op jit(solution)/shard_map/pallas_call | solution.py:149
  73.1 0.9 collective-permute-start.13
  74.0 4.6 %collective-permute-done.10.theirs = bf16[288,512]{1,0:T(8,128)(2,1)S(1)} collective-permute-done((bf16[288,512]{1,0:T(8,128)(2,1)S(1)}, bf16[288,512]{1,0:T(8,128)(2,1)S(1)}, u32[]{:S(2)}, u32[]{:S(2)}) %collective-permute-start.10) | collective-permute-done | bytes 294944 | tf_op jit(solution)/shard_map/ppermute | solution.py:345
  78.6 3.9 %shard_map.225 = (f32[144,1024]{1,0:T(8,128)S(1)}, bf16[144,1024]{1,0:T(8,128)(2,1)S(1)}, bf16[144,1024]{1,0:T(8,128)(2,1)S(1)}) custom-call(s32[1]{0:T(128)} %bitcast.9.me, bf16[288,1024]{1,0:T(8,128)(2,1)S(1)} %get-tuple-element.69.x, bf16[288,512]{1,0:T(8,128)(2,1)S(1)} %get-tuple-element.70.mine, bf16[288,512]{1,0:T(8,128)(2,1)S(1)} %collective-permute-done.10.theirs, ...), custom_call_target="tpu_custom_call" | custom-call | flops 100000000 | bytes 11665412 | tf_op jit(solution)/shard_map/pallas_call | solution.py:149
  82.5 2.8 %collective-permute-start.11 = (bf16[144,1024]{1,0:T(8,128)(2,1)S(1)}, bf16[144,1024]{1,0:T(8,128)(2,1)S(1)}, u32[]{:S(2)}, u32[]{:S(2)}) collective-permute-start(bf16[144,1024]{1,0:T(8,128)(2,1)S(1)} %get-tuple-element.73), channel_id=1, source_target_pairs={{0,1},{1,0},{2,3},{3,2},{4,5},{5,4},{6,7},{7,6},{8,9},{9,8},{10,11... | collective-permute-start | bytes 884744 | tf_op jit(solution)/shard_map/ppermute | solution.py:345
  85.3 3.9 %shard_map.228 = (f32[144,1024]{1,0:T(8,128)S(1)}, bf16[144,1024]{1,0:T(8,128)(2,1)S(1)}, bf16[144,1024]{1,0:T(8,128)(2,1)S(1)}) custom-call(s32[1]{0:T(128)} %bitcast.9.me, bf16[288,1024]{1,0:T(8,128)(2,1)S(1)} %get-tuple-element.77.x, bf16[288,512]{1,0:T(8,128)(2,1)S(1)} %get-tuple-element.78.mine, bf16[288,512]{1,0:T(8,128)(2,1)S(1)} %collective-permute-done.13.theirs, ...), custom_call_target="tpu_custom_call" | custom-call | flops 100000000 | bytes 11665412 | tf_op jit(solution)/shard_map/pallas_call | solution.py:149
  89.2 1.7 %collective-permute-start.14 = (bf16[144,1024]{1,0:T(8,128)(2,1)S(1)}, bf16[144,1024]{1,0:T(8,128)(2,1)S(1)}, u32[]{:S(2)}, u32[]{:S(2)}) collective-permute-start(bf16[144,1024]{1,0:T(8,128)(2,1)S(1)} %get-tuple-element.80), channel_id=1, source_target_pairs={{0,1},{1,0},{2,3},{3,2},{4,5},{5,4},{6,7},{7,6},{8,9},{9,8},{10,11... | collective-permute-start | bytes 884744 | tf_op jit(solution)/shard_map/ppermute | solution.py:345
  90.9 0.8 collective-permute-done.11.r
  91.7 0.5 shard_map.226.first
  92.2 5.9 %collective-permute-done.14.r = bf16[144,1024]{1,0:T(8,128)(2,1)S(1)} collective-permute-done((bf16[144,1024]{1,0:T(8,128)(2,1)S(1)}, bf16[144,1024]{1,0:T(8,128)(2,1)S(1)}, u32[]{:S(2)}, u32[]{:S(2)}) %collective-permute-start.14) | collective-permute-done | bytes 294944 | tf_op jit(solution)/shard_map/ppermute | solution.py:345
  98.1 1.3 %shard_map.229 = bf16[12,6,4,1024]{3,2,1,0:T(4,128)(2,1)} custom-call(bf16[6,6,4,1024]{3,2,1,0:T(4,128)(2,1)S(1)} %shard_map.226.first, f32[144,1024]{1,0:T(8,128)S(1)} %get-tuple-element.79.k, bf16[144,1024]{1,0:T(8,128)(2,1)S(1)} %collective-permute-done.14.r, bf16[144,1024]{1,0:T(8,128)(2,1)S(1)} %get-tuple-element.81.h, bf16[144,144]{1,0:T(8,128)(2,1)S(1)} %copy-done.5), custom_call_target="tpu_custom_call" | custom-call | flops 100000000 | bytes 1516032 | tf_op jit(solution)/shard_map/pallas_call | solution.py:149
  (42 shorter events, 0.1 us)
Async XLA Ops:
  0.6 8.5 %copy-start.19 = (bf16[8,512]{1,0:T(8,128)(2,1)S(1)}, bf16[8,512]{1,0:T(8,128)(2,1)}, u32[]{:S(2)}) copy-start(bf16[8,512]{1,0:T(8,128)(2,1)} %constant.30.clone.spread) | copy-start | bytes 24580
  0.6 8.5 %copy-start.4 = (bf16[512,1024]{1,0:T(8,128)(2,1)S(1)}, bf16[512,1024]{1,0:T(8,128)(2,1)}, u32[]{:S(2)}) copy-start(bf16[512,1024]{1,0:T(8,128)(2,1)} %o_mine.3) | copy-start | bytes 3145732
  0.7 1.4 %copy-start.10 = (bf16[4,24,12,512]{3,1,2,0:T(8,128)(2,1)S(1)}, bf16[4,24,12,512]{3,1,2,0:T(8,128)(2,1)}, u32[]{:S(2)}) copy-start(bf16[4,24,12,512]{3,1,2,0:T(8,128)(2,1)} %param.21) | copy-start | bytes 3538948
  2.0 7.1 %copy-start.12 = (s32[4,24,12]{1,0,2:T(4,128)S(1)}, s32[4,24,12]{1,0,2:T(4,128)}, u32[]{:S(2)}) copy-start(s32[4,24,12]{1,0,2:T(4,128)} %param.22) | copy-start | bytes 13828
  2.0 7.1 %copy-start.13 = (bf16[8]{0:T(256)(128)(2,1)S(1)}, bf16[8]{0:T(256)(128)(2,1)}, u32[]{:S(2)}) copy-start(bf16[8]{0:T(256)(128)(2,1)} %param.27) | copy-start | bytes 52
  2.0 7.1 %copy-start.14 = (bf16[8]{0:T(256)(128)(2,1)S(1)}, bf16[8]{0:T(256)(128)(2,1)}, u32[]{:S(2)}) copy-start(bf16[8]{0:T(256)(128)(2,1)} %param.33) | copy-start | bytes 52
  2.0 7.1 %copy-start.16 = (bf16[1152,48]{1,0:T(8,128)(2,1)S(1)}, bf16[1152,48]{1,0:T(8,128)(2,1)}, u32[]{:S(2)}) copy-start(bf16[1152,48]{1,0:T(8,128)(2,1)} %constant.31.clone.rows) | copy-start | bytes 331780
  2.0 7.1 %copy-start.17 = (bf16[1152,25]{1,0:T(8,128)(2,1)S(1)}, bf16[1152,25]{1,0:T(8,128)(2,1)}, u32[]{:S(2)}) copy-start(bf16[1152,25]{1,0:T(8,128)(2,1)} %constant.32.clone.keep) | copy-start | bytes 172804
  2.5 19.2 %collective-permute-start = (bf16[576,512]{1,0:T(8,128)(2,1)S(1)}, bf16[576,512]{1,0:T(8,128)(2,1)S(1)}, u32[]{:S(2)}, u32[]{:S(2)}) collective-permute-start(bf16[576,512]{1,0:T(8,128)(2,1)S(1)} %get-tuple-element.43), channel_id=1, source_target_pairs={{0,15},{1,0},{2,1},{3,2},{4,3},{5,4},{6,5},{7,6},{8,7},{9,8},{10,9... | collective-permute-start | bytes 1769480 | tf_op jit(solution)/shard_map/ppermute | solution.py:345
  9.2 15.5 %copy-start.9 = (bf16[512,3,512]{2,0,1:T(8,128)(2,1)S(1)}, bf16[512,3,512]{2,0,1:T(8,128)(2,1)}, u32[]{:S(2)}) copy-start(bf16[512,3,512]{2,0,1:T(8,128)(2,1)} %param.23) | copy-start | bytes 4718596
  9.2 15.5 %copy-start.11 = (bf16[512,512]{1,0:T(8,128)(2,1)S(1)}, bf16[512,512]{1,0:T(8,128)(2,1)}, u32[]{:S(2)}) copy-start(bf16[512,512]{1,0:T(8,128)(2,1)} %out.3) | copy-start | bytes 1572868
  9.2 15.5 %copy-start.18 = (bf16[256,256]{1,0:T(8,128)(2,1)S(1)}, bf16[256,256]{1,0:T(8,128)(2,1)}, u32[]{:S(2)}) copy-start(bf16[256,256]{1,0:T(8,128)(2,1)} %constant.28.clone.ones) | copy-start | bytes 393220
  9.2 15.5 %copy-start.20 = (bf16[8,128]{1,0:T(8,128)(2,1)S(1)}, bf16[8,128]{1,0:T(8,128)(2,1)}, u32[]{:S(2)}) copy-start(bf16[8,128]{1,0:T(8,128)(2,1)} %constant.29.clone.lanes) | copy-start | bytes 6148
  21.8 8.8 %collective-permute-start.2 = (bf16[216,512]{1,0:T(8,128)(2,1)S(1)}, bf16[216,512]{1,0:T(8,128)(2,1)S(1)}, u32[]{:S(2)}, u32[]{:S(2)}) collective-permute-start(bf16[216,512]{1,0:T(8,128)(2,1)S(1)} %get-tuple-element.46), channel_id=1, source_target_pairs={{0,16},{16,32},{32,48},{48,64},{64,80},{80,96},{96,112},{112,0},{1... | collective-permute-start | bytes 663560 | tf_op jit(solution)/shard_map/ppermute | solution.py:345
  21.8 8.8 %collective-permute-start.3 = (bf16[144,512]{1,0:T(8,128)(2,1)S(1)}, bf16[144,512]{1,0:T(8,128)(2,1)S(1)}, u32[]{:S(2)}, u32[]{:S(2)}) collective-permute-start(bf16[144,512]{1,0:T(8,128)(2,1)S(1)} %get-tuple-element.51), channel_id=1, source_target_pairs={{0,112},{16,0},{32,16},{48,32},{64,48},{80,64},{96,80},{112,96},{1... | collective-permute-start | bytes 442376 | tf_op jit(solution)/shard_map/ppermute | solution.py:345
  28.1 19.4 %collective-permute-start.1 = (bf16[288,512]{1,0:T(8,128)(2,1)S(1)}, bf16[288,512]{1,0:T(8,128)(2,1)S(1)}, u32[]{:S(2)}, u32[]{:S(2)}) collective-permute-start(bf16[288,512]{1,0:T(8,128)(2,1)S(1)} %get-tuple-element.49), channel_id=1, source_target_pairs={{0,1},{1,2},{2,3},{3,4},{4,5},{5,6},{6,7},{7,8},{8,9},{9,10},{10,1... | collective-permute-start | bytes 884744 | tf_op jit(solution)/shard_map/ppermute | solution.py:345
  29.8 8.2 %copy-start.7 = (bf16[512,2048]{1,0:T(8,128)(2,1)S(1)}, bf16[512,2048]{1,0:T(8,128)(2,1)}, u32[]{:S(2)}) copy-start(bf16[512,2048]{1,0:T(8,128)(2,1)} %expand.7) | copy-start | bytes 6291460
  29.8 8.2 %copy-start.8 = (bf16[2048,512]{1,0:T(8,128)(2,1)S(1)}, bf16[2048,512]{1,0:T(8,128)(2,1)}, u32[]{:S(2)}) copy-start(bf16[2048,512]{1,0:T(8,128)(2,1)} %shrink.7) | copy-start | bytes 6291460
  29.8 19.5 %collective-permute-start.5 = (bf16[128,1024]{1,0:T(8,128)(2,1)S(1)}, bf16[128,1024]{1,0:T(8,128)(2,1)S(1)}, u32[]{:S(2)}, u32[]{:S(2)}) collective-permute-start(bf16[128,1024]{1,0:T(8,128)(2,1)S(1)} %get-tuple-element.62), channel_id=1, source_target_pairs={{0,1},{1,0},{2,3},{3,2},{4,5},{5,4},{6,7},{7,6},{8,9},{9,8},{10,11... | collective-permute-start | bytes 786440 | tf_op jit(solution)/shard_map/ppermute | solution.py:345
  34.9 16.8 %collective-permute-start.4 = (bf16[288,512]{1,0:T(8,128)(2,1)S(1)}, bf16[288,512]{1,0:T(8,128)(2,1)S(1)}, u32[]{:S(2)}, u32[]{:S(2)}) collective-permute-start(bf16[288,512]{1,0:T(8,128)(2,1)S(1)} %get-tuple-element.56), channel_id=1, source_target_pairs={{0,1},{1,2},{2,3},{3,4},{4,5},{5,6},{6,7},{7,8},{8,9},{9,10},{10,1... | collective-permute-start | bytes 884744 | tf_op jit(solution)/shard_map/ppermute | solution.py:345
  49.2 4.2 %copy-start.2 = (bf16[2048,1024]{1,0:T(8,128)(2,1)S(1)}, bf16[2048,1024]{1,0:T(8,128)(2,1)}, u32[]{:S(2)}) copy-start(bf16[2048,1024]{1,0:T(8,128)(2,1)} %weight.3) | copy-start | bytes 12582916
  49.2 4.2 %copy-start.3 = (bf16[2,576,864]{2,1,0:T(8,128)(2,1)S(1)}, bf16[2,576,864]{2,1,0:T(8,128)(2,1)}, u32[]{:S(2)}) copy-start(bf16[2,576,864]{2,1,0:T(8,128)(2,1)} %constant.33.clone.pm) | copy-start | bytes 5971972
  49.2 13.6 %collective-permute-start.6 = (bf16[128,1024]{1,0:T(8,128)(2,1)S(1)}, bf16[128,1024]{1,0:T(8,128)(2,1)S(1)}, u32[]{:S(2)}, u32[]{:S(2)}) collective-permute-start(bf16[128,1024]{1,0:T(8,128)(2,1)S(1)} %collective-permute-done.5.a), channel_id=1, source_target_pairs={{0,16},{16,0},{32,48},{48,32},{64,80},{80,64},{96,112},{112,96},{1... | collective-permute-start | bytes 786440 | tf_op jit(solution)/shard_map/ppermute | solution.py:353
  49.3 8.7 %collective-permute-start.7 = (bf16[128,1024]{1,0:T(8,128)(2,1)S(1)}, bf16[128,1024]{1,0:T(8,128)(2,1)S(1)}, u32[]{:S(2)}, u32[]{:S(2)}) collective-permute-start(bf16[128,1024]{1,0:T(8,128)(2,1)S(1)} %collective-permute-done.5.a), channel_id=1, source_target_pairs={{0,32},{16,48},{32,0},{48,16},{64,96},{80,112},{96,64},{112,80},{1... | collective-permute-start | bytes 786440 | tf_op jit(solution)/shard_map/ppermute | solution.py:353
  55.3 5.5 %copy-start.15 = (bf16[576,576]{1,0:T(8,128)(2,1)S(1)}, bf16[576,576]{1,0:T(8,128)(2,1)}, u32[]{:S(2)}) copy-start(bf16[576,576]{1,0:T(8,128)(2,1)} %constant.34.clone.perm) | copy-start | bytes 1990660
  55.3 8.6 %collective-permute-start.9 = (bf16[144,1024]{1,0:T(8,128)(2,1)S(1)}, bf16[144,1024]{1,0:T(8,128)(2,1)S(1)}, u32[]{:S(2)}, u32[]{:S(2)}) collective-permute-start(bf16[144,1024]{1,0:T(8,128)(2,1)S(1)} %shard_map.220.own), channel_id=1, source_target_pairs={{0,1},{1,0},{2,3},{3,2},{4,5},{5,4},{6,7},{7,6},{8,9},{9,8},{10,11... | collective-permute-start | bytes 884744 | tf_op jit(solution)/shard_map/ppermute | solution.py:345
  58.1 4.8 %collective-permute-start.8 = (bf16[128,1024]{1,0:T(8,128)(2,1)S(1)}, bf16[128,1024]{1,0:T(8,128)(2,1)S(1)}, u32[]{:S(2)}, u32[]{:S(2)}) collective-permute-start(bf16[128,1024]{1,0:T(8,128)(2,1)S(1)} %collective-permute-done.7.c), channel_id=1, source_target_pairs={{0,16},{16,0},{32,48},{48,32},{64,80},{80,64},{96,112},{112,96},{1... | collective-permute-start | bytes 786440 | tf_op jit(solution)/shard_map/ppermute | solution.py:353
  59.8 11.0 %collective-permute-start.12 = (bf16[144,1024]{1,0:T(8,128)(2,1)S(1)}, bf16[144,1024]{1,0:T(8,128)(2,1)S(1)}, u32[]{:S(2)}, u32[]{:S(2)}) collective-permute-start(bf16[144,1024]{1,0:T(8,128)(2,1)S(1)} %shard_map.221.own), channel_id=1, source_target_pairs={{0,1},{1,0},{2,3},{3,2},{4,5},{5,4},{6,7},{7,6},{8,9},{9,8},{10,11... | collective-permute-start | bytes 884744 | tf_op jit(solution)/shard_map/ppermute | solution.py:345
  62.9 1.9 %copy-start.6 = (bf16[512,3,1024]{2,0,1:T(8,128)(2,1)S(1)}, bf16[512,3,1024]{2,0,1:T(8,128)(2,1)}, u32[]{:S(2)}) copy-start(bf16[512,3,1024]{2,0,1:T(8,128)(2,1)} %param.29) | copy-start | bytes 9437188
  64.7 13.9 %copy-start.1 = (bf16[2048,1024]{1,0:T(8,128)(2,1)S(1)}, bf16[2048,1024]{1,0:T(8,128)(2,1)}, u32[]{:S(2)}) copy-start(bf16[2048,1024]{1,0:T(8,128)(2,1)} %shrink.9) | copy-start | bytes 12582916
  67.0 11.7 %copy-start = (bf16[2048,1024]{1,0:T(8,128)(2,1)S(1)}, bf16[2048,1024]{1,0:T(8,128)(2,1)}, u32[]{:S(2)}) copy-start(bf16[2048,1024]{1,0:T(8,128)(2,1)} %expand.9) | copy-start | bytes 12582916
  67.0 11.6 %collective-permute-start.10 = (bf16[288,512]{1,0:T(8,128)(2,1)S(1)}, bf16[288,512]{1,0:T(8,128)(2,1)S(1)}, u32[]{:S(2)}, u32[]{:S(2)}) collective-permute-start(bf16[288,512]{1,0:T(8,128)(2,1)S(1)} %get-tuple-element.70.mine), channel_id=1, source_target_pairs={{0,1},{1,0},{2,3},{3,2},{4,5},{5,4},{6,7},{7,6},{8,9},{9,8},{10,11... | collective-permute-start | bytes 884744 | tf_op jit(solution)/shard_map/ppermute | solution.py:345
  73.1 12.3 %collective-permute-start.13 = (bf16[288,512]{1,0:T(8,128)(2,1)S(1)}, bf16[288,512]{1,0:T(8,128)(2,1)S(1)}, u32[]{:S(2)}, u32[]{:S(2)}) collective-permute-start(bf16[288,512]{1,0:T(8,128)(2,1)S(1)} %get-tuple-element.78.mine), channel_id=1, source_target_pairs={{0,1},{1,0},{2,3},{3,2},{4,5},{5,4},{6,7},{7,6},{8,9},{9,8},{10,11... | collective-permute-start | bytes 884744 | tf_op jit(solution)/shard_map/ppermute | solution.py:345
  82.5 9.2 %collective-permute-start.11 = (bf16[144,1024]{1,0:T(8,128)(2,1)S(1)}, bf16[144,1024]{1,0:T(8,128)(2,1)S(1)}, u32[]{:S(2)}, u32[]{:S(2)}) collective-permute-start(bf16[144,1024]{1,0:T(8,128)(2,1)S(1)} %get-tuple-element.73), channel_id=1, source_target_pairs={{0,1},{1,0},{2,3},{3,2},{4,5},{5,4},{6,7},{7,6},{8,9},{9,8},{10,11... | collective-permute-start | bytes 884744 | tf_op jit(solution)/shard_map/ppermute | solution.py:345
  85.3 6.4 %copy-start.5 = (bf16[144,144]{1,0:T(8,128)(2,1)S(1)}, bf16[144,144]{1,0:T(8,128)(2,1)}, u32[]{:S(2)}) copy-start(bf16[144,144]{1,0:T(8,128)(2,1)} %constant.35.clone.pout) | copy-start | bytes 124420
  89.2 8.9 %collective-permute-start.14 = (bf16[144,1024]{1,0:T(8,128)(2,1)S(1)}, bf16[144,1024]{1,0:T(8,128)(2,1)S(1)}, u32[]{:S(2)}, u32[]{:S(2)}) collective-permute-start(bf16[144,1024]{1,0:T(8,128)(2,1)S(1)} %get-tuple-element.80), channel_id=1, source_target_pairs={{0,1},{1,0},{2,3},{3,2},{4,5},{5,4},{6,7},{7,6},{8,9},{9,8},{10,11... | collective-permute-start | bytes 884744 | tf_op jit(solution)/shard_map/ppermute | solution.py:345

commit v3 on v2

--- a/solution.py
+++ b/solution.py
@@ -419,7 +419,7 @@
     shared = [classes, w_one, output_one, ones, lanes, s_one]
     hr1, hl1 = call(first_kernel, [tok(288)] * 2, [right, left] + shared, 4 * 10**9)
     hl1 = behind(hl1, col_axes, 1)
-    shared[0] = after(classes, hr1)
+    shared[0] = after(classes, (hr1, oa))
     hr2, hl2 = call(
         second_kernel, [tok(288)] * 2, [right, left, down, up] + shared, 6 * 10**9
     )

time: 99.6 us -> 97.8 us (0.982)
  waiting for transfers between devices: 36.5 us -> 35.1 us
    ppermute x3, waiting for transfers between devices: 2.7 us -> 0.01 us  [across(): lax.ppermute(value, axis, [(s, s ^ flip) for s in range(lax.axis_size(axi...]
    ppermute x3, starting transfers between devices: 0.37 us -> 1.74 us  [across(): lax.ppermute(value, axis, [(s, s ^ flip) for s in range(lax.axis_size(axi...]
    ppermute x12, waiting for transfers between devices: 33.8 us -> 35.1 us  [behind(): lax.ppermute(value, axis, [(s, (s + steps) % count) for s in range(count)])]
  transfers between devices with their start and end apart: 15 -> 15, of which waited for: 9 -> 9; matrix products, arithmetic and copies ran while one was open for 0% -> 0% of each run, Pallas kernels for 33% -> 34%
where the time goes in v3:
time: 97.8 us; the launch traced here: 97.7 us
  waiting for transfers between devices  35.1 us (36%)
  Pallas kernels  34.8 us (36%)
  starting transfers between devices  25.3 us (26%)
  local copies, waits for them, and re-layouts  1.46 us (1%)
  between operations  0.99 us (1%)
    ppermute x12, waiting for transfers between devices, behind(): lax.ppermute(value, axis, [(s, (s + steps) % count) for s in range(count)])  35.1 us
    pallas_call x18, Pallas kernels, call(): pl.pallas_call(kernel, out_shape=[jax.ShapeDtypeStruct(shape, kind) for s...  34.8 us
    ppermute x12, starting transfers between devices, behind(): lax.ppermute(value, axis, [(s, (s + steps) % count) for s in range(count)])  23.6 us
  transfers between devices with their start and end apart: 15, of which 9 were waited for; matrix products, arithmetic and copies ran while one was open for 0% of the time, Pallas kernels for 34%

profile of v3, /device:TPU:0, one launch (start us, length us, event | category | flops | bytes accessed | tf_op | source)
XLA Modules:
  0.0 97.7 jit_solution(806406681357371023)
XLA Ops:
  0.6 0.0 copy-start.19
  0.7 1.4 %copy-done.10 = bf16[4,24,12,512]{3,1,2,0:T(8,128)(2,1)S(1)} copy-done((bf16[4,24,12,512]{3,1,2,0:T(8,128)(2,1)S(1)}, bf16[4,24,12,512]{3,1,2,0:T(8,128)(2,1)}, u32[]{:S(2)}) %copy-start.10) | copy-done | bytes 1179672
  2.0 0.0 copy-start.17
  2.0 0.5 shard_map.212
  2.5 6.6 %collective-permute-start = (bf16[576,512]{1,0:T(8,128)(2,1)S(1)}, bf16[576,512]{1,0:T(8,128)(2,1)S(1)}, u32[]{:S(2)}, u32[]{:S(2)}) collective-permute-start(bf16[576,512]{1,0:T(8,128)(2,1)S(1)} %get-tuple-element.43), channel_id=1, source_target_pairs={{0,15},{1,0},{2,1},{3,2},{4,3},{5,4},{6,5},{7,6},{8,7},{9,8},{10,9... | collective-permute-start | bytes 1769480 | tf_op jit(solution)/shard_map/ppermute | solution.py:345
  9.2 0.0 copy-start.20
  9.2 0.4 shard_map.213
  9.6 12.1 %collective-permute-done.left_all.left = bf16[576,512]{1,0:T(8,128)(2,1)S(1)} collective-permute-done((bf16[576,512]{1,0:T(8,128)(2,1)S(1)}, bf16[576,512]{1,0:T(8,128)(2,1)S(1)}, u32[]{:S(2)}, u32[]{:S(2)}) %collective-permute-start) | collective-permute-done | bytes 589856 | tf_op jit(solution)/shard_map/ppermute | solution.py:345
  21.8 0.0 collective-permute-start.2
  21.8 2.9 %collective-permute-start.3 = (bf16[144,512]{1,0:T(8,128)(2,1)S(1)}, bf16[144,512]{1,0:T(8,128)(2,1)S(1)}, u32[]{:S(2)}, u32[]{:S(2)}) collective-permute-start(bf16[144,512]{1,0:T(8,128)(2,1)S(1)} %get-tuple-element.51), channel_id=1, source_target_pairs={{0,112},{16,0},{32,16},{48,32},{64,48},{80,64},{96,80},{112,96},{1... | collective-permute-start | bytes 442376 | tf_op jit(solution)/shard_map/ppermute | solution.py:345
  24.7 1.6 %collective-permute-start.4 = (bf16[128,1024]{1,0:T(8,128)(2,1)S(1)}, bf16[128,1024]{1,0:T(8,128)(2,1)S(1)}, u32[]{:S(2)}, u32[]{:S(2)}) collective-permute-start(bf16[128,1024]{1,0:T(8,128)(2,1)S(1)} %get-tuple-element.53), channel_id=1, source_target_pairs={{0,1},{1,0},{2,3},{3,2},{4,5},{5,4},{6,7},{7,6},{8,9},{9,8},{10,11... | collective-permute-start | bytes 786440 | tf_op jit(solution)/shard_map/ppermute | solution.py:345
  26.3 3.4 %shard_map.215 = (bf16[288,512]{1,0:T(8,128)(2,1)S(1)}, bf16[288,512]{1,0:T(8,128)(2,1)S(1)}) custom-call(bf16[576,512]{1,0:T(8,128)(2,1)S(1)} %get-tuple-element.42.right_all.right, bf16[576,512]{1,0:T(8,128)(2,1)S(1)} %collective-permute-done.left_all.left, bf16[1152,128]{1,0:T(8,128)(2,1)S(1)} %get-tuple-element.54.classes, ...), custom_call_target="tpu_custom_call" | custom-call | flops 4000000000 | bytes 3706880 | tf_op jit(solution)/shard_map/pallas_call | solution.py:149
  29.7 2.0 %collective-permute-start.1 = (bf16[288,512]{1,0:T(8,128)(2,1)S(1)}, bf16[288,512]{1,0:T(8,128)(2,1)S(1)}, u32[]{:S(2)}, u32[]{:S(2)}) collective-permute-start(bf16[288,512]{1,0:T(8,128)(2,1)S(1)} %get-tuple-element.49), channel_id=1, source_target_pairs={{0,1},{1,2},{2,3},{3,4},{4,5},{5,6},{6,7},{7,8},{8,9},{9,10},{10,1... | collective-permute-start | bytes 884744 | tf_op jit(solution)/shard_map/ppermute | solution.py:345
  31.7 1.4 %collective-permute-done.4.a = bf16[128,1024]{1,0:T(8,128)(2,1)S(1)} collective-permute-done((bf16[128,1024]{1,0:T(8,128)(2,1)S(1)}, bf16[128,1024]{1,0:T(8,128)(2,1)S(1)}, u32[]{:S(2)}, u32[]{:S(2)}) %collective-permute-start.4) | collective-permute-done | bytes 262176 | tf_op jit(solution)/shard_map/ppermute | solution.py:345
  33.1 4.4 %shard_map.216 = (bf16[288,512]{1,0:T(8,128)(2,1)S(1)}, bf16[288,512]{1,0:T(8,128)(2,1)S(1)}) custom-call(bf16[576,512]{1,0:T(8,128)(2,1)S(1)} %get-tuple-element.42.right_all.right, bf16[576,512]{1,0:T(8,128)(2,1)S(1)} %collective-permute-done.left_all.left, bf16[216,512]{1,0:T(8,128)(2,1)S(1)} %collective-permute-done.2.down, ...), custom_call_target="tpu_custom_call" | custom-call | flops 6000000000 | bytes 4075520 | tf_op jit(solution)/shard_map/pallas_call | solution.py:149
  37.5 2.3 %collective-permute-start.5 = (bf16[288,512]{1,0:T(8,128)(2,1)S(1)}, bf16[288,512]{1,0:T(8,128)(2,1)S(1)}, u32[]{:S(2)}, u32[]{:S(2)}) collective-permute-start(bf16[288,512]{1,0:T(8,128)(2,1)S(1)} %get-tuple-element.58), channel_id=1, source_target_pairs={{0,1},{1,2},{2,3},{3,4},{4,5},{5,6},{6,7},{7,8},{8,9},{9,10},{10,1... | collective-permute-start | bytes 884744 | tf_op jit(solution)/shard_map/ppermute | solution.py:345
  39.8 3.1 %shard_map.217 = (bf16[288,512]{1,0:T(8,128)(2,1)S(1)}, bf16[288,512]{1,0:T(8,128)(2,1)S(1)}) custom-call(bf16[288,512]{1,0:T(8,128)(2,1)S(1)} %get-tuple-element.50.h1, bf16[288,512]{1,0:T(8,128)(2,1)S(1)} %get-tuple-element.55.h2, bf16[512,2048]{1,0:T(8,128)(2,1)S(1)} %copy-done.7, bf16[2048,512]{1,0:T(8,128)(2,1)S(1)} %copy-done.8), custom_call_target="tpu_custom_call" | custom-call | flops 3000000000 | bytes 4784128 | tf_op jit(solution)/shard_map/pallas_call | solution.py:149
  42.9 1.7 %shard_map.218.l1 = bf16[288,512]{1,0:T(8,128)(2,1)S(1)} custom-call(bf16[288,512]{1,0:T(8,128)(2,1)S(1)} %collective-permute-done.1.h, bf16[512,2048]{1,0:T(8,128)(2,1)S(1)} %copy-done.7, bf16[2048,512]{1,0:T(8,128)(2,1)S(1)} %copy-done.8), custom_call_target="tpu_custom_call" | custom-call | flops 2000000000 | bytes 4489216 | tf_op jit(solution)/shard_map/pallas_call | solution.py:149
  44.6 0.0 copy-start.3
  44.6 0.1 collective-permute-start.6
  44.7 1.6 %collective-permute-start.7 = (bf16[128,1024]{1,0:T(8,128)(2,1)S(1)}, bf16[128,1024]{1,0:T(8,128)(2,1)S(1)}, u32[]{:S(2)}, u32[]{:S(2)}) collective-permute-start(bf16[128,1024]{1,0:T(8,128)(2,1)S(1)} %collective-permute-done.4.a), channel_id=1, source_target_pairs={{0,32},{16,48},{32,0},{48,16},{64,96},{80,112},{96,64},{112,80},{1... | collective-permute-start | bytes 786440 | tf_op jit(solution)/shard_map/ppermute | solution.py:353
  46.3 4.1 %collective-permute-done.5.h = bf16[288,512]{1,0:T(8,128)(2,1)S(1)} collective-permute-done((bf16[288,512]{1,0:T(8,128)(2,1)S(1)}, bf16[288,512]{1,0:T(8,128)(2,1)S(1)}, u32[]{:S(2)}, u32[]{:S(2)}) %collective-permute-start.5) | collective-permute-done | bytes 294944 | tf_op jit(solution)/shard_map/ppermute | solution.py:345
  50.4 1.7 %shard_map.219.l2 = bf16[288,512]{1,0:T(8,128)(2,1)S(1)} custom-call(bf16[288,512]{1,0:T(8,128)(2,1)S(1)} %collective-permute-done.5.h, bf16[512,2048]{1,0:T(8,128)(2,1)S(1)} %copy-done.7, bf16[2048,512]{1,0:T(8,128)(2,1)S(1)} %copy-done.8), custom_call_target="tpu_custom_call" | custom-call | flops 2000000000 | bytes 4489216 | tf_op jit(solution)/shard_map/pallas_call | solution.py:149
  52.1 1.8 %shard_map.220.own = bf16[144,1024]{1,0:T(8,128)(2,1)S(1)} custom-call(bf16[288,512]{1,0:T(8,128)(2,1)S(1)} %shard_map.218.l1, bf16[288,512]{1,0:T(8,128)(2,1)S(1)} %shard_map.219.l2, bf16[288,512]{1,0:T(8,128)(2,1)S(1)} %get-tuple-element.56.r1, bf16[288,512]{1,0:T(8,128)(2,1)S(1)} %get-tuple-element.60.r2, bf16[2,576,864]{2,1,0:T(8,128)(2,1)S(1)} %copy-done.3, ...), custom_call_target="tpu_custom_call" | custom-call | flops 1000000000 | bytes 7364608 | tf_op jit(solution)/shard_map/pallas_call | solution.py:149
  53.9 0.0 copy-start.15
  53.9 0.1 collective-permute-start.9
  54.0 0.1 collective-permute-start.8
  54.1 1.8 %shard_map.221.own = bf16[144,1024]{1,0:T(8,128)(2,1)S(1)} custom-call(bf16[288,512]{1,0:T(8,128)(2,1)S(1)} %shard_map.218.l1, bf16[288,512]{1,0:T(8,128)(2,1)S(1)} %shard_map.219.l2, bf16[288,512]{1,0:T(8,128)(2,1)S(1)} %get-tuple-element.56.r1, bf16[288,512]{1,0:T(8,128)(2,1)S(1)} %get-tuple-element.60.r2, bf16[2,576,864]{2,1,0:T(8,128)(2,1)S(1)} %copy-done.3, ...), custom_call_target="tpu_custom_call" | custom-call | flops 1000000000 | bytes 7364608 | tf_op jit(solution)/shard_map/pallas_call | solution.py:149
  55.9 3.5 %collective-permute-start.12 = (bf16[144,1024]{1,0:T(8,128)(2,1)S(1)}, bf16[144,1024]{1,0:T(8,128)(2,1)S(1)}, u32[]{:S(2)}, u32[]{:S(2)}) collective-permute-start(bf16[144,1024]{1,0:T(8,128)(2,1)S(1)} %shard_map.221.own), channel_id=1, source_target_pairs={{0,1},{1,0},{2,3},{3,2},{4,5},{5,4},{6,7},{7,6},{8,9},{9,8},{10,11... | collective-permute-start | bytes 884744 | tf_op jit(solution)/shard_map/ppermute | solution.py:345
  59.4 2.1 %shard_map.222 = bf16[1152,512]{1,0:T(8,128)(2,1)} custom-call(bf16[288,512]{1,0:T(8,128)(2,1)S(1)} %shard_map.218.l1, bf16[288,512]{1,0:T(8,128)(2,1)S(1)} %shard_map.219.l2, bf16[288,512]{1,0:T(8,128)(2,1)S(1)} %get-tuple-element.56.r1, bf16[288,512]{1,0:T(8,128)(2,1)S(1)} %get-tuple-element.60.r2, bf16[576,576]{1,0:T(8,128)(2,1)S(1)} %copy-done.15), custom_call_target="tpu_custom_call" | custom-call | flops 2000000000 | bytes 1843200 | tf_op jit(solution)/shard_map/pallas_call | solution.py:149
  61.5 0.1 shard_map.223.o_theirs
  61.6 2.0 %collective-permute-done.9.other = bf16[144,1024]{1,0:T(8,128)(2,1)S(1)} collective-permute-done((bf16[144,1024]{1,0:T(8,128)(2,1)S(1)}, bf16[144,1024]{1,0:T(8,128)(2,1)S(1)}, u32[]{:S(2)}, u32[]{:S(2)}) %collective-permute-start.9) | collective-permute-done | bytes 294944 | tf_op jit(solution)/shard_map/ppermute | solution.py:345
  63.6 2.2 %shard_map.224 = (bf16[288,1024]{1,0:T(8,128)(2,1)S(1)}, bf16[288,512]{1,0:T(8,128)(2,1)S(1)}) custom-call(s32[1]{0:T(128)} %bitcast.9.me, bf16[144,1024]{1,0:T(8,128)(2,1)S(1)} %shard_map.220.own, bf16[144,1024]{1,0:T(8,128)(2,1)S(1)} %collective-permute-done.9.other, bf16[3,512,1024]{2,1,0:T(8,128)(2,1)S(1)} %bitcast.14, bf16[256,256]{1,0:T(8,128)(2,1)S(1)} %copy-done.18, ...), custom_call_target="tpu_custom_call" | custom-call | flops 2000000000 | bytes 3870724 | tf_op jit(solution)/shard_map/pallas_call | solution.py:149
  65.8 0.3 collective-permute-start.10
  66.1 2.4 %collective-permute-done.12.other = bf16[144,1024]{1,0:T(8,128)(2,1)S(1)} collective-permute-done((bf16[144,1024]{1,0:T(8,128)(2,1)S(1)}, bf16[144,1024]{1,0:T(8,128)(2,1)S(1)}, u32[]{:S(2)}, u32[]{:S(2)}) %collective-permute-start.12) | collective-permute-done | bytes 294944 | tf_op jit(solution)/shard_map/ppermute | solution.py:345
  68.5 2.2 %shard_map.227 = (bf16[288,1024]{1,0:T(8,128)(2,1)S(1)}, bf16[288,512]{1,0:T(8,128)(2,1)S(1)}) custom-call(s32[1]{0:T(128)} %bitcast.9.me, bf16[144,1024]{1,0:T(8,128)(2,1)S(1)} %shard_map.221.own, bf16[144,1024]{1,0:T(8,128)(2,1)S(1)} %collective-permute-done.12.other, bf16[3,512,1024]{2,1,0:T(8,128)(2,1)S(1)} %bitcast.15, bf16[256,256]{1,0:T(8,128)(2,1)S(1)} %copy-done.18, ...), custom_call_target="tpu_custom_call" | custom-call | flops 2000000000 | bytes 3870724 | tf_op jit(solution)/shard_map/pallas_call | solution.py:149
  70.7 1.8 %collective-permute-start.13 = (bf16[288,512]{1,0:T(8,128)(2,1)S(1)}, bf16[288,512]{1,0:T(8,128)(2,1)S(1)}, u32[]{:S(2)}, u32[]{:S(2)}) collective-permute-start(bf16[288,512]{1,0:T(8,128)(2,1)S(1)} %get-tuple-element.78.mine), channel_id=1, source_target_pairs={{0,1},{1,0},{2,3},{3,2},{4,5},{5,4},{6,7},{7,6},{8,9},{9,8},{10,11... | collective-permute-start | bytes 884744 | tf_op jit(solution)/shard_map/ppermute | solution.py:345
  72.6 4.9 %collective-permute-done.10.theirs = bf16[288,512]{1,0:T(8,128)(2,1)S(1)} collective-permute-done((bf16[288,512]{1,0:T(8,128)(2,1)S(1)}, bf16[288,512]{1,0:T(8,128)(2,1)S(1)}, u32[]{:S(2)}, u32[]{:S(2)}) %collective-permute-start.10) | collective-permute-done | bytes 294944 | tf_op jit(solution)/shard_map/ppermute | solution.py:345
  77.5 3.9 %shard_map.225 = (f32[144,1024]{1,0:T(8,128)S(1)}, bf16[144,1024]{1,0:T(8,128)(2,1)S(1)}, bf16[144,1024]{1,0:T(8,128)(2,1)S(1)}) custom-call(s32[1]{0:T(128)} %bitcast.9.me, bf16[288,1024]{1,0:T(8,128)(2,1)S(1)} %get-tuple-element.69.x, bf16[288,512]{1,0:T(8,128)(2,1)S(1)} %get-tuple-element.70.mine, bf16[288,512]{1,0:T(8,128)(2,1)S(1)} %collective-permute-done.10.theirs, ...), custom_call_target="tpu_custom_call" | custom-call | flops 100000000 | bytes 11665412 | tf_op jit(solution)/shard_map/pallas_call | solution.py:149
  81.4 0.1 collective-permute-start.11
  81.5 0.0 copy-start.5
  81.5 1.3 %collective-permute-done.13.theirs = bf16[288,512]{1,0:T(8,128)(2,1)S(1)} collective-permute-done((bf16[288,512]{1,0:T(8,128)(2,1)S(1)}, bf16[288,512]{1,0:T(8,128)(2,1)S(1)}, u32[]{:S(2)}, u32[]{:S(2)}) %collective-permute-start.13) | collective-permute-done | bytes 294944 | tf_op jit(solution)/shard_map/ppermute | solution.py:345
  82.8 3.9 %shard_map.228 = (f32[144,1024]{1,0:T(8,128)S(1)}, bf16[144,1024]{1,0:T(8,128)(2,1)S(1)}, bf16[144,1024]{1,0:T(8,128)(2,1)S(1)}) custom-call(s32[1]{0:T(128)} %bitcast.9.me, bf16[288,1024]{1,0:T(8,128)(2,1)S(1)} %get-tuple-element.77.x, bf16[288,512]{1,0:T(8,128)(2,1)S(1)} %get-tuple-element.78.mine, bf16[288,512]{1,0:T(8,128)(2,1)S(1)} %collective-permute-done.13.theirs, ...), custom_call_target="tpu_custom_call" | custom-call | flops 100000000 | bytes 11665412 | tf_op jit(solution)/shard_map/pallas_call | solution.py:149
  86.7 2.2 %collective-permute-start.14 = (bf16[144,1024]{1,0:T(8,128)(2,1)S(1)}, bf16[144,1024]{1,0:T(8,128)(2,1)S(1)}, u32[]{:S(2)}, u32[]{:S(2)}) collective-permute-start(bf16[144,1024]{1,0:T(8,128)(2,1)S(1)} %get-tuple-element.80), channel_id=1, source_target_pairs={{0,1},{1,0},{2,3},{3,2},{4,5},{5,4},{6,7},{7,6},{8,9},{9,8},{10,11... | collective-permute-start | bytes 884744 | tf_op jit(solution)/shard_map/ppermute | solution.py:345
  89.0 1.1 %collective-permute-done.11.r = bf16[144,1024]{1,0:T(8,128)(2,1)S(1)} collective-permute-done((bf16[144,1024]{1,0:T(8,128)(2,1)S(1)}, bf16[144,1024]{1,0:T(8,128)(2,1)S(1)}, u32[]{:S(2)}, u32[]{:S(2)}) %collective-permute-start.11) | collective-permute-done | bytes 294944 | tf_op jit(solution)/shard_map/ppermute | solution.py:345
  90.1 0.5 shard_map.226.first
  90.5 5.8 %collective-permute-done.14.r = bf16[144,1024]{1,0:T(8,128)(2,1)S(1)} collective-permute-done((bf16[144,1024]{1,0:T(8,128)(2,1)S(1)}, bf16[144,1024]{1,0:T(8,128)(2,1)S(1)}, u32[]{:S(2)}, u32[]{:S(2)}) %collective-permute-start.14) | collective-permute-done | bytes 294944 | tf_op jit(solution)/shard_map/ppermute | solution.py:345
  96.4 1.3 %shard_map.229 = bf16[12,6,4,1024]{3,2,1,0:T(4,128)(2,1)} custom-call(bf16[6,6,4,1024]{3,2,1,0:T(4,128)(2,1)S(1)} %shard_map.226.first, f32[144,1024]{1,0:T(8,128)S(1)} %get-tuple-element.79.k, bf16[144,1024]{1,0:T(8,128)(2,1)S(1)} %collective-permute-done.14.r, bf16[144,1024]{1,0:T(8,128)(2,1)S(1)} %get-tuple-element.81.h, bf16[144,144]{1,0:T(8,128)(2,1)S(1)} %copy-done.5), custom_call_target="tpu_custom_call" | custom-call | flops 100000000 | bytes 1516032 | tf_op jit(solution)/shard_map/pallas_call | solution.py:149
  (42 shorter events, 0.1 us)
Async XLA Ops:
  0.6 8.5 %copy-start.19 = (bf16[8,512]{1,0:T(8,128)(2,1)S(1)}, bf16[8,512]{1,0:T(8,128)(2,1)}, u32[]{:S(2)}) copy-start(bf16[8,512]{1,0:T(8,128)(2,1)} %constant.30.clone.spread) | copy-start | bytes 24580
  0.6 8.5 %copy-start.4 = (bf16[512,1024]{1,0:T(8,128)(2,1)S(1)}, bf16[512,1024]{1,0:T(8,128)(2,1)}, u32[]{:S(2)}) copy-start(bf16[512,1024]{1,0:T(8,128)(2,1)} %o_mine.3) | copy-start | bytes 3145732
  0.7 1.4 %copy-start.10 = (bf16[4,24,12,512]{3,1,2,0:T(8,128)(2,1)S(1)}, bf16[4,24,12,512]{3,1,2,0:T(8,128)(2,1)}, u32[]{:S(2)}) copy-start(bf16[4,24,12,512]{3,1,2,0:T(8,128)(2,1)} %param.21) | copy-start | bytes 3538948
  2.0 7.1 %copy-start.12 = (s32[4,24,12]{1,0,2:T(4,128)S(1)}, s32[4,24,12]{1,0,2:T(4,128)}, u32[]{:S(2)}) copy-start(s32[4,24,12]{1,0,2:T(4,128)} %param.22) | copy-start | bytes 13828
  2.0 7.1 %copy-start.13 = (bf16[8]{0:T(256)(128)(2,1)S(1)}, bf16[8]{0:T(256)(128)(2,1)}, u32[]{:S(2)}) copy-start(bf16[8]{0:T(256)(128)(2,1)} %param.27) | copy-start | bytes 52
  2.0 7.1 %copy-start.14 = (bf16[8]{0:T(256)(128)(2,1)S(1)}, bf16[8]{0:T(256)(128)(2,1)}, u32[]{:S(2)}) copy-start(bf16[8]{0:T(256)(128)(2,1)} %param.33) | copy-start | bytes 52
  2.0 7.1 %copy-start.16 = (bf16[1152,48]{1,0:T(8,128)(2,1)S(1)}, bf16[1152,48]{1,0:T(8,128)(2,1)}, u32[]{:S(2)}) copy-start(bf16[1152,48]{1,0:T(8,128)(2,1)} %constant.31.clone.rows) | copy-start | bytes 331780
  2.0 7.1 %copy-start.17 = (bf16[1152,25]{1,0:T(8,128)(2,1)S(1)}, bf16[1152,25]{1,0:T(8,128)(2,1)}, u32[]{:S(2)}) copy-start(bf16[1152,25]{1,0:T(8,128)(2,1)} %constant.32.clone.keep) | copy-start | bytes 172804
  2.5 19.2 %collective-permute-start = (bf16[576,512]{1,0:T(8,128)(2,1)S(1)}, bf16[576,512]{1,0:T(8,128)(2,1)S(1)}, u32[]{:S(2)}, u32[]{:S(2)}) collective-permute-start(bf16[576,512]{1,0:T(8,128)(2,1)S(1)} %get-tuple-element.43), channel_id=1, source_target_pairs={{0,15},{1,0},{2,1},{3,2},{4,3},{5,4},{6,5},{7,6},{8,7},{9,8},{10,9... | collective-permute-start | bytes 1769480 | tf_op jit(solution)/shard_map/ppermute | solution.py:345
  9.2 17.1 %copy-start.9 = (bf16[512,3,512]{2,0,1:T(8,128)(2,1)S(1)}, bf16[512,3,512]{2,0,1:T(8,128)(2,1)}, u32[]{:S(2)}) copy-start(bf16[512,3,512]{2,0,1:T(8,128)(2,1)} %param.23) | copy-start | bytes 4718596
  9.2 17.1 %copy-start.11 = (bf16[512,512]{1,0:T(8,128)(2,1)S(1)}, bf16[512,512]{1,0:T(8,128)(2,1)}, u32[]{:S(2)}) copy-start(bf16[512,512]{1,0:T(8,128)(2,1)} %out.3) | copy-start | bytes 1572868
  9.2 17.1 %copy-start.18 = (bf16[256,256]{1,0:T(8,128)(2,1)S(1)}, bf16[256,256]{1,0:T(8,128)(2,1)}, u32[]{:S(2)}) copy-start(bf16[256,256]{1,0:T(8,128)(2,1)} %constant.28.clone.ones) | copy-start | bytes 393220
  9.2 17.1 %copy-start.20 = (bf16[8,128]{1,0:T(8,128)(2,1)S(1)}, bf16[8,128]{1,0:T(8,128)(2,1)}, u32[]{:S(2)}) copy-start(bf16[8,128]{1,0:T(8,128)(2,1)} %constant.29.clone.lanes) | copy-start | bytes 6148
  21.8 11.3 %collective-permute-start.2 = (bf16[216,512]{1,0:T(8,128)(2,1)S(1)}, bf16[216,512]{1,0:T(8,128)(2,1)S(1)}, u32[]{:S(2)}, u32[]{:S(2)}) collective-permute-start(bf16[216,512]{1,0:T(8,128)(2,1)S(1)} %get-tuple-element.46), channel_id=1, source_target_pairs={{0,16},{16,32},{32,48},{48,64},{64,80},{80,96},{96,112},{112,0},{1... | collective-permute-start | bytes 663560 | tf_op jit(solution)/shard_map/ppermute | solution.py:345
  21.8 11.3 %collective-permute-start.3 = (bf16[144,512]{1,0:T(8,128)(2,1)S(1)}, bf16[144,512]{1,0:T(8,128)(2,1)S(1)}, u32[]{:S(2)}, u32[]{:S(2)}) collective-permute-start(bf16[144,512]{1,0:T(8,128)(2,1)S(1)} %get-tuple-element.51), channel_id=1, source_target_pairs={{0,112},{16,0},{32,16},{48,32},{64,48},{80,64},{96,80},{112,96},{1... | collective-permute-start | bytes 442376 | tf_op jit(solution)/shard_map/ppermute | solution.py:345
  24.7 8.4 %collective-permute-start.4 = (bf16[128,1024]{1,0:T(8,128)(2,1)S(1)}, bf16[128,1024]{1,0:T(8,128)(2,1)S(1)}, u32[]{:S(2)}, u32[]{:S(2)}) collective-permute-start(bf16[128,1024]{1,0:T(8,128)(2,1)S(1)} %get-tuple-element.53), channel_id=1, source_target_pairs={{0,1},{1,0},{2,3},{3,2},{4,5},{5,4},{6,7},{7,6},{8,9},{9,8},{10,11... | collective-permute-start | bytes 786440 | tf_op jit(solution)/shard_map/ppermute | solution.py:345
  29.7 13.2 %collective-permute-start.1 = (bf16[288,512]{1,0:T(8,128)(2,1)S(1)}, bf16[288,512]{1,0:T(8,128)(2,1)S(1)}, u32[]{:S(2)}, u32[]{:S(2)}) collective-permute-start(bf16[288,512]{1,0:T(8,128)(2,1)S(1)} %get-tuple-element.49), channel_id=1, source_target_pairs={{0,1},{1,2},{2,3},{3,4},{4,5},{5,6},{6,7},{7,8},{8,9},{9,10},{10,1... | collective-permute-start | bytes 884744 | tf_op jit(solution)/shard_map/ppermute | solution.py:345
  33.1 6.7 %copy-start.7 = (bf16[512,2048]{1,0:T(8,128)(2,1)S(1)}, bf16[512,2048]{1,0:T(8,128)(2,1)}, u32[]{:S(2)}) copy-start(bf16[512,2048]{1,0:T(8,128)(2,1)} %expand.7) | copy-start | bytes 6291460
  33.1 6.7 %copy-start.8 = (bf16[2048,512]{1,0:T(8,128)(2,1)S(1)}, bf16[2048,512]{1,0:T(8,128)(2,1)}, u32[]{:S(2)}) copy-start(bf16[2048,512]{1,0:T(8,128)(2,1)} %shrink.7) | copy-start | bytes 6291460
  37.5 12.9 %collective-permute-start.5 = (bf16[288,512]{1,0:T(8,128)(2,1)S(1)}, bf16[288,512]{1,0:T(8,128)(2,1)S(1)}, u32[]{:S(2)}, u32[]{:S(2)}) collective-permute-start(bf16[288,512]{1,0:T(8,128)(2,1)S(1)} %get-tuple-element.58), channel_id=1, source_target_pairs={{0,1},{1,2},{2,3},{3,4},{4,5},{5,6},{6,7},{7,8},{8,9},{9,10},{10,1... | collective-permute-start | bytes 884744 | tf_op jit(solution)/shard_map/ppermute | solution.py:345
  44.6 7.5 %copy-start.2 = (bf16[2048,1024]{1,0:T(8,128)(2,1)S(1)}, bf16[2048,1024]{1,0:T(8,128)(2,1)}, u32[]{:S(2)}) copy-start(bf16[2048,1024]{1,0:T(8,128)(2,1)} %weight.3) | copy-start | bytes 12582916
  44.6 7.5 %copy-start.3 = (bf16[2,576,864]{2,1,0:T(8,128)(2,1)S(1)}, bf16[2,576,864]{2,1,0:T(8,128)(2,1)}, u32[]{:S(2)}) copy-start(bf16[2,576,864]{2,1,0:T(8,128)(2,1)} %constant.33.clone.pm) | copy-start | bytes 5971972
  44.6 16.8 %collective-permute-start.6 = (bf16[128,1024]{1,0:T(8,128)(2,1)S(1)}, bf16[128,1024]{1,0:T(8,128)(2,1)S(1)}, u32[]{:S(2)}, u32[]{:S(2)}) collective-permute-start(bf16[128,1024]{1,0:T(8,128)(2,1)S(1)} %collective-permute-done.4.a), channel_id=1, source_target_pairs={{0,16},{16,0},{32,48},{48,32},{64,80},{80,64},{96,112},{112,96},{1... | collective-permute-start | bytes 786440 | tf_op jit(solution)/shard_map/ppermute | solution.py:353
  44.7 9.3 %collective-permute-start.7 = (bf16[128,1024]{1,0:T(8,128)(2,1)S(1)}, bf16[128,1024]{1,0:T(8,128)(2,1)S(1)}, u32[]{:S(2)}, u32[]{:S(2)}) collective-permute-start(bf16[128,1024]{1,0:T(8,128)(2,1)S(1)} %collective-permute-done.4.a), channel_id=1, source_target_pairs={{0,32},{16,48},{32,0},{48,16},{64,96},{80,112},{96,64},{112,80},{1... | collective-permute-start | bytes 786440 | tf_op jit(solution)/shard_map/ppermute | solution.py:353
  53.9 5.5 %copy-start.15 = (bf16[576,576]{1,0:T(8,128)(2,1)S(1)}, bf16[576,576]{1,0:T(8,128)(2,1)}, u32[]{:S(2)}) copy-start(bf16[576,576]{1,0:T(8,128)(2,1)} %constant.34.clone.perm) | copy-start | bytes 1990660
  53.9 9.7 %collective-permute-start.9 = (bf16[144,1024]{1,0:T(8,128)(2,1)S(1)}, bf16[144,1024]{1,0:T(8,128)(2,1)S(1)}, u32[]{:S(2)}, u32[]{:S(2)}) collective-permute-start(bf16[144,1024]{1,0:T(8,128)(2,1)S(1)} %shard_map.220.own), channel_id=1, source_target_pairs={{0,1},{1,0},{2,3},{3,2},{4,5},{5,4},{6,7},{7,6},{8,9},{9,8},{10,11... | collective-permute-start | bytes 884744 | tf_op jit(solution)/shard_map/ppermute | solution.py:345
  54.0 7.5 %collective-permute-start.8 = (bf16[128,1024]{1,0:T(8,128)(2,1)S(1)}, bf16[128,1024]{1,0:T(8,128)(2,1)S(1)}, u32[]{:S(2)}, u32[]{:S(2)}) collective-permute-start(bf16[128,1024]{1,0:T(8,128)(2,1)S(1)} %collective-permute-done.7.c), channel_id=1, source_target_pairs={{0,16},{16,0},{32,48},{48,32},{64,80},{80,64},{96,112},{112,96},{1... | collective-permute-start | bytes 786440 | tf_op jit(solution)/shard_map/ppermute | solution.py:353
  55.9 12.7 %collective-permute-start.12 = (bf16[144,1024]{1,0:T(8,128)(2,1)S(1)}, bf16[144,1024]{1,0:T(8,128)(2,1)S(1)}, u32[]{:S(2)}, u32[]{:S(2)}) collective-permute-start(bf16[144,1024]{1,0:T(8,128)(2,1)S(1)} %shard_map.221.own), channel_id=1, source_target_pairs={{0,1},{1,0},{2,3},{3,2},{4,5},{5,4},{6,7},{7,6},{8,9},{9,8},{10,11... | collective-permute-start | bytes 884744 | tf_op jit(solution)/shard_map/ppermute | solution.py:345
  61.5 2.1 %copy-start.6 = (bf16[512,3,1024]{2,0,1:T(8,128)(2,1)S(1)}, bf16[512,3,1024]{2,0,1:T(8,128)(2,1)}, u32[]{:S(2)}) copy-start(bf16[512,3,1024]{2,0,1:T(8,128)(2,1)} %param.29) | copy-start | bytes 9437188
  63.6 13.9 %copy-start.1 = (bf16[2048,1024]{1,0:T(8,128)(2,1)S(1)}, bf16[2048,1024]{1,0:T(8,128)(2,1)}, u32[]{:S(2)}) copy-start(bf16[2048,1024]{1,0:T(8,128)(2,1)} %shrink.9) | copy-start | bytes 12582916
  65.8 11.7 %copy-start = (bf16[2048,1024]{1,0:T(8,128)(2,1)S(1)}, bf16[2048,1024]{1,0:T(8,128)(2,1)}, u32[]{:S(2)}) copy-start(bf16[2048,1024]{1,0:T(8,128)(2,1)} %expand.9) | copy-start | bytes 12582916
  65.8 11.7 %collective-permute-start.10 = (bf16[288,512]{1,0:T(8,128)(2,1)S(1)}, bf16[288,512]{1,0:T(8,128)(2,1)S(1)}, u32[]{:S(2)}, u32[]{:S(2)}) collective-permute-start(bf16[288,512]{1,0:T(8,128)(2,1)S(1)} %get-tuple-element.70.mine), channel_id=1, source_target_pairs={{0,1},{1,0},{2,3},{3,2},{4,5},{5,4},{6,7},{7,6},{8,9},{9,8},{10,11... | collective-permute-start | bytes 884744 | tf_op jit(solution)/shard_map/ppermute | solution.py:345
  70.7 12.1 %collective-permute-start.13 = (bf16[288,512]{1,0:T(8,128)(2,1)S(1)}, bf16[288,512]{1,0:T(8,128)(2,1)S(1)}, u32[]{:S(2)}, u32[]{:S(2)}) collective-permute-start(bf16[288,512]{1,0:T(8,128)(2,1)S(1)} %get-tuple-element.78.mine), channel_id=1, source_target_pairs={{0,1},{1,0},{2,3},{3,2},{4,5},{5,4},{6,7},{7,6},{8,9},{9,8},{10,11... | collective-permute-start | bytes 884744 | tf_op jit(solution)/shard_map/ppermute | solution.py:345
  81.4 8.7 %collective-permute-start.11 = (bf16[144,1024]{1,0:T(8,128)(2,1)S(1)}, bf16[144,1024]{1,0:T(8,128)(2,1)S(1)}, u32[]{:S(2)}, u32[]{:S(2)}) collective-permute-start(bf16[144,1024]{1,0:T(8,128)(2,1)S(1)} %get-tuple-element.73), channel_id=1, source_target_pairs={{0,1},{1,0},{2,3},{3,2},{4,5},{5,4},{6,7},{7,6},{8,9},{9,8},{10,11... | collective-permute-start | bytes 884744 | tf_op jit(solution)/shard_map/ppermute | solution.py:345
  81.5 8.6 %copy-start.5 = (bf16[144,144]{1,0:T(8,128)(2,1)S(1)}, bf16[144,144]{1,0:T(8,128)(2,1)}, u32[]{:S(2)}) copy-start(bf16[144,144]{1,0:T(8,128)(2,1)} %constant.35.clone.pout) | copy-start | bytes 124420
  86.7 9.6 %collective-permute-start.14 = (bf16[144,1024]{1,0:T(8,128)(2,1)S(1)}, bf16[144,1024]{1,0:T(8,128)(2,1)S(1)}, u32[]{:S(2)}, u32[]{:S(2)}) collective-permute-start(bf16[144,1024]{1,0:T(8,128)(2,1)S(1)} %get-tuple-element.80), channel_id=1, source_target_pairs={{0,1},{1,0},{2,3},{3,2},{4,5},{5,4},{6,7},{7,6},{8,9},{9,8},{10,11... | collective-permute-start | bytes 884744 | tf_op jit(solution)/shard_map/ppermute | solution.py:345

commit v4 on v3

--- a/solution.py
+++ b/solution.py
@@ -104,8 +104,9 @@
 
 
 def gelu(x):
-    inner = x * (0.7978845608028654 + 0.035677408136300125 * (x * x))
-    return (0.5 * x) * (1.0 + jnp.tanh(inner))
+    x = x.astype(BF)
+    inner = x * (jnp.asarray(0.7978845608, BF) + jnp.asarray(0.0356774081, BF) * (x * x))
+    return (x * jnp.asarray(0.5, BF)) * (jnp.asarray(1.0, BF) + jnp.tanh(inner))
 
 
 def unit(packed, ones, factor=None):

time: 97.8 us -> 97.5 us (level)
  Pallas kernels: 34.8 us -> 33.8 us
    pallas_call x18, Pallas kernels: 34.8 us -> 33.8 us  [call(): pl.pallas_call(kernel, out_shape=[jax.ShapeDtypeStruct(shape, kind) for s...]
  transfers between devices with their start and end apart: 15 -> 15, of which waited for: 9 -> 9; matrix products, arithmetic and copies ran while one was open for 0% -> 0% of each run, Pallas kernels for 34% -> 33%
where the time goes in v4:
time: 97.5 us; the launch traced here: 97.3 us
  waiting for transfers between devices  36 us (37%)
  Pallas kernels  33.8 us (35%)
  starting transfers between devices  25.1 us (26%)
  local copies, waits for them, and re-layouts  1.46 us (1%)
  between operations  0.99 us (1%)
    ppermute x12, waiting for transfers between devices, behind(): lax.ppermute(value, axis, [(s, (s + steps) % count) for s in range(count)])  36 us
    pallas_call x18, Pallas kernels, call(): pl.pallas_call(kernel, out_shape=[jax.ShapeDtypeStruct(shape, kind) for s...  33.8 us
    ppermute x12, starting transfers between devices, behind(): lax.ppermute(value, axis, [(s, (s + steps) % count) for s in range(count)])  23.3 us
  transfers between devices with their start and end apart: 15, of which 9 were waited for; matrix products, arithmetic and copies ran while one was open for 0% of the time, Pallas kernels for 33%

profile of v4, /device:TPU:0, one launch (start us, length us, event | category | flops | bytes accessed | tf_op | source)
XLA Modules:
  0.0 97.3 jit_solution(15909635150686064952)
XLA Ops:
  0.6 0.0 copy-start.19
  0.7 1.4 %copy-done.10 = bf16[4,24,12,512]{3,1,2,0:T(8,128)(2,1)S(1)} copy-done((bf16[4,24,12,512]{3,1,2,0:T(8,128)(2,1)S(1)}, bf16[4,24,12,512]{3,1,2,0:T(8,128)(2,1)}, u32[]{:S(2)}) %copy-start.10) | copy-done | bytes 1179672
  2.0 0.0 copy-start.17
  2.0 0.5 shard_map.212
  2.5 6.6 %collective-permute-start = (bf16[576,512]{1,0:T(8,128)(2,1)S(1)}, bf16[576,512]{1,0:T(8,128)(2,1)S(1)}, u32[]{:S(2)}, u32[]{:S(2)}) collective-permute-start(bf16[576,512]{1,0:T(8,128)(2,1)S(1)} %get-tuple-element.43), channel_id=1, source_target_pairs={{0,15},{1,0},{2,1},{3,2},{4,3},{5,4},{6,5},{7,6},{8,7},{9,8},{10,9... | collective-permute-start | bytes 1769480 | tf_op jit(solution)/shard_map/ppermute | solution.py:346
  9.2 0.0 copy-start.18
  9.2 0.0 copy-start.20
  9.2 0.4 shard_map.213
  9.6 12.1 %collective-permute-done.left_all.left = bf16[576,512]{1,0:T(8,128)(2,1)S(1)} collective-permute-done((bf16[576,512]{1,0:T(8,128)(2,1)S(1)}, bf16[576,512]{1,0:T(8,128)(2,1)S(1)}, u32[]{:S(2)}, u32[]{:S(2)}) %collective-permute-start) | collective-permute-done | bytes 589856 | tf_op jit(solution)/shard_map/ppermute | solution.py:346
  21.8 0.0 collective-permute-start.2
  21.8 2.9 %collective-permute-start.3 = (bf16[144,512]{1,0:T(8,128)(2,1)S(1)}, bf16[144,512]{1,0:T(8,128)(2,1)S(1)}, u32[]{:S(2)}, u32[]{:S(2)}) collective-permute-start(bf16[144,512]{1,0:T(8,128)(2,1)S(1)} %get-tuple-element.51), channel_id=1, source_target_pairs={{0,112},{16,0},{32,16},{48,32},{64,48},{80,64},{96,80},{112,96},{1... | collective-permute-start | bytes 442376 | tf_op jit(solution)/shard_map/ppermute | solution.py:346
  24.7 1.6 %collective-permute-start.4 = (bf16[128,1024]{1,0:T(8,128)(2,1)S(1)}, bf16[128,1024]{1,0:T(8,128)(2,1)S(1)}, u32[]{:S(2)}, u32[]{:S(2)}) collective-permute-start(bf16[128,1024]{1,0:T(8,128)(2,1)S(1)} %get-tuple-element.53), channel_id=1, source_target_pairs={{0,1},{1,0},{2,3},{3,2},{4,5},{5,4},{6,7},{7,6},{8,9},{9,8},{10,11... | collective-permute-start | bytes 786440 | tf_op jit(solution)/shard_map/ppermute | solution.py:346
  26.3 3.4 %shard_map.215 = (bf16[288,512]{1,0:T(8,128)(2,1)S(1)}, bf16[288,512]{1,0:T(8,128)(2,1)S(1)}) custom-call(bf16[576,512]{1,0:T(8,128)(2,1)S(1)} %get-tuple-element.42.right_all.right, bf16[576,512]{1,0:T(8,128)(2,1)S(1)} %collective-permute-done.left_all.left, bf16[1152,128]{1,0:T(8,128)(2,1)S(1)} %get-tuple-element.54.classes, ...), custom_call_target="tpu_custom_call" | custom-call | flops 4000000000 | bytes 3706880 | tf_op jit(solution)/shard_map/pallas_call | solution.py:150
  29.7 2.0 %collective-permute-start.1 = (bf16[288,512]{1,0:T(8,128)(2,1)S(1)}, bf16[288,512]{1,0:T(8,128)(2,1)S(1)}, u32[]{:S(2)}, u32[]{:S(2)}) collective-permute-start(bf16[288,512]{1,0:T(8,128)(2,1)S(1)} %get-tuple-element.49), channel_id=1, source_target_pairs={{0,1},{1,2},{2,3},{3,4},{4,5},{5,6},{6,7},{7,8},{8,9},{9,10},{10,1... | collective-permute-start | bytes 884744 | tf_op jit(solution)/shard_map/ppermute | solution.py:346
  31.7 1.4 %collective-permute-done.4.a = bf16[128,1024]{1,0:T(8,128)(2,1)S(1)} collective-permute-done((bf16[128,1024]{1,0:T(8,128)(2,1)S(1)}, bf16[128,1024]{1,0:T(8,128)(2,1)S(1)}, u32[]{:S(2)}, u32[]{:S(2)}) %collective-permute-start.4) | collective-permute-done | bytes 262176 | tf_op jit(solution)/shard_map/ppermute | solution.py:346
  33.1 4.4 %shard_map.216 = (bf16[288,512]{1,0:T(8,128)(2,1)S(1)}, bf16[288,512]{1,0:T(8,128)(2,1)S(1)}) custom-call(bf16[576,512]{1,0:T(8,128)(2,1)S(1)} %get-tuple-element.42.right_all.right, bf16[576,512]{1,0:T(8,128)(2,1)S(1)} %collective-permute-done.left_all.left, bf16[216,512]{1,0:T(8,128)(2,1)S(1)} %collective-permute-done.2.down, ...), custom_call_target="tpu_custom_call" | custom-call | flops 6000000000 | bytes 4075520 | tf_op jit(solution)/shard_map/pallas_call | solution.py:150
  37.5 2.3 %collective-permute-start.5 = (bf16[288,512]{1,0:T(8,128)(2,1)S(1)}, bf16[288,512]{1,0:T(8,128)(2,1)S(1)}, u32[]{:S(2)}, u32[]{:S(2)}) collective-permute-start(bf16[288,512]{1,0:T(8,128)(2,1)S(1)} %get-tuple-element.58), channel_id=1, source_target_pairs={{0,1},{1,2},{2,3},{3,4},{4,5},{5,6},{6,7},{7,8},{8,9},{9,10},{10,1... | collective-permute-start | bytes 884744 | tf_op jit(solution)/shard_map/ppermute | solution.py:346
  39.8 2.8 %shard_map.217 = (bf16[288,512]{1,0:T(8,128)(2,1)S(1)}, bf16[288,512]{1,0:T(8,128)(2,1)S(1)}) custom-call(bf16[288,512]{1,0:T(8,128)(2,1)S(1)} %get-tuple-element.50.h1, bf16[288,512]{1,0:T(8,128)(2,1)S(1)} %get-tuple-element.55.h2, bf16[512,2048]{1,0:T(8,128)(2,1)S(1)} %copy-done.7, bf16[2048,512]{1,0:T(8,128)(2,1)S(1)} %copy-done.8), custom_call_target="tpu_custom_call" | custom-call | flops 3000000000 | bytes 4784128 | tf_op jit(solution)/shard_map/pallas_call | solution.py:150
  42.6 1.6 %shard_map.218.l1 = bf16[288,512]{1,0:T(8,128)(2,1)S(1)} custom-call(bf16[288,512]{1,0:T(8,128)(2,1)S(1)} %collective-permute-done.1.h, bf16[512,2048]{1,0:T(8,128)(2,1)S(1)} %copy-done.7, bf16[2048,512]{1,0:T(8,128)(2,1)S(1)} %copy-done.8), custom_call_target="tpu_custom_call" | custom-call | flops 2000000000 | bytes 4489216 | tf_op jit(solution)/shard_map/pallas_call | solution.py:150
  44.2 0.0 copy-start.3
  44.2 0.1 collective-permute-start.6
  44.3 1.6 %collective-permute-start.7 = (bf16[128,1024]{1,0:T(8,128)(2,1)S(1)}, bf16[128,1024]{1,0:T(8,128)(2,1)S(1)}, u32[]{:S(2)}, u32[]{:S(2)}) collective-permute-start(bf16[128,1024]{1,0:T(8,128)(2,1)S(1)} %collective-permute-done.4.a), channel_id=1, source_target_pairs={{0,32},{16,48},{32,0},{48,16},{64,96},{80,112},{96,64},{112,80},{1... | collective-permute-start | bytes 786440 | tf_op jit(solution)/shard_map/ppermute | solution.py:354
  45.9 4.5 %collective-permute-done.5.h = bf16[288,512]{1,0:T(8,128)(2,1)S(1)} collective-permute-done((bf16[288,512]{1,0:T(8,128)(2,1)S(1)}, bf16[288,512]{1,0:T(8,128)(2,1)S(1)}, u32[]{:S(2)}, u32[]{:S(2)}) %collective-permute-start.5) | collective-permute-done | bytes 294944 | tf_op jit(solution)/shard_map/ppermute | solution.py:346
  50.4 1.6 %shard_map.219.l2 = bf16[288,512]{1,0:T(8,128)(2,1)S(1)} custom-call(bf16[288,512]{1,0:T(8,128)(2,1)S(1)} %collective-permute-done.5.h, bf16[512,2048]{1,0:T(8,128)(2,1)S(1)} %copy-done.7, bf16[2048,512]{1,0:T(8,128)(2,1)S(1)} %copy-done.8), custom_call_target="tpu_custom_call" | custom-call | flops 2000000000 | bytes 4489216 | tf_op jit(solution)/shard_map/pallas_call | solution.py:150
  52.0 1.8 %shard_map.220.own = bf16[144,1024]{1,0:T(8,128)(2,1)S(1)} custom-call(bf16[288,512]{1,0:T(8,128)(2,1)S(1)} %shard_map.218.l1, bf16[288,512]{1,0:T(8,128)(2,1)S(1)} %shard_map.219.l2, bf16[288,512]{1,0:T(8,128)(2,1)S(1)} %get-tuple-element.56.r1, bf16[288,512]{1,0:T(8,128)(2,1)S(1)} %get-tuple-element.60.r2, bf16[2,576,864]{2,1,0:T(8,128)(2,1)S(1)} %copy-done.3, ...), custom_call_target="tpu_custom_call" | custom-call | flops 1000000000 | bytes 7364608 | tf_op jit(solution)/shard_map/pallas_call | solution.py:150
  53.7 0.0 copy-start.15
  53.7 0.1 collective-permute-start.9
  53.9 0.1 collective-permute-start.8
  53.9 1.8 %shard_map.221.own = bf16[144,1024]{1,0:T(8,128)(2,1)S(1)} custom-call(bf16[288,512]{1,0:T(8,128)(2,1)S(1)} %shard_map.218.l1, bf16[288,512]{1,0:T(8,128)(2,1)S(1)} %shard_map.219.l2, bf16[288,512]{1,0:T(8,128)(2,1)S(1)} %get-tuple-element.56.r1, bf16[288,512]{1,0:T(8,128)(2,1)S(1)} %get-tuple-element.60.r2, bf16[2,576,864]{2,1,0:T(8,128)(2,1)S(1)} %copy-done.3, ...), custom_call_target="tpu_custom_call" | custom-call | flops 1000000000 | bytes 7364608 | tf_op jit(solution)/shard_map/pallas_call | solution.py:150
  55.7 3.5 %collective-permute-start.12 = (bf16[144,1024]{1,0:T(8,128)(2,1)S(1)}, bf16[144,1024]{1,0:T(8,128)(2,1)S(1)}, u32[]{:S(2)}, u32[]{:S(2)}) collective-permute-start(bf16[144,1024]{1,0:T(8,128)(2,1)S(1)} %shard_map.221.own), channel_id=1, source_target_pairs={{0,1},{1,0},{2,3},{3,2},{4,5},{5,4},{6,7},{7,6},{8,9},{9,8},{10,11... | collective-permute-start | bytes 884744 | tf_op jit(solution)/shard_map/ppermute | solution.py:346
  59.2 2.1 %shard_map.222 = bf16[1152,512]{1,0:T(8,128)(2,1)} custom-call(bf16[288,512]{1,0:T(8,128)(2,1)S(1)} %shard_map.218.l1, bf16[288,512]{1,0:T(8,128)(2,1)S(1)} %shard_map.219.l2, bf16[288,512]{1,0:T(8,128)(2,1)S(1)} %get-tuple-element.56.r1, bf16[288,512]{1,0:T(8,128)(2,1)S(1)} %get-tuple-element.60.r2, bf16[576,576]{1,0:T(8,128)(2,1)S(1)} %copy-done.15), custom_call_target="tpu_custom_call" | custom-call | flops 2000000000 | bytes 1843200 | tf_op jit(solution)/shard_map/pallas_call | solution.py:150
  61.3 0.1 shard_map.223.o_theirs
  61.4 2.0 %collective-permute-done.9.other = bf16[144,1024]{1,0:T(8,128)(2,1)S(1)} collective-permute-done((bf16[144,1024]{1,0:T(8,128)(2,1)S(1)}, bf16[144,1024]{1,0:T(8,128)(2,1)S(1)}, u32[]{:S(2)}, u32[]{:S(2)}) %collective-permute-start.9) | collective-permute-done | bytes 294944 | tf_op jit(solution)/shard_map/ppermute | solution.py:346
  63.5 2.2 %shard_map.224 = (bf16[288,1024]{1,0:T(8,128)(2,1)S(1)}, bf16[288,512]{1,0:T(8,128)(2,1)S(1)}) custom-call(s32[1]{0:T(128)} %bitcast.9.me, bf16[144,1024]{1,0:T(8,128)(2,1)S(1)} %shard_map.220.own, bf16[144,1024]{1,0:T(8,128)(2,1)S(1)} %collective-permute-done.9.other, bf16[3,512,1024]{2,1,0:T(8,128)(2,1)S(1)} %bitcast.14, bf16[256,256]{1,0:T(8,128)(2,1)S(1)} %copy-done.18, ...), custom_call_target="tpu_custom_call" | custom-call | flops 2000000000 | bytes 3870724 | tf_op jit(solution)/shard_map/pallas_call | solution.py:150
  65.7 0.3 collective-permute-start.10
  66.0 2.4 %collective-permute-done.12.other = bf16[144,1024]{1,0:T(8,128)(2,1)S(1)} collective-permute-done((bf16[144,1024]{1,0:T(8,128)(2,1)S(1)}, bf16[144,1024]{1,0:T(8,128)(2,1)S(1)}, u32[]{:S(2)}, u32[]{:S(2)}) %collective-permute-start.12) | collective-permute-done | bytes 294944 | tf_op jit(solution)/shard_map/ppermute | solution.py:346
  68.4 2.2 %shard_map.227 = (bf16[288,1024]{1,0:T(8,128)(2,1)S(1)}, bf16[288,512]{1,0:T(8,128)(2,1)S(1)}) custom-call(s32[1]{0:T(128)} %bitcast.9.me, bf16[144,1024]{1,0:T(8,128)(2,1)S(1)} %shard_map.221.own, bf16[144,1024]{1,0:T(8,128)(2,1)S(1)} %collective-permute-done.12.other, bf16[3,512,1024]{2,1,0:T(8,128)(2,1)S(1)} %bitcast.15, bf16[256,256]{1,0:T(8,128)(2,1)S(1)} %copy-done.18, ...), custom_call_target="tpu_custom_call" | custom-call | flops 2000000000 | bytes 3870724 | tf_op jit(solution)/shard_map/pallas_call | solution.py:150
  70.6 1.8 %collective-permute-start.13 = (bf16[288,512]{1,0:T(8,128)(2,1)S(1)}, bf16[288,512]{1,0:T(8,128)(2,1)S(1)}, u32[]{:S(2)}, u32[]{:S(2)}) collective-permute-start(bf16[288,512]{1,0:T(8,128)(2,1)S(1)} %get-tuple-element.78.mine), channel_id=1, source_target_pairs={{0,1},{1,0},{2,3},{3,2},{4,5},{5,4},{6,7},{7,6},{8,9},{9,8},{10,11... | collective-permute-start | bytes 884744 | tf_op jit(solution)/shard_map/ppermute | solution.py:346
  72.4 4.9 %collective-permute-done.10.theirs = bf16[288,512]{1,0:T(8,128)(2,1)S(1)} collective-permute-done((bf16[288,512]{1,0:T(8,128)(2,1)S(1)}, bf16[288,512]{1,0:T(8,128)(2,1)S(1)}, u32[]{:S(2)}, u32[]{:S(2)}) %collective-permute-start.10) | collective-permute-done | bytes 294944 | tf_op jit(solution)/shard_map/ppermute | solution.py:346
  77.4 3.7 %shard_map.225 = (f32[144,1024]{1,0:T(8,128)S(1)}, bf16[144,1024]{1,0:T(8,128)(2,1)S(1)}, bf16[144,1024]{1,0:T(8,128)(2,1)S(1)}) custom-call(s32[1]{0:T(128)} %bitcast.9.me, bf16[288,1024]{1,0:T(8,128)(2,1)S(1)} %get-tuple-element.69.x, bf16[288,512]{1,0:T(8,128)(2,1)S(1)} %get-tuple-element.70.mine, bf16[288,512]{1,0:T(8,128)(2,1)S(1)} %collective-permute-done.10.theirs, ...), custom_call_target="tpu_custom_call" | custom-call | flops 100000000 | bytes 11665412 | tf_op jit(solution)/shard_map/pallas_call | solution.py:150
  81.1 0.1 collective-permute-start.11
  81.2 1.6 %collective-permute-done.13.theirs = bf16[288,512]{1,0:T(8,128)(2,1)S(1)} collective-permute-done((bf16[288,512]{1,0:T(8,128)(2,1)S(1)}, bf16[288,512]{1,0:T(8,128)(2,1)S(1)}, u32[]{:S(2)}, u32[]{:S(2)}) %collective-permute-start.13) | collective-permute-done | bytes 294944 | tf_op jit(solution)/shard_map/ppermute | solution.py:346
  82.7 3.7 %shard_map.228 = (f32[144,1024]{1,0:T(8,128)S(1)}, bf16[144,1024]{1,0:T(8,128)(2,1)S(1)}, bf16[144,1024]{1,0:T(8,128)(2,1)S(1)}) custom-call(s32[1]{0:T(128)} %bitcast.9.me, bf16[288,1024]{1,0:T(8,128)(2,1)S(1)} %get-tuple-element.77.x, bf16[288,512]{1,0:T(8,128)(2,1)S(1)} %get-tuple-element.78.mine, bf16[288,512]{1,0:T(8,128)(2,1)S(1)} %collective-permute-done.13.theirs, ...), custom_call_target="tpu_custom_call" | custom-call | flops 100000000 | bytes 11665412 | tf_op jit(solution)/shard_map/pallas_call | solution.py:150
  86.4 2.0 %collective-permute-start.14 = (bf16[144,1024]{1,0:T(8,128)(2,1)S(1)}, bf16[144,1024]{1,0:T(8,128)(2,1)S(1)}, u32[]{:S(2)}, u32[]{:S(2)}) collective-permute-start(bf16[144,1024]{1,0:T(8,128)(2,1)S(1)} %get-tuple-element.80), channel_id=1, source_target_pairs={{0,1},{1,0},{2,3},{3,2},{4,5},{5,4},{6,7},{7,6},{8,9},{9,8},{10,11... | collective-permute-start | bytes 884744 | tf_op jit(solution)/shard_map/ppermute | solution.py:346
  88.4 1.3 %collective-permute-done.11.r = bf16[144,1024]{1,0:T(8,128)(2,1)S(1)} collective-permute-done((bf16[144,1024]{1,0:T(8,128)(2,1)S(1)}, bf16[144,1024]{1,0:T(8,128)(2,1)S(1)}, u32[]{:S(2)}, u32[]{:S(2)}) %collective-permute-start.11) | collective-permute-done | bytes 294944 | tf_op jit(solution)/shard_map/ppermute | solution.py:346
  89.7 0.5 shard_map.226.first
  90.2 5.8 %collective-permute-done.14.r = bf16[144,1024]{1,0:T(8,128)(2,1)S(1)} collective-permute-done((bf16[144,1024]{1,0:T(8,128)(2,1)S(1)}, bf16[144,1024]{1,0:T(8,128)(2,1)S(1)}, u32[]{:S(2)}, u32[]{:S(2)}) %collective-permute-start.14) | collective-permute-done | bytes 294944 | tf_op jit(solution)/shard_map/ppermute | solution.py:346
  96.0 1.3 %shard_map.229 = bf16[12,6,4,1024]{3,2,1,0:T(4,128)(2,1)} custom-call(bf16[6,6,4,1024]{3,2,1,0:T(4,128)(2,1)S(1)} %shard_map.226.first, f32[144,1024]{1,0:T(8,128)S(1)} %get-tuple-element.79.k, bf16[144,1024]{1,0:T(8,128)(2,1)S(1)} %collective-permute-done.14.r, bf16[144,1024]{1,0:T(8,128)(2,1)S(1)} %get-tuple-element.81.h, bf16[144,144]{1,0:T(8,128)(2,1)S(1)} %copy-done.5), custom_call_target="tpu_custom_call" | custom-call | flops 100000000 | bytes 1516032 | tf_op jit(solution)/shard_map/pallas_call | solution.py:150
  (42 shorter events, 0.1 us)
Async XLA Ops:
  0.6 8.5 %copy-start.19 = (bf16[8,512]{1,0:T(8,128)(2,1)S(1)}, bf16[8,512]{1,0:T(8,128)(2,1)}, u32[]{:S(2)}) copy-start(bf16[8,512]{1,0:T(8,128)(2,1)} %constant.30.clone.spread) | copy-start | bytes 24580
  0.6 8.5 %copy-start.4 = (bf16[512,1024]{1,0:T(8,128)(2,1)S(1)}, bf16[512,1024]{1,0:T(8,128)(2,1)}, u32[]{:S(2)}) copy-start(bf16[512,1024]{1,0:T(8,128)(2,1)} %o_mine.3) | copy-start | bytes 3145732
  0.7 1.4 %copy-start.10 = (bf16[4,24,12,512]{3,1,2,0:T(8,128)(2,1)S(1)}, bf16[4,24,12,512]{3,1,2,0:T(8,128)(2,1)}, u32[]{:S(2)}) copy-start(bf16[4,24,12,512]{3,1,2,0:T(8,128)(2,1)} %param.21) | copy-start | bytes 3538948
  2.0 7.1 %copy-start.12 = (s32[4,24,12]{1,0,2:T(4,128)S(1)}, s32[4,24,12]{1,0,2:T(4,128)}, u32[]{:S(2)}) copy-start(s32[4,24,12]{1,0,2:T(4,128)} %param.22) | copy-start | bytes 13828
  2.0 7.1 %copy-start.13 = (bf16[8]{0:T(256)(128)(2,1)S(1)}, bf16[8]{0:T(256)(128)(2,1)}, u32[]{:S(2)}) copy-start(bf16[8]{0:T(256)(128)(2,1)} %param.27) | copy-start | bytes 52
  2.0 7.1 %copy-start.14 = (bf16[8]{0:T(256)(128)(2,1)S(1)}, bf16[8]{0:T(256)(128)(2,1)}, u32[]{:S(2)}) copy-start(bf16[8]{0:T(256)(128)(2,1)} %param.33) | copy-start | bytes 52
  2.0 7.1 %copy-start.16 = (bf16[1152,48]{1,0:T(8,128)(2,1)S(1)}, bf16[1152,48]{1,0:T(8,128)(2,1)}, u32[]{:S(2)}) copy-start(bf16[1152,48]{1,0:T(8,128)(2,1)} %constant.31.clone.rows) | copy-start | bytes 331780
  2.0 7.1 %copy-start.17 = (bf16[1152,25]{1,0:T(8,128)(2,1)S(1)}, bf16[1152,25]{1,0:T(8,128)(2,1)}, u32[]{:S(2)}) copy-start(bf16[1152,25]{1,0:T(8,128)(2,1)} %constant.32.clone.keep) | copy-start | bytes 172804
  2.5 19.2 %collective-permute-start = (bf16[576,512]{1,0:T(8,128)(2,1)S(1)}, bf16[576,512]{1,0:T(8,128)(2,1)S(1)}, u32[]{:S(2)}, u32[]{:S(2)}) collective-permute-start(bf16[576,512]{1,0:T(8,128)(2,1)S(1)} %get-tuple-element.43), channel_id=1, source_target_pairs={{0,15},{1,0},{2,1},{3,2},{4,3},{5,4},{6,5},{7,6},{8,7},{9,8},{10,9... | collective-permute-start | bytes 1769480 | tf_op jit(solution)/shard_map/ppermute | solution.py:346
  9.2 17.1 %copy-start.9 = (bf16[512,3,512]{2,0,1:T(8,128)(2,1)S(1)}, bf16[512,3,512]{2,0,1:T(8,128)(2,1)}, u32[]{:S(2)}) copy-start(bf16[512,3,512]{2,0,1:T(8,128)(2,1)} %param.23) | copy-start | bytes 4718596
  9.2 17.1 %copy-start.11 = (bf16[512,512]{1,0:T(8,128)(2,1)S(1)}, bf16[512,512]{1,0:T(8,128)(2,1)}, u32[]{:S(2)}) copy-start(bf16[512,512]{1,0:T(8,128)(2,1)} %out.3) | copy-start | bytes 1572868
  9.2 17.1 %copy-start.18 = (bf16[256,256]{1,0:T(8,128)(2,1)S(1)}, bf16[256,256]{1,0:T(8,128)(2,1)}, u32[]{:S(2)}) copy-start(bf16[256,256]{1,0:T(8,128)(2,1)} %constant.28.clone.ones) | copy-start | bytes 393220
  9.2 17.1 %copy-start.20 = (bf16[8,128]{1,0:T(8,128)(2,1)S(1)}, bf16[8,128]{1,0:T(8,128)(2,1)}, u32[]{:S(2)}) copy-start(bf16[8,128]{1,0:T(8,128)(2,1)} %constant.29.clone.lanes) | copy-start | bytes 6148
  21.8 11.3 %collective-permute-start.2 = (bf16[216,512]{1,0:T(8,128)(2,1)S(1)}, bf16[216,512]{1,0:T(8,128)(2,1)S(1)}, u32[]{:S(2)}, u32[]{:S(2)}) collective-permute-start(bf16[216,512]{1,0:T(8,128)(2,1)S(1)} %get-tuple-element.46), channel_id=1, source_target_pairs={{0,16},{16,32},{32,48},{48,64},{64,80},{80,96},{96,112},{112,0},{1... | collective-permute-start | bytes 663560 | tf_op jit(solution)/shard_map/ppermute | solution.py:346
  21.8 11.3 %collective-permute-start.3 = (bf16[144,512]{1,0:T(8,128)(2,1)S(1)}, bf16[144,512]{1,0:T(8,128)(2,1)S(1)}, u32[]{:S(2)}, u32[]{:S(2)}) collective-permute-start(bf16[144,512]{1,0:T(8,128)(2,1)S(1)} %get-tuple-element.51), channel_id=1, source_target_pairs={{0,112},{16,0},{32,16},{48,32},{64,48},{80,64},{96,80},{112,96},{1... | collective-permute-start | bytes 442376 | tf_op jit(solution)/shard_map/ppermute | solution.py:346
  24.7 8.4 %collective-permute-start.4 = (bf16[128,1024]{1,0:T(8,128)(2,1)S(1)}, bf16[128,1024]{1,0:T(8,128)(2,1)S(1)}, u32[]{:S(2)}, u32[]{:S(2)}) collective-permute-start(bf16[128,1024]{1,0:T(8,128)(2,1)S(1)} %get-tuple-element.53), channel_id=1, source_target_pairs={{0,1},{1,0},{2,3},{3,2},{4,5},{5,4},{6,7},{7,6},{8,9},{9,8},{10,11... | collective-permute-start | bytes 786440 | tf_op jit(solution)/shard_map/ppermute | solution.py:346
  29.7 12.9 %collective-permute-start.1 = (bf16[288,512]{1,0:T(8,128)(2,1)S(1)}, bf16[288,512]{1,0:T(8,128)(2,1)S(1)}, u32[]{:S(2)}, u32[]{:S(2)}) collective-permute-start(bf16[288,512]{1,0:T(8,128)(2,1)S(1)} %get-tuple-element.49), channel_id=1, source_target_pairs={{0,1},{1,2},{2,3},{3,4},{4,5},{5,6},{6,7},{7,8},{8,9},{9,10},{10,1... | collective-permute-start | bytes 884744 | tf_op jit(solution)/shard_map/ppermute | solution.py:346
  33.1 6.7 %copy-start.7 = (bf16[512,2048]{1,0:T(8,128)(2,1)S(1)}, bf16[512,2048]{1,0:T(8,128)(2,1)}, u32[]{:S(2)}) copy-start(bf16[512,2048]{1,0:T(8,128)(2,1)} %expand.7) | copy-start | bytes 6291460
  33.1 6.7 %copy-start.8 = (bf16[2048,512]{1,0:T(8,128)(2,1)S(1)}, bf16[2048,512]{1,0:T(8,128)(2,1)}, u32[]{:S(2)}) copy-start(bf16[2048,512]{1,0:T(8,128)(2,1)} %shrink.7) | copy-start | bytes 6291460
  37.5 12.9 %collective-permute-start.5 = (bf16[288,512]{1,0:T(8,128)(2,1)S(1)}, bf16[288,512]{1,0:T(8,128)(2,1)S(1)}, u32[]{:S(2)}, u32[]{:S(2)}) collective-permute-start(bf16[288,512]{1,0:T(8,128)(2,1)S(1)} %get-tuple-element.58), channel_id=1, source_target_pairs={{0,1},{1,2},{2,3},{3,4},{4,5},{5,6},{6,7},{7,8},{8,9},{9,10},{10,1... | collective-permute-start | bytes 884744 | tf_op jit(solution)/shard_map/ppermute | solution.py:346
  44.2 7.8 %copy-start.2 = (bf16[2048,1024]{1,0:T(8,128)(2,1)S(1)}, bf16[2048,1024]{1,0:T(8,128)(2,1)}, u32[]{:S(2)}) copy-start(bf16[2048,1024]{1,0:T(8,128)(2,1)} %weight.3) | copy-start | bytes 12582916
  44.2 7.8 %copy-start.3 = (bf16[2,576,864]{2,1,0:T(8,128)(2,1)S(1)}, bf16[2,576,864]{2,1,0:T(8,128)(2,1)}, u32[]{:S(2)}) copy-start(bf16[2,576,864]{2,1,0:T(8,128)(2,1)} %constant.33.clone.pm) | copy-start | bytes 5971972
  44.2 17.1 %collective-permute-start.6 = (bf16[128,1024]{1,0:T(8,128)(2,1)S(1)}, bf16[128,1024]{1,0:T(8,128)(2,1)S(1)}, u32[]{:S(2)}, u32[]{:S(2)}) collective-permute-start(bf16[128,1024]{1,0:T(8,128)(2,1)S(1)} %collective-permute-done.4.a), channel_id=1, source_target_pairs={{0,16},{16,0},{32,48},{48,32},{64,80},{80,64},{96,112},{112,96},{1... | collective-permute-start | bytes 786440 | tf_op jit(solution)/shard_map/ppermute | solution.py:354
  44.3 9.6 %collective-permute-start.7 = (bf16[128,1024]{1,0:T(8,128)(2,1)S(1)}, bf16[128,1024]{1,0:T(8,128)(2,1)S(1)}, u32[]{:S(2)}, u32[]{:S(2)}) collective-permute-start(bf16[128,1024]{1,0:T(8,128)(2,1)S(1)} %collective-permute-done.4.a), channel_id=1, source_target_pairs={{0,32},{16,48},{32,0},{48,16},{64,96},{80,112},{96,64},{112,80},{1... | collective-permute-start | bytes 786440 | tf_op jit(solution)/shard_map/ppermute | solution.py:354
  53.7 5.5 %copy-start.15 = (bf16[576,576]{1,0:T(8,128)(2,1)S(1)}, bf16[576,576]{1,0:T(8,128)(2,1)}, u32[]{:S(2)}) copy-start(bf16[576,576]{1,0:T(8,128)(2,1)} %constant.34.clone.perm) | copy-start | bytes 1990660
  53.7 9.7 %collective-permute-start.9 = (bf16[144,1024]{1,0:T(8,128)(2,1)S(1)}, bf16[144,1024]{1,0:T(8,128)(2,1)S(1)}, u32[]{:S(2)}, u32[]{:S(2)}) collective-permute-start(bf16[144,1024]{1,0:T(8,128)(2,1)S(1)} %shard_map.220.own), channel_id=1, source_target_pairs={{0,1},{1,0},{2,3},{3,2},{4,5},{5,4},{6,7},{7,6},{8,9},{9,8},{10,11... | collective-permute-start | bytes 884744 | tf_op jit(solution)/shard_map/ppermute | solution.py:346
  53.9 7.5 %collective-permute-start.8 = (bf16[128,1024]{1,0:T(8,128)(2,1)S(1)}, bf16[128,1024]{1,0:T(8,128)(2,1)S(1)}, u32[]{:S(2)}, u32[]{:S(2)}) collective-permute-start(bf16[128,1024]{1,0:T(8,128)(2,1)S(1)} %collective-permute-done.7.c), channel_id=1, source_target_pairs={{0,16},{16,0},{32,48},{48,32},{64,80},{80,64},{96,112},{112,96},{1... | collective-permute-start | bytes 786440 | tf_op jit(solution)/shard_map/ppermute | solution.py:354
  55.7 12.7 %collective-permute-start.12 = (bf16[144,1024]{1,0:T(8,128)(2,1)S(1)}, bf16[144,1024]{1,0:T(8,128)(2,1)S(1)}, u32[]{:S(2)}, u32[]{:S(2)}) collective-permute-start(bf16[144,1024]{1,0:T(8,128)(2,1)S(1)} %shard_map.221.own), channel_id=1, source_target_pairs={{0,1},{1,0},{2,3},{3,2},{4,5},{5,4},{6,7},{7,6},{8,9},{9,8},{10,11... | collective-permute-start | bytes 884744 | tf_op jit(solution)/shard_map/ppermute | solution.py:346
  61.3 2.1 %copy-start.6 = (bf16[512,3,1024]{2,0,1:T(8,128)(2,1)S(1)}, bf16[512,3,1024]{2,0,1:T(8,128)(2,1)}, u32[]{:S(2)}) copy-start(bf16[512,3,1024]{2,0,1:T(8,128)(2,1)} %param.29) | copy-start | bytes 9437188
  63.5 13.9 %copy-start.1 = (bf16[2048,1024]{1,0:T(8,128)(2,1)S(1)}, bf16[2048,1024]{1,0:T(8,128)(2,1)}, u32[]{:S(2)}) copy-start(bf16[2048,1024]{1,0:T(8,128)(2,1)} %shrink.9) | copy-start | bytes 12582916
  65.7 11.7 %copy-start = (bf16[2048,1024]{1,0:T(8,128)(2,1)S(1)}, bf16[2048,1024]{1,0:T(8,128)(2,1)}, u32[]{:S(2)}) copy-start(bf16[2048,1024]{1,0:T(8,128)(2,1)} %expand.9) | copy-start | bytes 12582916
  65.7 11.7 %collective-permute-start.10 = (bf16[288,512]{1,0:T(8,128)(2,1)S(1)}, bf16[288,512]{1,0:T(8,128)(2,1)S(1)}, u32[]{:S(2)}, u32[]{:S(2)}) collective-permute-start(bf16[288,512]{1,0:T(8,128)(2,1)S(1)} %get-tuple-element.70.mine), channel_id=1, source_target_pairs={{0,1},{1,0},{2,3},{3,2},{4,5},{5,4},{6,7},{7,6},{8,9},{9,8},{10,11... | collective-permute-start | bytes 884744 | tf_op jit(solution)/shard_map/ppermute | solution.py:346
  70.6 12.1 %collective-permute-start.13 = (bf16[288,512]{1,0:T(8,128)(2,1)S(1)}, bf16[288,512]{1,0:T(8,128)(2,1)S(1)}, u32[]{:S(2)}, u32[]{:S(2)}) collective-permute-start(bf16[288,512]{1,0:T(8,128)(2,1)S(1)} %get-tuple-element.78.mine), channel_id=1, source_target_pairs={{0,1},{1,0},{2,3},{3,2},{4,5},{5,4},{6,7},{7,6},{8,9},{9,8},{10,11... | collective-permute-start | bytes 884744 | tf_op jit(solution)/shard_map/ppermute | solution.py:346
  81.1 8.7 %collective-permute-start.11 = (bf16[144,1024]{1,0:T(8,128)(2,1)S(1)}, bf16[144,1024]{1,0:T(8,128)(2,1)S(1)}, u32[]{:S(2)}, u32[]{:S(2)}) collective-permute-start(bf16[144,1024]{1,0:T(8,128)(2,1)S(1)} %get-tuple-element.73), channel_id=1, source_target_pairs={{0,1},{1,0},{2,3},{3,2},{4,5},{5,4},{6,7},{7,6},{8,9},{9,8},{10,11... | collective-permute-start | bytes 884744 | tf_op jit(solution)/shard_map/ppermute | solution.py:346
  81.1 8.6 %copy-start.5 = (bf16[144,144]{1,0:T(8,128)(2,1)S(1)}, bf16[144,144]{1,0:T(8,128)(2,1)}, u32[]{:S(2)}) copy-start(bf16[144,144]{1,0:T(8,128)(2,1)} %constant.35.clone.pout) | copy-start | bytes 124420
  86.4 9.6 %collective-permute-start.14 = (bf16[144,1024]{1,0:T(8,128)(2,1)S(1)}, bf16[144,1024]{1,0:T(8,128)(2,1)S(1)}, u32[]{:S(2)}, u32[]{:S(2)}) collective-permute-start(bf16[144,1024]{1,0:T(8,128)(2,1)S(1)} %get-tuple-element.80), channel_id=1, source_target_pairs={{0,1},{1,0},{2,3},{3,2},{4,5},{5,4},{6,7},{7,6},{8,9},{9,8},{10,11... | collective-permute-start | bytes 884744 | tf_op jit(solution)/shard_map/ppermute | solution.py:346

commit v5 on v4

--- a/solution.py
+++ b/solution.py
@@ -158,21 +158,17 @@
     )(*args)
 
 
-def pack_kernel(x, left, right):
+def pack_kernel(x, out):
     row = lax.broadcasted_iota(jnp.int32, (144, 144), 0)
     col = lax.broadcasted_iota(jnp.int32, (144, 144), 1)
     six = (row * 10923) >> 16
     lat = jnp.where(row < 18, six, jnp.where(row < 36, six + 18, six - 3))
     perm = jnp.where(col == (row - 6 * six) * 24 + lat, 1.0, 0.0).astype(BF)
-    for half, dst in enumerate((left, right)):
-        got = []
-        for level in (1, 2, 3, 0):
-            at = level * 288 + half * 144
-            got.append(dot(perm, x[at:at + 144]))
-        rows = [g[e:e + 18] for e in (0, 18) for g in got]
-        dst[:144] = jnp.concatenate(rows, axis=0).astype(BF)
-        rows = [g[w:w + 36] for w in (36, 72, 108) for g in got]
-        dst[144:] = jnp.concatenate(rows, axis=0).astype(BF)
+    got = [dot(perm, x[level]) for level in (1, 2, 3, 0)]
+    rows = [g[e:e + 18] for e in (0, 18) for g in got]
+    out[:144] = jnp.concatenate(rows, axis=0).astype(BF)
+    rows = [g[w:w + 36] for w in (36, 72, 108) for g in got]
+    out[144:] = jnp.concatenate(rows, axis=0).astype(BF)
 
 
 def ready_kernel(
@@ -382,13 +378,9 @@
     col_axes = ("lon", "tp")
     tok = lambda n: ((n, 512), BF)
 
-    flat = patches.transpose(0, 2, 1, 3).reshape(1152, 512)
-    left, right = call(
-        pack_kernel,
-        [tok(576)] * 2,
-        [flat],
-        10**9,
-    )
+    home = patches.transpose(0, 2, 1, 3).reshape(4, 2, 144, 512)
+    left = call(pack_kernel, [tok(576)], [home[:, 0]], 10**8)[0]
+    right = call(pack_kernel, [tok(576)], [after(home, left)[:, 1]], 10**9)[0]
     region_ids = after(region_ids, right)
     left = behind(left, col_axes, -1)
     pick, keep = pick_rows()

time: 97.5 us -> 97.7 us (level)
  local copies, waits for them, and re-layouts: 1.46 us -> 2.97 us
  waiting for transfers between devices: 36 us -> 34.6 us
    ppermute x12, waiting for transfers between devices: 36 us -> 34.5 us  [behind(): lax.ppermute(value, axis, [(s, (s + steps) % count) for s in range(count)])]
    squeeze x0 -> x2, local copies, waits for them, and re-layouts: none -> 1.25 us  [the longest x1 1.2 us: shards(): left = call(pack_kernel, [tok(576)], [home[:, 0]], 10 ** 8)[0]]
    pallas_call x18 -> x19, Pallas kernels: 33.8 us -> 33.9 us  [call(): pl.pallas_call(kernel, out_shape=[jax.ShapeDtypeStruct(shape, kind) for s...]
where the time goes in v5:
time: 97.7 us; the launch traced here: 97.5 us
  waiting for transfers between devices  34.6 us (35%)
  Pallas kernels  33.9 us (35%)
  starting transfers between devices  25.1 us (26%)
  local copies, waits for them, and re-layouts  2.97 us (3%)
    ppermute x12, waiting for transfers between devices, behind(): lax.ppermute(value, axis, [(s, (s + steps) % count) for s in range(count)])  34.5 us
    pallas_call x19, Pallas kernels, call(): pl.pallas_call(kernel, out_shape=[jax.ShapeDtypeStruct(shape, kind) for s...  33.9 us
    ppermute x12, starting transfers between devices, behind(): lax.ppermute(value, axis, [(s, (s + steps) % count) for s in range(count)])  23.4 us
  transfers between devices with their start and end apart: 15, of which 9 were waited for; matrix products, arithmetic and copies ran while one was open for 0% of the time, Pallas kernels for 33%

profile of v5, /device:TPU:0, one launch (start us, length us, event | category | flops | bytes accessed | tf_op | source)
XLA Modules:
  0.0 97.5 jit_solution(16115471313036136954)
XLA Ops:
  0.6 1.2 %slice_bitcast_fusion.1.x = bf16[4,144,512]{2,1,0:T(8,128)(2,1)S(1)} fusion(bf16[4,2,144,512]{3,2,1,0:T(8,128)(2,1)} %bitcast.27), kind=kLoop, calls=%fused_computation.1 | loop fusion | bytes 1179648 | tf_op jit(solution)/shard_map/squeeze | solution.py:382
  1.8 0.3 shard_map.212
  2.1 6.6 %collective-permute-start = (bf16[576,512]{1,0:T(8,128)(2,1)S(1)}, bf16[576,512]{1,0:T(8,128)(2,1)S(1)}, u32[]{:S(2)}, u32[]{:S(2)}) collective-permute-start(bf16[576,512]{1,0:T(8,128)(2,1)S(1)} %shard_map.212), channel_id=1, source_target_pairs={{0,15},{1,0},{2,1},{3,2},{4,3},{5,4},{6,5},{7,6},{8,7},{9,8},{10,9... | collective-permute-start | bytes 1769480 | tf_op jit(solution)/shard_map/ppermute | solution.py:342
  8.9 0.0 copy-start.16
  8.9 0.3 shard_map.213.right_all.right
  9.2 0.8 copy-done.4
  10.1 0.1 copy-done.15
  10.2 0.1 copy-done.16
  10.3 0.4 shard_map.214
  10.7 10.7 %collective-permute-done.left_all.left = bf16[576,512]{1,0:T(8,128)(2,1)S(1)} collective-permute-done((bf16[576,512]{1,0:T(8,128)(2,1)S(1)}, bf16[576,512]{1,0:T(8,128)(2,1)S(1)}, u32[]{:S(2)}, u32[]{:S(2)}) %collective-permute-start) | collective-permute-done | bytes 589856 | tf_op jit(solution)/shard_map/ppermute | solution.py:342
  21.4 0.0 collective-permute-start.2
  21.4 2.9 %collective-permute-start.3 = (bf16[144,512]{1,0:T(8,128)(2,1)S(1)}, bf16[144,512]{1,0:T(8,128)(2,1)S(1)}, u32[]{:S(2)}, u32[]{:S(2)}) collective-permute-start(bf16[144,512]{1,0:T(8,128)(2,1)S(1)} %get-tuple-element.49), channel_id=1, source_target_pairs={{0,112},{16,0},{32,16},{48,32},{64,48},{80,64},{96,80},{112,96},{1... | collective-permute-start | bytes 442376 | tf_op jit(solution)/shard_map/ppermute | solution.py:342
  24.4 1.6 %collective-permute-start.4 = (bf16[128,1024]{1,0:T(8,128)(2,1)S(1)}, bf16[128,1024]{1,0:T(8,128)(2,1)S(1)}, u32[]{:S(2)}, u32[]{:S(2)}) collective-permute-start(bf16[128,1024]{1,0:T(8,128)(2,1)S(1)} %get-tuple-element.51), channel_id=1, source_target_pairs={{0,1},{1,0},{2,3},{3,2},{4,5},{5,4},{6,7},{7,6},{8,9},{9,8},{10,11... | collective-permute-start | bytes 786440 | tf_op jit(solution)/shard_map/ppermute | solution.py:342
  26.0 3.4 %shard_map.216 = (bf16[288,512]{1,0:T(8,128)(2,1)S(1)}, bf16[288,512]{1,0:T(8,128)(2,1)S(1)}) custom-call(bf16[576,512]{1,0:T(8,128)(2,1)S(1)} %shard_map.213.right_all.right, bf16[576,512]{1,0:T(8,128)(2,1)S(1)} %collective-permute-done.left_all.left, bf16[1152,128]{1,0:T(8,128)(2,1)S(1)} %get-tuple-element.52.classes, bf16[3,512,512]{2,1,0:T(8,128)(2,1)S(1)} %bitcast.22, ...), custom_call_target="tpu_custom_call" | custom-call | flops 4000000000 | bytes 3706880 | tf_op jit(solution)/shard_map/pallas_call | solution.py:150
  29.3 2.0 %collective-permute-start.1 = (bf16[288,512]{1,0:T(8,128)(2,1)S(1)}, bf16[288,512]{1,0:T(8,128)(2,1)S(1)}, u32[]{:S(2)}, u32[]{:S(2)}) collective-permute-start(bf16[288,512]{1,0:T(8,128)(2,1)S(1)} %get-tuple-element.47), channel_id=1, source_target_pairs={{0,1},{1,2},{2,3},{3,4},{4,5},{5,6},{6,7},{7,8},{8,9},{9,10},{10,1... | collective-permute-start | bytes 884744 | tf_op jit(solution)/shard_map/ppermute | solution.py:342
  31.3 1.4 %collective-permute-done.4.a = bf16[128,1024]{1,0:T(8,128)(2,1)S(1)} collective-permute-done((bf16[128,1024]{1,0:T(8,128)(2,1)S(1)}, bf16[128,1024]{1,0:T(8,128)(2,1)S(1)}, u32[]{:S(2)}, u32[]{:S(2)}) %collective-permute-start.4) | collective-permute-done | bytes 262176 | tf_op jit(solution)/shard_map/ppermute | solution.py:342
  32.8 4.4 %shard_map.217 = (bf16[288,512]{1,0:T(8,128)(2,1)S(1)}, bf16[288,512]{1,0:T(8,128)(2,1)S(1)}) custom-call(bf16[576,512]{1,0:T(8,128)(2,1)S(1)} %shard_map.213.right_all.right, bf16[576,512]{1,0:T(8,128)(2,1)S(1)} %collective-permute-done.left_all.left, bf16[216,512]{1,0:T(8,128)(2,1)S(1)} %collective-permute-done.2.down, ...), custom_call_target="tpu_custom_call" | custom-call | flops 6000000000 | bytes 4075520 | tf_op jit(solution)/shard_map/pallas_call | solution.py:150
  37.1 2.3 %collective-permute-start.5 = (bf16[288,512]{1,0:T(8,128)(2,1)S(1)}, bf16[288,512]{1,0:T(8,128)(2,1)S(1)}, u32[]{:S(2)}, u32[]{:S(2)}) collective-permute-start(bf16[288,512]{1,0:T(8,128)(2,1)S(1)} %get-tuple-element.56), channel_id=1, source_target_pairs={{0,1},{1,2},{2,3},{3,4},{4,5},{5,6},{6,7},{7,8},{8,9},{9,10},{10,1... | collective-permute-start | bytes 884744 | tf_op jit(solution)/shard_map/ppermute | solution.py:342
  39.4 2.8 %shard_map.218 = (bf16[288,512]{1,0:T(8,128)(2,1)S(1)}, bf16[288,512]{1,0:T(8,128)(2,1)S(1)}) custom-call(bf16[288,512]{1,0:T(8,128)(2,1)S(1)} %get-tuple-element.48.h1, bf16[288,512]{1,0:T(8,128)(2,1)S(1)} %get-tuple-element.53.h2, bf16[512,2048]{1,0:T(8,128)(2,1)S(1)} %copy-done.7, bf16[2048,512]{1,0:T(8,128)(2,1)S(1)} %copy-done.8), custom_call_target="tpu_custom_call" | custom-call | flops 3000000000 | bytes 4784128 | tf_op jit(solution)/shard_map/pallas_call | solution.py:150
  42.3 1.6 %shard_map.219.l1 = bf16[288,512]{1,0:T(8,128)(2,1)S(1)} custom-call(bf16[288,512]{1,0:T(8,128)(2,1)S(1)} %collective-permute-done.1.h, bf16[512,2048]{1,0:T(8,128)(2,1)S(1)} %copy-done.7, bf16[2048,512]{1,0:T(8,128)(2,1)S(1)} %copy-done.8), custom_call_target="tpu_custom_call" | custom-call | flops 2000000000 | bytes 4489216 | tf_op jit(solution)/shard_map/pallas_call | solution.py:150
  43.8 0.1 collective-permute-start.6
  43.9 1.6 %collective-permute-start.7 = (bf16[128,1024]{1,0:T(8,128)(2,1)S(1)}, bf16[128,1024]{1,0:T(8,128)(2,1)S(1)}, u32[]{:S(2)}, u32[]{:S(2)}) collective-permute-start(bf16[128,1024]{1,0:T(8,128)(2,1)S(1)} %collective-permute-done.4.a), channel_id=1, source_target_pairs={{0,32},{16,48},{32,0},{48,16},{64,96},{80,112},{96,64},{112,80},{1... | collective-permute-start | bytes 786440 | tf_op jit(solution)/shard_map/ppermute | solution.py:350
  45.5 4.5 %collective-permute-done.5.h = bf16[288,512]{1,0:T(8,128)(2,1)S(1)} collective-permute-done((bf16[288,512]{1,0:T(8,128)(2,1)S(1)}, bf16[288,512]{1,0:T(8,128)(2,1)S(1)}, u32[]{:S(2)}, u32[]{:S(2)}) %collective-permute-start.5) | collective-permute-done | bytes 294944 | tf_op jit(solution)/shard_map/ppermute | solution.py:342
  50.0 1.6 %shard_map.220.l2 = bf16[288,512]{1,0:T(8,128)(2,1)S(1)} custom-call(bf16[288,512]{1,0:T(8,128)(2,1)S(1)} %collective-permute-done.5.h, bf16[512,2048]{1,0:T(8,128)(2,1)S(1)} %copy-done.7, bf16[2048,512]{1,0:T(8,128)(2,1)S(1)} %copy-done.8), custom_call_target="tpu_custom_call" | custom-call | flops 2000000000 | bytes 4489216 | tf_op jit(solution)/shard_map/pallas_call | solution.py:150
  51.6 0.6 copy-done.2
  52.2 1.8 %shard_map.221.own = bf16[144,1024]{1,0:T(8,128)(2,1)S(1)} custom-call(bf16[288,512]{1,0:T(8,128)(2,1)S(1)} %shard_map.219.l1, bf16[288,512]{1,0:T(8,128)(2,1)S(1)} %shard_map.220.l2, bf16[288,512]{1,0:T(8,128)(2,1)S(1)} %get-tuple-element.54.r1, bf16[288,512]{1,0:T(8,128)(2,1)S(1)} %get-tuple-element.58.r2, bf16[2,576,864]{2,1,0:T(8,128)(2,1)S(1)} %copy-done.3, ...), custom_call_target="tpu_custom_call" | custom-call | flops 1000000000 | bytes 7364608 | tf_op jit(solution)/shard_map/pallas_call | solution.py:150
  54.0 0.1 collective-permute-start.9
  54.1 0.1 collective-permute-start.8
  54.2 1.8 %shard_map.222.own = bf16[144,1024]{1,0:T(8,128)(2,1)S(1)} custom-call(bf16[288,512]{1,0:T(8,128)(2,1)S(1)} %shard_map.219.l1, bf16[288,512]{1,0:T(8,128)(2,1)S(1)} %shard_map.220.l2, bf16[288,512]{1,0:T(8,128)(2,1)S(1)} %get-tuple-element.54.r1, bf16[288,512]{1,0:T(8,128)(2,1)S(1)} %get-tuple-element.58.r2, bf16[2,576,864]{2,1,0:T(8,128)(2,1)S(1)} %copy-done.3, ...), custom_call_target="tpu_custom_call" | custom-call | flops 1000000000 | bytes 7364608 | tf_op jit(solution)/shard_map/pallas_call | solution.py:150
  56.0 3.5 %collective-permute-start.12 = (bf16[144,1024]{1,0:T(8,128)(2,1)S(1)}, bf16[144,1024]{1,0:T(8,128)(2,1)S(1)}, u32[]{:S(2)}, u32[]{:S(2)}) collective-permute-start(bf16[144,1024]{1,0:T(8,128)(2,1)S(1)} %shard_map.222.own), channel_id=1, source_target_pairs={{0,1},{1,0},{2,3},{3,2},{4,5},{5,4},{6,7},{7,6},{8,9},{9,8},{10,11... | collective-permute-start | bytes 884744 | tf_op jit(solution)/shard_map/ppermute | solution.py:342
  59.5 2.1 %shard_map.223 = bf16[1152,512]{1,0:T(8,128)(2,1)} custom-call(bf16[288,512]{1,0:T(8,128)(2,1)S(1)} %shard_map.219.l1, bf16[288,512]{1,0:T(8,128)(2,1)S(1)} %shard_map.220.l2, bf16[288,512]{1,0:T(8,128)(2,1)S(1)} %get-tuple-element.54.r1, bf16[288,512]{1,0:T(8,128)(2,1)S(1)} %get-tuple-element.58.r2, bf16[576,576]{1,0:T(8,128)(2,1)S(1)} %copy-done.14), custom_call_target="tpu_custom_call" | custom-call | flops 2000000000 | bytes 1843200 | tf_op jit(solution)/shard_map/pallas_call | solution.py:150
  61.6 0.1 shard_map.224.o_theirs
  61.7 2.0 %collective-permute-done.9.other = bf16[144,1024]{1,0:T(8,128)(2,1)S(1)} collective-permute-done((bf16[144,1024]{1,0:T(8,128)(2,1)S(1)}, bf16[144,1024]{1,0:T(8,128)(2,1)S(1)}, u32[]{:S(2)}, u32[]{:S(2)}) %collective-permute-start.9) | collective-permute-done | bytes 294944 | tf_op jit(solution)/shard_map/ppermute | solution.py:342
  63.7 2.2 %shard_map.225 = (bf16[288,1024]{1,0:T(8,128)(2,1)S(1)}, bf16[288,512]{1,0:T(8,128)(2,1)S(1)}) custom-call(s32[1]{0:T(128)} %bitcast.12.me, bf16[144,1024]{1,0:T(8,128)(2,1)S(1)} %shard_map.221.own, bf16[144,1024]{1,0:T(8,128)(2,1)S(1)} %collective-permute-done.9.other, bf16[3,512,1024]{2,1,0:T(8,128)(2,1)S(1)} %bitcast.20, bf16[256,256]{1,0:T(8,128)(2,1)S(1)} %copy-done.17, ...), custom_call_target="tpu_custom_call" | custom-call | flops 2000000000 | bytes 3870724 | tf_op jit(solution)/shard_map/pallas_call | solution.py:150
  65.9 0.3 collective-permute-start.10
  66.2 2.4 %collective-permute-done.12.other = bf16[144,1024]{1,0:T(8,128)(2,1)S(1)} collective-permute-done((bf16[144,1024]{1,0:T(8,128)(2,1)S(1)}, bf16[144,1024]{1,0:T(8,128)(2,1)S(1)}, u32[]{:S(2)}, u32[]{:S(2)}) %collective-permute-start.12) | collective-permute-done | bytes 294944 | tf_op jit(solution)/shard_map/ppermute | solution.py:342
  68.6 2.2 %shard_map.228 = (bf16[288,1024]{1,0:T(8,128)(2,1)S(1)}, bf16[288,512]{1,0:T(8,128)(2,1)S(1)}) custom-call(s32[1]{0:T(128)} %bitcast.12.me, bf16[144,1024]{1,0:T(8,128)(2,1)S(1)} %shard_map.222.own, bf16[144,1024]{1,0:T(8,128)(2,1)S(1)} %collective-permute-done.12.other, bf16[3,512,1024]{2,1,0:T(8,128)(2,1)S(1)} %bitcast.21, ...), custom_call_target="tpu_custom_call" | custom-call | flops 2000000000 | bytes 3870724 | tf_op jit(solution)/shard_map/pallas_call | solution.py:150
  70.8 1.9 %collective-permute-start.13 = (bf16[288,512]{1,0:T(8,128)(2,1)S(1)}, bf16[288,512]{1,0:T(8,128)(2,1)S(1)}, u32[]{:S(2)}, u32[]{:S(2)}) collective-permute-start(bf16[288,512]{1,0:T(8,128)(2,1)S(1)} %get-tuple-element.76.mine), channel_id=1, source_target_pairs={{0,1},{1,0},{2,3},{3,2},{4,5},{5,4},{6,7},{7,6},{8,9},{9,8},{10,11... | collective-permute-start | bytes 884744 | tf_op jit(solution)/shard_map/ppermute | solution.py:342
  72.7 4.9 %collective-permute-done.10.theirs = bf16[288,512]{1,0:T(8,128)(2,1)S(1)} collective-permute-done((bf16[288,512]{1,0:T(8,128)(2,1)S(1)}, bf16[288,512]{1,0:T(8,128)(2,1)S(1)}, u32[]{:S(2)}, u32[]{:S(2)}) %collective-permute-start.10) | collective-permute-done | bytes 294944 | tf_op jit(solution)/shard_map/ppermute | solution.py:342
  77.6 3.7 %shard_map.226 = (f32[144,1024]{1,0:T(8,128)S(1)}, bf16[144,1024]{1,0:T(8,128)(2,1)S(1)}, bf16[144,1024]{1,0:T(8,128)(2,1)S(1)}) custom-call(s32[1]{0:T(128)} %bitcast.12.me, bf16[288,1024]{1,0:T(8,128)(2,1)S(1)} %get-tuple-element.67.x, bf16[288,512]{1,0:T(8,128)(2,1)S(1)} %get-tuple-element.68.mine, bf16[288,512]{1,0:T(8,128)(2,1)S(1)} %collective-permute-done.10.theirs, ...), custom_call_target="tpu_custom_call" | custom-call | flops 100000000 | bytes 11665412 | tf_op jit(solution)/shard_map/pallas_call | solution.py:150
  81.3 0.1 collective-permute-start.11
  81.4 1.5 %collective-permute-done.13.theirs = bf16[288,512]{1,0:T(8,128)(2,1)S(1)} collective-permute-done((bf16[288,512]{1,0:T(8,128)(2,1)S(1)}, bf16[288,512]{1,0:T(8,128)(2,1)S(1)}, u32[]{:S(2)}, u32[]{:S(2)}) %collective-permute-start.13) | collective-permute-done | bytes 294944 | tf_op jit(solution)/shard_map/ppermute | solution.py:342
  82.9 3.7 %shard_map.229 = (f32[144,1024]{1,0:T(8,128)S(1)}, bf16[144,1024]{1,0:T(8,128)(2,1)S(1)}, bf16[144,1024]{1,0:T(8,128)(2,1)S(1)}) custom-call(s32[1]{0:T(128)} %bitcast.12.me, bf16[288,1024]{1,0:T(8,128)(2,1)S(1)} %get-tuple-element.75.x, bf16[288,512]{1,0:T(8,128)(2,1)S(1)} %get-tuple-element.76.mine, bf16[288,512]{1,0:T(8,128)(2,1)S(1)} %collective-permute-done.13.theirs, ...), custom_call_target="tpu_custom_call" | custom-call | flops 100000000 | bytes 11665412 | tf_op jit(solution)/shard_map/pallas_call | solution.py:150
  86.6 2.0 %collective-permute-start.14 = (bf16[144,1024]{1,0:T(8,128)(2,1)S(1)}, bf16[144,1024]{1,0:T(8,128)(2,1)S(1)}, u32[]{:S(2)}, u32[]{:S(2)}) collective-permute-start(bf16[144,1024]{1,0:T(8,128)(2,1)S(1)} %get-tuple-element.78), channel_id=1, source_target_pairs={{0,1},{1,0},{2,3},{3,2},{4,5},{5,4},{6,7},{7,6},{8,9},{9,8},{10,11... | collective-permute-start | bytes 884744 | tf_op jit(solution)/shard_map/ppermute | solution.py:342
  88.7 1.2 %collective-permute-done.11.r = bf16[144,1024]{1,0:T(8,128)(2,1)S(1)} collective-permute-done((bf16[144,1024]{1,0:T(8,128)(2,1)S(1)}, bf16[144,1024]{1,0:T(8,128)(2,1)S(1)}, u32[]{:S(2)}, u32[]{:S(2)}) %collective-permute-start.11) | collective-permute-done | bytes 294944 | tf_op jit(solution)/shard_map/ppermute | solution.py:342
  89.9 0.5 shard_map.227.first
  90.4 5.8 %collective-permute-done.14.r = bf16[144,1024]{1,0:T(8,128)(2,1)S(1)} collective-permute-done((bf16[144,1024]{1,0:T(8,128)(2,1)S(1)}, bf16[144,1024]{1,0:T(8,128)(2,1)S(1)}, u32[]{:S(2)}, u32[]{:S(2)}) %collective-permute-start.14) | collective-permute-done | bytes 294944 | tf_op jit(solution)/shard_map/ppermute | solution.py:342
  96.2 1.3 %shard_map.230 = bf16[12,6,4,1024]{3,2,1,0:T(4,128)(2,1)} custom-call(bf16[6,6,4,1024]{3,2,1,0:T(4,128)(2,1)S(1)} %shard_map.227.first, f32[144,1024]{1,0:T(8,128)S(1)} %get-tuple-element.77.k, bf16[144,1024]{1,0:T(8,128)(2,1)S(1)} %collective-permute-done.14.r, bf16[144,1024]{1,0:T(8,128)(2,1)S(1)} %get-tuple-element.79.h, bf16[144,144]{1,0:T(8,128)(2,1)S(1)} %copy-done.5), custom_call_target="tpu_custom_call" | custom-call | flops 100000000 | bytes 1516032 | tf_op jit(solution)/shard_map/pallas_call | solution.py:150
  (45 shorter events, 0.2 us)
Async XLA Ops:
  0.6 8.2 %copy-start.20 = (bf16[4,24,12,512]{3,1,2,0:T(8,128)(2,1)S(1)}, bf16[4,24,12,512]{3,1,2,0:T(8,128)(2,1)}, u32[]{:S(2)}) copy-start(bf16[4,24,12,512]{3,1,2,0:T(8,128)(2,1)} %param.21) | copy-start | bytes 3538948
  2.1 19.2 %collective-permute-start = (bf16[576,512]{1,0:T(8,128)(2,1)S(1)}, bf16[576,512]{1,0:T(8,128)(2,1)S(1)}, u32[]{:S(2)}, u32[]{:S(2)}) collective-permute-start(bf16[576,512]{1,0:T(8,128)(2,1)S(1)} %shard_map.212), channel_id=1, source_target_pairs={{0,15},{1,0},{2,1},{3,2},{4,3},{5,4},{6,5},{7,6},{8,7},{9,8},{10,9... | collective-permute-start | bytes 1769480 | tf_op jit(solution)/shard_map/ppermute | solution.py:342
  8.8 1.2 %copy-start.4 = (bf16[512,1024]{1,0:T(8,128)(2,1)S(1)}, bf16[512,1024]{1,0:T(8,128)(2,1)}, u32[]{:S(2)}) copy-start(bf16[512,1024]{1,0:T(8,128)(2,1)} %o_mine.3) | copy-start | bytes 3145732
  8.9 1.2 %copy-start.11 = (s32[4,24,12]{1,0,2:T(4,128)S(1)}, s32[4,24,12]{1,0,2:T(4,128)}, u32[]{:S(2)}) copy-start(s32[4,24,12]{1,0,2:T(4,128)} %param.22) | copy-start | bytes 13828
  8.9 1.2 %copy-start.12 = (bf16[8]{0:T(256)(128)(2,1)S(1)}, bf16[8]{0:T(256)(128)(2,1)}, u32[]{:S(2)}) copy-start(bf16[8]{0:T(256)(128)(2,1)} %param.27) | copy-start | bytes 52
  8.9 1.2 %copy-start.13 = (bf16[8]{0:T(256)(128)(2,1)S(1)}, bf16[8]{0:T(256)(128)(2,1)}, u32[]{:S(2)}) copy-start(bf16[8]{0:T(256)(128)(2,1)} %param.33) | copy-start | bytes 52
  8.9 1.3 %copy-start.15 = (bf16[1152,48]{1,0:T(8,128)(2,1)S(1)}, bf16[1152,48]{1,0:T(8,128)(2,1)}, u32[]{:S(2)}) copy-start(bf16[1152,48]{1,0:T(8,128)(2,1)} %constant.31.clone.rows) | copy-start | bytes 331780
  8.9 1.4 %copy-start.16 = (bf16[1152,25]{1,0:T(8,128)(2,1)S(1)}, bf16[1152,25]{1,0:T(8,128)(2,1)}, u32[]{:S(2)}) copy-start(bf16[1152,25]{1,0:T(8,128)(2,1)} %constant.32.clone.keep) | copy-start | bytes 172804
  8.9 1.4 %copy-start.18 = (bf16[8,512]{1,0:T(8,128)(2,1)S(1)}, bf16[8,512]{1,0:T(8,128)(2,1)}, u32[]{:S(2)}) copy-start(bf16[8,512]{1,0:T(8,128)(2,1)} %constant.30.clone.spread) | copy-start | bytes 24580
  10.3 15.7 %copy-start.9 = (bf16[512,3,512]{2,0,1:T(8,128)(2,1)S(1)}, bf16[512,3,512]{2,0,1:T(8,128)(2,1)}, u32[]{:S(2)}) copy-start(bf16[512,3,512]{2,0,1:T(8,128)(2,1)} %param.23) | copy-start | bytes 4718596
  10.3 15.7 %copy-start.10 = (bf16[512,512]{1,0:T(8,128)(2,1)S(1)}, bf16[512,512]{1,0:T(8,128)(2,1)}, u32[]{:S(2)}) copy-start(bf16[512,512]{1,0:T(8,128)(2,1)} %out.3) | copy-start | bytes 1572868
  10.3 15.7 %copy-start.17 = (bf16[256,256]{1,0:T(8,128)(2,1)S(1)}, bf16[256,256]{1,0:T(8,128)(2,1)}, u32[]{:S(2)}) copy-start(bf16[256,256]{1,0:T(8,128)(2,1)} %constant.28.clone.ones) | copy-start | bytes 393220
  10.3 15.7 %copy-start.19 = (bf16[8,128]{1,0:T(8,128)(2,1)S(1)}, bf16[8,128]{1,0:T(8,128)(2,1)}, u32[]{:S(2)}) copy-start(bf16[8,128]{1,0:T(8,128)(2,1)} %constant.29.clone.lanes) | copy-start | bytes 6148
  21.4 11.3 %collective-permute-start.2 = (bf16[216,512]{1,0:T(8,128)(2,1)S(1)}, bf16[216,512]{1,0:T(8,128)(2,1)S(1)}, u32[]{:S(2)}, u32[]{:S(2)}) collective-permute-start(bf16[216,512]{1,0:T(8,128)(2,1)S(1)} %get-tuple-element.44), channel_id=1, source_target_pairs={{0,16},{16,32},{32,48},{48,64},{64,80},{80,96},{96,112},{112,0},{1... | collective-permute-start | bytes 663560 | tf_op jit(solution)/shard_map/ppermute | solution.py:342
  21.4 11.3 %collective-permute-start.3 = (bf16[144,512]{1,0:T(8,128)(2,1)S(1)}, bf16[144,512]{1,0:T(8,128)(2,1)S(1)}, u32[]{:S(2)}, u32[]{:S(2)}) collective-permute-start(bf16[144,512]{1,0:T(8,128)(2,1)S(1)} %get-tuple-element.49), channel_id=1, source_target_pairs={{0,112},{16,0},{32,16},{48,32},{64,48},{80,64},{96,80},{112,96},{1... | collective-permute-start | bytes 442376 | tf_op jit(solution)/shard_map/ppermute | solution.py:342
  24.4 8.4 %collective-permute-start.4 = (bf16[128,1024]{1,0:T(8,128)(2,1)S(1)}, bf16[128,1024]{1,0:T(8,128)(2,1)S(1)}, u32[]{:S(2)}, u32[]{:S(2)}) collective-permute-start(bf16[128,1024]{1,0:T(8,128)(2,1)S(1)} %get-tuple-element.51), channel_id=1, source_target_pairs={{0,1},{1,0},{2,3},{3,2},{4,5},{5,4},{6,7},{7,6},{8,9},{9,8},{10,11... | collective-permute-start | bytes 786440 | tf_op jit(solution)/shard_map/ppermute | solution.py:342
  29.3 12.9 %collective-permute-start.1 = (bf16[288,512]{1,0:T(8,128)(2,1)S(1)}, bf16[288,512]{1,0:T(8,128)(2,1)S(1)}, u32[]{:S(2)}, u32[]{:S(2)}) collective-permute-start(bf16[288,512]{1,0:T(8,128)(2,1)S(1)} %get-tuple-element.47), channel_id=1, source_target_pairs={{0,1},{1,2},{2,3},{3,4},{4,5},{5,6},{6,7},{7,8},{8,9},{9,10},{10,1... | collective-permute-start | bytes 884744 | tf_op jit(solution)/shard_map/ppermute | solution.py:342
  32.7 6.7 %copy-start.7 = (bf16[512,2048]{1,0:T(8,128)(2,1)S(1)}, bf16[512,2048]{1,0:T(8,128)(2,1)}, u32[]{:S(2)}) copy-start(bf16[512,2048]{1,0:T(8,128)(2,1)} %expand.7) | copy-start | bytes 6291460
  32.7 6.7 %copy-start.8 = (bf16[2048,512]{1,0:T(8,128)(2,1)S(1)}, bf16[2048,512]{1,0:T(8,128)(2,1)}, u32[]{:S(2)}) copy-start(bf16[2048,512]{1,0:T(8,128)(2,1)} %shrink.7) | copy-start | bytes 6291460
  37.1 12.9 %collective-permute-start.5 = (bf16[288,512]{1,0:T(8,128)(2,1)S(1)}, bf16[288,512]{1,0:T(8,128)(2,1)S(1)}, u32[]{:S(2)}, u32[]{:S(2)}) collective-permute-start(bf16[288,512]{1,0:T(8,128)(2,1)S(1)} %get-tuple-element.56), channel_id=1, source_target_pairs={{0,1},{1,2},{2,3},{3,4},{4,5},{5,6},{6,7},{7,8},{8,9},{9,10},{10,1... | collective-permute-start | bytes 884744 | tf_op jit(solution)/shard_map/ppermute | solution.py:342
  43.8 7.8 %copy-start.3 = (bf16[2,576,864]{2,1,0:T(8,128)(2,1)S(1)}, bf16[2,576,864]{2,1,0:T(8,128)(2,1)}, u32[]{:S(2)}) copy-start(bf16[2,576,864]{2,1,0:T(8,128)(2,1)} %constant.33.clone.pm) | copy-start | bytes 5971972
  43.8 17.7 %collective-permute-start.6 = (bf16[128,1024]{1,0:T(8,128)(2,1)S(1)}, bf16[128,1024]{1,0:T(8,128)(2,1)S(1)}, u32[]{:S(2)}, u32[]{:S(2)}) collective-permute-start(bf16[128,1024]{1,0:T(8,128)(2,1)S(1)} %collective-permute-done.4.a), channel_id=1, source_target_pairs={{0,16},{16,0},{32,48},{48,32},{64,80},{80,64},{96,112},{112,96},{1... | collective-permute-start | bytes 786440 | tf_op jit(solution)/shard_map/ppermute | solution.py:350
  43.9 10.1 %collective-permute-start.7 = (bf16[128,1024]{1,0:T(8,128)(2,1)S(1)}, bf16[128,1024]{1,0:T(8,128)(2,1)S(1)}, u32[]{:S(2)}, u32[]{:S(2)}) collective-permute-start(bf16[128,1024]{1,0:T(8,128)(2,1)S(1)} %collective-permute-done.4.a), channel_id=1, source_target_pairs={{0,32},{16,48},{32,0},{48,16},{64,96},{80,112},{96,64},{112,80},{1... | collective-permute-start | bytes 786440 | tf_op jit(solution)/shard_map/ppermute | solution.py:350
  50.0 2.2 %copy-start.2 = (bf16[2048,1024]{1,0:T(8,128)(2,1)S(1)}, bf16[2048,1024]{1,0:T(8,128)(2,1)}, u32[]{:S(2)}) copy-start(bf16[2048,1024]{1,0:T(8,128)(2,1)} %weight.3) | copy-start | bytes 12582916
  54.0 5.5 %copy-start.14 = (bf16[576,576]{1,0:T(8,128)(2,1)S(1)}, bf16[576,576]{1,0:T(8,128)(2,1)}, u32[]{:S(2)}) copy-start(bf16[576,576]{1,0:T(8,128)(2,1)} %constant.34.clone.perm) | copy-start | bytes 1990660
  54.0 9.7 %collective-permute-start.9 = (bf16[144,1024]{1,0:T(8,128)(2,1)S(1)}, bf16[144,1024]{1,0:T(8,128)(2,1)S(1)}, u32[]{:S(2)}, u32[]{:S(2)}) collective-permute-start(bf16[144,1024]{1,0:T(8,128)(2,1)S(1)} %shard_map.221.own), channel_id=1, source_target_pairs={{0,1},{1,0},{2,3},{3,2},{4,5},{5,4},{6,7},{7,6},{8,9},{9,8},{10,11... | collective-permute-start | bytes 884744 | tf_op jit(solution)/shard_map/ppermute | solution.py:342
  54.1 7.5 %collective-permute-start.8 = (bf16[128,1024]{1,0:T(8,128)(2,1)S(1)}, bf16[128,1024]{1,0:T(8,128)(2,1)S(1)}, u32[]{:S(2)}, u32[]{:S(2)}) collective-permute-start(bf16[128,1024]{1,0:T(8,128)(2,1)S(1)} %collective-permute-done.7.c), channel_id=1, source_target_pairs={{0,16},{16,0},{32,48},{48,32},{64,80},{80,64},{96,112},{112,96},{1... | collective-permute-start | bytes 786440 | tf_op jit(solution)/shard_map/ppermute | solution.py:350
  56.0 12.7 %collective-permute-start.12 = (bf16[144,1024]{1,0:T(8,128)(2,1)S(1)}, bf16[144,1024]{1,0:T(8,128)(2,1)S(1)}, u32[]{:S(2)}, u32[]{:S(2)}) collective-permute-start(bf16[144,1024]{1,0:T(8,128)(2,1)S(1)} %shard_map.222.own), channel_id=1, source_target_pairs={{0,1},{1,0},{2,3},{3,2},{4,5},{5,4},{6,7},{7,6},{8,9},{9,8},{10,11... | collective-permute-start | bytes 884744 | tf_op jit(solution)/shard_map/ppermute | solution.py:342
  61.6 2.1 %copy-start.6 = (bf16[512,3,1024]{2,0,1:T(8,128)(2,1)S(1)}, bf16[512,3,1024]{2,0,1:T(8,128)(2,1)}, u32[]{:S(2)}) copy-start(bf16[512,3,1024]{2,0,1:T(8,128)(2,1)} %param.29) | copy-start | bytes 9437188
  63.7 13.9 %copy-start.1 = (bf16[2048,1024]{1,0:T(8,128)(2,1)S(1)}, bf16[2048,1024]{1,0:T(8,128)(2,1)}, u32[]{:S(2)}) copy-start(bf16[2048,1024]{1,0:T(8,128)(2,1)} %shrink.9) | copy-start | bytes 12582916
  65.9 11.7 %collective-permute-start.10 = (bf16[288,512]{1,0:T(8,128)(2,1)S(1)}, bf16[288,512]{1,0:T(8,128)(2,1)S(1)}, u32[]{:S(2)}, u32[]{:S(2)}) collective-permute-start(bf16[288,512]{1,0:T(8,128)(2,1)S(1)} %get-tuple-element.68.mine), channel_id=1, source_target_pairs={{0,1},{1,0},{2,3},{3,2},{4,5},{5,4},{6,7},{7,6},{8,9},{9,8},{10,11... | collective-permute-start | bytes 884744 | tf_op jit(solution)/shard_map/ppermute | solution.py:342
  68.6 9.0 %copy-start = (bf16[2048,1024]{1,0:T(8,128)(2,1)S(1)}, bf16[2048,1024]{1,0:T(8,128)(2,1)}, u32[]{:S(2)}) copy-start(bf16[2048,1024]{1,0:T(8,128)(2,1)} %expand.9) | copy-start | bytes 12582916
  70.8 12.1 %collective-permute-start.13 = (bf16[288,512]{1,0:T(8,128)(2,1)S(1)}, bf16[288,512]{1,0:T(8,128)(2,1)S(1)}, u32[]{:S(2)}, u32[]{:S(2)}) collective-permute-start(bf16[288,512]{1,0:T(8,128)(2,1)S(1)} %get-tuple-element.76.mine), channel_id=1, source_target_pairs={{0,1},{1,0},{2,3},{3,2},{4,5},{5,4},{6,7},{7,6},{8,9},{9,8},{10,11... | collective-permute-start | bytes 884744 | tf_op jit(solution)/shard_map/ppermute | solution.py:342
  81.3 8.6 %collective-permute-start.11 = (bf16[144,1024]{1,0:T(8,128)(2,1)S(1)}, bf16[144,1024]{1,0:T(8,128)(2,1)S(1)}, u32[]{:S(2)}, u32[]{:S(2)}) collective-permute-start(bf16[144,1024]{1,0:T(8,128)(2,1)S(1)} %get-tuple-element.71), channel_id=1, source_target_pairs={{0,1},{1,0},{2,3},{3,2},{4,5},{5,4},{6,7},{7,6},{8,9},{9,8},{10,11... | collective-permute-start | bytes 884744 | tf_op jit(solution)/shard_map/ppermute | solution.py:342
  81.4 8.5 %copy-start.5 = (bf16[144,144]{1,0:T(8,128)(2,1)S(1)}, bf16[144,144]{1,0:T(8,128)(2,1)}, u32[]{:S(2)}) copy-start(bf16[144,144]{1,0:T(8,128)(2,1)} %constant.35.clone.pout) | copy-start | bytes 124420
  86.6 9.6 %collective-permute-start.14 = (bf16[144,1024]{1,0:T(8,128)(2,1)S(1)}, bf16[144,1024]{1,0:T(8,128)(2,1)S(1)}, u32[]{:S(2)}, u32[]{:S(2)}) collective-permute-start(bf16[144,1024]{1,0:T(8,128)(2,1)S(1)} %get-tuple-element.78), channel_id=1, source_target_pairs={{0,1},{1,0},{2,3},{3,2},{4,5},{5,4},{6,7},{7,6},{8,9},{9,8},{10,11... | collective-permute-start | bytes 884744 | tf_op jit(solution)/shard_map/ppermute | solution.py:342
